TPU v7x, 32 devices: a whole 2x2x4 slice. The times are simulated.
32 devices in a mesh: dp: 8 (over y, x, core), seq: 4 (over z).
Axes of the slice: x: 2, y: 2, z: 4, core: 2. Of those that a mesh axis runs over, the one named last changes fastest.
Arguments:
- block_in: bfloat16 [16, 1024, 2048], P('dp', 'seq'), may hold values from -6 to 6
- doc_starts: int32 [16, 1024], P('dp', 'seq'), may hold values from 0 to 1, as said below
- out_grad: bfloat16 [16, 1024, 2048], P('dp', 'seq'), may hold values from -6 to 6
- w_mix: bfloat16 [2048, 8192], P(('dp', 'seq')), may hold values from -0.125 to 0.125
- w_out: bfloat16 [2048, 2048], P(('dp', 'seq')), may hold values from -0.1875 to 0.1875
- w_gu: bfloat16 [2048, 11264], P(('dp', 'seq')), may hold values from -0.125 to 0.125
- w_down: bfloat16 [5632, 2048], P(('dp', 'seq')), may hold values from -0.109375 to 0.109375
- attn_gain: bfloat16 [2048], P(('dp', 'seq')), may hold values from 0.5 to 1.5
- ffn_gain: bfloat16 [2048], P(('dp', 'seq')), may hold values from 0.5 to 1.5
- group_gain: bfloat16 [128], P(('dp', 'seq')), may hold values from 0.5 to 1.5
- lower_logit: bfloat16 [2048], P(('dp', 'seq')), may hold values from 3 to 10
Outputs:
- block_out: bfloat16 [16, 1024, 2048], P('dp', 'seq')
- in_grad: float32 [16, 1024, 2048], P('dp', 'seq')
- grad_mix: float32 [2048, 8192], P(('dp', 'seq'))
- grad_out: float32 [2048, 2048], P(('dp', 'seq'))
- grad_gu: float32 [2048, 11264], P(('dp', 'seq'))
- grad_down: float32 [5632, 2048], P(('dp', 'seq'))
- grad_attn_gain: float32 [2048], P(('dp', 'seq'))
- grad_ffn_gain: float32 [2048], P(('dp', 'seq'))
- grad_group: float32 [128], P(('dp', 'seq'))
- grad_logit: float32 [2048], P(('dp', 'seq'))
Inputs may be any that keep to these rules, and one draw needn't show every extreme that they name: `doc_starts`: position 0 of every sequence is 1. In each group of 2 consecutive sequences, one sequence has no start at positions 128 to 895.
All inputs are finite; a program needn't handle non-finite values.
Results may differ from a plain program's by a relative error of at most 0.014.
Values may be sent and summed in bfloat16 or wider, within the bound.
No kernel may reach another device: no remote copies, remote signals or barrier semaphores. Data moves between devices by JAX's collectives and lax.ppermute only.
A program may use at most 512 MiB of HBM per device.

v0:
```python
from functools import partial

import jax
import jax.numpy as jnp
from jax import lax
from jax.sharding import PartitionSpec as P

HEAD = 128
STRETCH = 128


EPSILON = 1e-06
PRECISE = lax.Precision.HIGHEST


def prefix(value, axis, combine, identity):
    size, here = (lax.axis_size(axis), lax.axis_index(axis))
    everything = jax.tree.map(
        lambda part, kind: lax.all_gather(part.astype(kind), axis),
        value,
        (jnp.bfloat16, jnp.bfloat16),
    )
    start = jax.tree.map(
        lambda part, zero: jnp.broadcast_to(jnp.asarray(zero, part.dtype), part.shape),
        value,
        identity,
    )

    def turn(k, before):
        reached = k < here
        new = combine(
            before, jax.tree.map(lambda part, own: part[k].astype(own.dtype), everything, value)
        )
        return jax.tree.map(lambda a, b: jnp.where(reached, a, b), new, before)

    return lax.fori_loop(0, size, turn, start)


def prefix_2(value, axis, join, neutral):
    count = lax.axis_size(axis)
    place = lax.axis_index(axis)
    ahead = count - 1 - place
    gathered = jax.tree.map(
        lambda a, kind: lax.all_gather(a.astype(kind), axis),
        value,
        jax.tree.map(lambda a: jnp.bfloat16 if a.dtype == jnp.float32 else a.dtype, value),
    )
    state = jax.tree.map(lambda a, e: jnp.zeros_like(a) + jnp.asarray(e, a.dtype), value, neutral)

    def one(turn, state):
        source = count - 1 - turn
        return join(
            state,
            jax.tree.map(
                lambda a, own: lax.dynamic_index_in_dim(a, source, 0, False).astype(own.dtype),
                gathered,
                value,
            ),
        )

    return lax.fori_loop(0, ahead, one, state)


def rms_scale(tensor):
    return lax.rsqrt(jnp.mean(tensor * tensor, axis=-1, keepdims=True) + EPSILON)


def silu_slope(inputs):
    sigmoid_value = jax.nn.sigmoid(inputs)
    return sigmoid_value * (1.0 + inputs * (1.0 - sigmoid_value))


def product(left, right):
    return jnp.dot(left, right, preferred_element_type=jnp.float32)


def contract_rows(left, right):
    return lax.dot_general(
        left, right, (((0,), (0,)), ((), ())), preferred_element_type=jnp.float32
    )


def times_transpose(left, right):
    return lax.dot_general(
        left, right, (((1,), (1,)), ((), ())), preferred_element_type=jnp.float32
    )


def to_heads(tensor, micro, piece):
    return jnp.transpose(tensor.reshape(micro, piece, -1, HEAD), (0, 2, 1, 3))


def from_heads(tensor):
    micro, heads, piece, head_size = tensor.shape
    return jnp.transpose(tensor, (0, 2, 1, 3)).reshape(micro * piece, heads * head_size)


def stretch_step(carry_state, inputs):
    queries, keys_in, values, logdecay, starts = inputs
    head_size = queries.shape[-1]
    running = jnp.cumsum(logdecay, axis=2)
    doc_count = jnp.cumsum(starts, axis=1)
    alive_mask = (doc_count == 0).astype(jnp.float32)
    positions = jnp.arange(queries.shape[2])
    causal = positions[:, None] >= positions[None, :]
    same_doc = ((doc_count[:, :, None] == doc_count[:, None, :]) & causal[None]).astype(jnp.float32)
    q_decayed = queries * jnp.exp(running)
    k_grown = keys_in * jnp.exp(-running)
    scores = (
        jnp.einsum("mhte,mhse->mhts", q_decayed, k_grown, precision=PRECISE) * same_doc[:, None]
    )
    inside = jnp.einsum("mhts,mhse->mhte", scores, values, precision=PRECISE)
    carried = (
        jnp.einsum("mhte,mhef->mhtf", q_decayed, carry_state, precision=PRECISE)
        * alive_mask[:, None, :, None]
    )
    mixed_out = (inside + carried) * head_size ** (-0.5)
    final_sum = running[:, :, -1:, :]
    tail_mask = (doc_count == doc_count[:, -1:]).astype(jnp.float32)
    k_last = keys_in * jnp.exp(final_sum - running) * tail_mask[:, None, :, None]
    fade_out = jnp.exp(final_sum[:, :, 0, :]) * alive_mask[:, None, -1:]
    new_state = fade_out[..., None] * carry_state + jnp.einsum(
        "mhse,mhsf->mhef", k_last, values, precision=PRECISE
    )
    return (new_state, mixed_out)


def local_stretches(queries, keys_in, values, logdecay, starts):
    micro, heads, piece, head_size = queries.shape
    blocks = piece // STRETCH

    def split_blocks(tensor):
        return jnp.transpose(
            tensor.reshape(micro, heads, blocks, STRETCH, head_size), (2, 0, 1, 3, 4)
        )

    start_blocks = jnp.transpose(starts.reshape(micro, blocks, STRETCH), (1, 0, 2))
    initial = jnp.zeros((micro, heads, head_size, head_size), jnp.float32)
    final_state, outputs = lax.scan(
        stretch_step,
        initial,
        (
            split_blocks(queries),
            split_blocks(keys_in),
            split_blocks(values),
            split_blocks(logdecay),
            start_blocks,
        ),
    )
    return (
        jnp.transpose(outputs, (1, 2, 0, 3, 4)).reshape(micro, heads, piece, head_size),
        final_state,
    )


def fade_factor(logdecay, starts):
    alive_end = (jnp.sum(starts, axis=1) == 0).astype(jnp.float32)
    return jnp.exp(jnp.sum(logdecay, axis=2)) * alive_end[:, None, None]


def carry_in(queries, logdecay, starts, incoming):
    running = jnp.cumsum(logdecay, axis=2)
    alive_mask = (jnp.cumsum(starts, axis=1) == 0).astype(jnp.float32)
    weighted = queries * jnp.exp(running) * alive_mask[:, None, :, None]
    return jnp.einsum("mhte,mhef->mhtf", weighted, incoming, precision=PRECISE) * queries.shape[
        -1
    ] ** (-0.5)


def device_mix(queries, keys_in, values, logdecay, incoming, starts):
    inside, leaving = local_stretches(queries, keys_in, values, logdecay, starts)
    extra = carry_in(queries, logdecay, starts, incoming)
    return (inside + extra, fade_factor(logdecay, starts)[..., None] * incoming + leaving)


def compose(earlier, later):
    return (earlier[0] * later[0], later[0][..., None] * earlier[1] + later[1])


def local(
    block_in,
    doc_starts,
    out_grad,
    w_mix,
    w_out,
    w_gu,
    w_down,
    attn_gain,
    ffn_gain,
    group_gain,
    lower_logit,
):
    micro, piece, features = block_in.shape
    tokens = micro * piece
    heads = features // HEAD
    whole_mix, whole_out, attn_scale, group_scale, logit_all = (
        lax.all_gather(w_mix, ("dp", "seq"), axis=0, tiled=True),
        lax.all_gather(w_out, ("dp", "seq"), axis=0, tiled=True),
        lax.all_gather(attn_gain, ("dp", "seq"), axis=0, tiled=True),
        lax.all_gather(group_gain, ("dp", "seq"), axis=0, tiled=True),
        lax.all_gather(lower_logit, ("dp", "seq"), axis=0, tiled=True),
    )
    inputs_f = block_in.astype(jnp.float32).reshape(tokens, features)
    rms_one = rms_scale(inputs_f)
    normed = (inputs_f * rms_one * attn_scale.astype(jnp.float32)).astype(jnp.bfloat16)
    projected = product(normed, whole_mix)
    q_pre, f_pre, v_pre, o_pre = jnp.split(projected, 4, axis=1)
    lower_bound = jax.nn.sigmoid(logit_all.astype(jnp.float32))
    opened = jax.nn.sigmoid(f_pre)
    closed = jax.nn.sigmoid(-f_pre)
    decays = lower_bound + (1.0 - lower_bound) * opened
    queries = to_heads(jax.nn.silu(q_pre), micro, piece)
    keys_in = to_heads((1.0 - lower_bound) * closed, micro, piece)
    values = to_heads(v_pre, micro, piece)
    logdecay = to_heads(jnp.log(decays), micro, piece)
    inside, leaving = local_stretches(queries, keys_in, values, logdecay, doc_starts)
    fade_out = fade_factor(logdecay, doc_starts)
    identity = (jnp.ones_like(fade_out), jnp.zeros_like(leaving))
    _, incoming = prefix((fade_out, leaving), "seq", compose, identity)
    mixed_heads = inside + carry_in(queries, logdecay, doc_starts, incoming)
    rms_heads = rms_scale(mixed_heads)
    unit_norm = mixed_heads * rms_heads
    unit_rows = from_heads(unit_norm)
    gate_out = jax.nn.silu(o_pre)
    group_row = jnp.tile(group_scale.astype(jnp.float32), heads)
    gated_out = (unit_rows * group_row * gate_out).astype(jnp.bfloat16)
    residual = inputs_f + product(gated_out, whole_out)
    whole_gu, whole_down, ffn_scale = (
        lax.all_gather(w_gu, ("dp", "seq"), axis=0, tiled=True),
        lax.all_gather(w_down, ("dp", "seq"), axis=0, tiled=True),
        lax.all_gather(ffn_gain, ("dp", "seq"), axis=0, tiled=True),
    )
    rms_two = rms_scale(residual)
    normed2 = (residual * rms_two * ffn_scale.astype(jnp.float32)).astype(jnp.bfloat16)
    gate_up = product(normed2, whole_gu)
    gate_pre, up_pre = jnp.split(gate_up, 2, axis=1)
    hidden = (jax.nn.silu(gate_pre) * up_pre).astype(jnp.bfloat16)
    block_out = (
        (residual + product(hidden, whole_down))
        .astype(jnp.bfloat16)
        .reshape(micro, piece, features)
    )
    whole_gu, whole_down, ffn_scale = (
        lax.all_gather(w_gu, ("dp", "seq"), axis=0, tiled=True),
        lax.all_gather(w_down, ("dp", "seq"), axis=0, tiled=True),
        lax.all_gather(ffn_gain, ("dp", "seq"), axis=0, tiled=True),
    )
    cotangent = out_grad.reshape(tokens, features)
    grad_down = contract_rows(hidden, cotangent)
    d_hidden = times_transpose(cotangent, whole_down)
    d_both = jnp.concatenate(
        [d_hidden * up_pre * silu_slope(gate_pre), d_hidden * jax.nn.silu(gate_pre)], axis=1
    ).astype(jnp.bfloat16)
    grad_gu = contract_rows(normed2, d_both)
    d_normed2 = times_transpose(d_both, whole_gu)
    grad_ffn_gain = jnp.sum(d_normed2 * residual * rms_two, axis=0)
    scaled_two = d_normed2 * ffn_scale.astype(jnp.float32)
    d_residual = cotangent.astype(jnp.float32) + rms_two * (
        scaled_two
        - residual * rms_two * rms_two * jnp.mean(scaled_two * residual, axis=1, keepdims=True)
    )
    ffn_grads = (
        lax.psum_scatter(grad_gu, ("dp", "seq"), scatter_dimension=0, tiled=True),
        lax.psum_scatter(grad_down, ("dp", "seq"), scatter_dimension=0, tiled=True),
        lax.psum_scatter(grad_ffn_gain, ("dp", "seq"), scatter_dimension=0, tiled=True),
    )
    whole_mix, whole_out, attn_scale, group_scale, logit_all = (
        lax.all_gather(w_mix, ("dp", "seq"), axis=0, tiled=True),
        lax.all_gather(w_out, ("dp", "seq"), axis=0, tiled=True),
        lax.all_gather(attn_gain, ("dp", "seq"), axis=0, tiled=True),
        lax.all_gather(group_gain, ("dp", "seq"), axis=0, tiled=True),
        lax.all_gather(lower_logit, ("dp", "seq"), axis=0, tiled=True),
    )
    bound_back = jax.nn.sigmoid(logit_all.astype(jnp.float32))
    group_back = jnp.tile(group_scale.astype(jnp.float32), heads)
    d_branch = d_residual.astype(jnp.bfloat16)
    grad_out = contract_rows(gated_out, d_branch)
    d_gated = times_transpose(d_branch, whole_out)
    grad_group = jnp.sum(d_gated * unit_rows * gate_out, axis=0).reshape(heads, HEAD).sum(axis=0)
    d_o_pre = d_gated * unit_rows * group_back * silu_slope(o_pre)
    d_unit = to_heads(d_gated * group_back * gate_out, micro, piece)
    d_mixed = rms_heads * (
        d_unit - unit_norm * jnp.mean(d_unit * unit_norm, axis=-1, keepdims=True)
    )
    _, carry_pull = jax.vjp(
        lambda state_in: carry_in(queries, logdecay, doc_starts, state_in), incoming
    )
    (toward_in,) = carry_pull(d_mixed)
    _, toward_out = prefix_2((fade_out, toward_in), "seq", compose, identity)
    _, mix_pull = jax.vjp(
        partial(device_mix, starts=doc_starts), queries, keys_in, values, logdecay, incoming
    )
    d_queries, d_keys, d_values, d_logdecay, _ = mix_pull((d_mixed, toward_out))
    common = from_heads(d_logdecay) / decays - from_heads(d_keys)
    d_f_pre = (1.0 - bound_back) * opened * closed * common
    grad_logit = bound_back * (1.0 - bound_back) * jnp.sum(closed * common, axis=0)
    d_proj = jnp.concatenate(
        [from_heads(d_queries) * silu_slope(q_pre), d_f_pre, from_heads(d_values), d_o_pre], axis=1
    ).astype(jnp.bfloat16)
    grad_mix = contract_rows(normed, d_proj)
    d_normed = times_transpose(d_proj, whole_mix)
    grad_attn_gain = jnp.sum(d_normed * inputs_f * rms_one, axis=0)
    scaled_one = d_normed * attn_scale.astype(jnp.float32)
    in_grad = d_residual + rms_one * (
        scaled_one
        - inputs_f * rms_one * rms_one * jnp.mean(scaled_one * inputs_f, axis=1, keepdims=True)
    )
    attn_grads = (
        lax.psum_scatter(grad_mix, ("dp", "seq"), scatter_dimension=0, tiled=True),
        lax.psum_scatter(grad_out, ("dp", "seq"), scatter_dimension=0, tiled=True),
        lax.psum_scatter(grad_attn_gain, ("dp", "seq"), scatter_dimension=0, tiled=True),
        lax.psum_scatter(grad_group, ("dp", "seq"), scatter_dimension=0, tiled=True),
        lax.psum_scatter(grad_logit, ("dp", "seq"), scatter_dimension=0, tiled=True),
    )
    return (
        block_out,
        in_grad.reshape(micro, piece, features),
        attn_grads[0],
        attn_grads[1],
        ffn_grads[0],
        ffn_grads[1],
        attn_grads[2],
        ffn_grads[2],
        attn_grads[3],
        attn_grads[4],
    )


def solution(mesh):
    in_specs = (
        P("dp", "seq", None),
        P("dp", "seq"),
        P("dp", "seq", None),
        P(("dp", "seq"), None),
        P(("dp", "seq"), None),
        P(("dp", "seq"), None),
        P(("dp", "seq"), None),
        P(("dp", "seq")),
        P(("dp", "seq")),
        P(("dp", "seq")),
        P(("dp", "seq")),
    )
    out_specs = (
        P("dp", "seq", None),
        P("dp", "seq", None),
        P(("dp", "seq"), None),
        P(("dp", "seq"), None),
        P(("dp", "seq"), None),
        P(("dp", "seq"), None),
        P(("dp", "seq")),
        P(("dp", "seq")),
        P(("dp", "seq")),
        P(("dp", "seq")),
    )
    return jax.shard_map(local, mesh=mesh, in_specs=in_specs, out_specs=out_specs, check_vma=False)
```

profile of v0, /device:TPU:0, one launch (start us, length us, event | category | flops | bytes accessed | tf_op | source)
XLA Modules:
  0.0 5779.5 jit_solution(9383333483330456800)
XLA Ops:
  11.4 44.5 all-reduce.10
  60.1 149.4 %all-gather.9.cloned.1.call-done = bf16[2048,8192]{1,0:T(8,128)(2,1)} async-done(((bf16[64,8192]{1,0:T(8,128)(2,1)}), bf16[2048,8192]{1,0:T(8,128)(2,1)}) %all-gather.9.cloned.1.call-update) | async-done | bytes 33554448 | tf_op jit(solution)/shard_map/all_gather | solution.py:197
  209.5 27.4 fusion.172
  237.0 22.3 multiply_bitcast_fusion.2
  277.8 60.6 %while.105 = (s32[]{:T(128)}, f32[2,16,128,128]{3,2,1,0:T(8,128)}, f32[2,2,16,128,128]{4,3,2,1,0:T(8,128)}, f32[2,2,16,128,128]{4,2,3,1,0:T(8,128)}, s32[2,2,128...) while((s32[]{:T(128)}, f32[2,16,128,128]{3,2,1,0:T(8,128)}, ...), condition=%wide.region_4.5_spmd.clone, body=%wide.region_1.4_spmd.clone.sunk | while | flops 3295302400 | bytes 130428288 | solution.py:139
  290.3 6.8 multiply_add_fusion.11
  321.2 6.8 multiply_add_fusion.11
  355.0 13.3 all_gather.53
  371.8 48.8 all-gather.17.cloned.1.call-done
  420.7 7.6 while.106
  428.3 8.2 multiply_reduce_fusion.5
  442.9 6.4 fusion.126
  449.3 50.3 all-gather.11.cloned.1.call-done
  499.6 10.7 multiply_reduce_fusion.4
  510.4 245.9 %all-gather.13.cloned.1.call-done = bf16[2048,11264]{1,0:T(8,128)(2,1)} async-done(((bf16[64,11264]{1,0:T(8,128)(2,1)}), bf16[2048,11264]{1,0:T(8,128)(2,1)}) %all-gather.13.cloned.1.call-update) | async-done | bytes 46137360 | tf_op jit(solution)/shard_map/all_gather | solution.py:229
  756.2 33.1 fusion.170
  789.4 112.4 %all-gather.15.cloned.1.call-done = bf16[5632,2048]{1,0:T(8,128)(2,1)} async-done(((bf16[176,2048]{1,0:T(8,128)(2,1)}), bf16[5632,2048]{1,0:T(8,128)(2,1)}) %all-gather.15.cloned.1.call-update) | async-done | bytes 23068688 | tf_op jit(solution)/shard_map/all_gather | solution.py:230
  901.7 27.1 multiply_convert_fusion.1
  928.8 34.7 multiply_reduce_fusion.2
  968.3 8.7 fusion.158
  992.9 8.2 fusion.151
  1001.2 10.8 fusion.156
  1013.5 21.2 fusion.173
  1041.8 51.7 while.107
  1074.4 7.3 multiply_add_fusion.12
  1098.5 9.6 fusion.127
  1108.1 10.5 fusion.142
  1121.2 7.8 while.103
  1139.4 170.3 %while.104 = (s32[]{:T(128)}, f32[2,16,128,128]{3,2,1,0:T(8,128)S(1)}, f32[2,2,16,128,128]{4,3,2,1,0:T(8,128)}, f32[2,2,16,128,128]{4,3,0,2,1:T(8,128)}, bf16[2,...) while((s32[]{:T(128)}, ...), condition=%wide.region_27.28_spmd, body=%wide.region_23.27_spmd.sunk | while | flops 6526341120 | bytes 546125632 | solution.py:139
  1164.3 6.8 fusion.247
  1189.5 6.6 bitcast_dynamic-update-slice_fusion.14
  1196.2 6.5 bitcast_dynamic-update-slice_fusion.15
  1204.9 6.7 fusion.251
  1245.1 7.0 fusion.247
  1270.6 6.4 bitcast_dynamic-update-slice_fusion.14
  1277.0 6.5 bitcast_dynamic-update-slice_fusion.15
  1285.6 6.7 fusion.251
  1324.5 6.9 bitcast_add_fusion.1
  1340.5 14.2 multiply_reduce_fusion
  1354.7 30.6 fusion.154
  1385.9 41.5 fusion.122
  1427.5 20.0 add_convert_fusion
  1447.5 27.7 fusion.141
  1475.3 44.7 all-reduce.9
  1522.3 6.8 fusion.137
  1529.1 890.9 %reduce-scatter.11.cloned.1.call-done = f32[176,2048]{1,0:T(8,128)} async-done(((f32[5632,2048]{1,0:T(8,128)}), f32[176,2048]{1,0:T(8,128)}) %reduce-scatter.11.cloned.1.call-update) | async-done | bytes 1441808 | tf_op jit(solution)/shard_map/reduce_scatter | solution.py:264
  2420.1 1414.0 %reduce-scatter.5.cloned.1.call-done = f32[64,8192]{1,0:T(8,128)} async-done(((f32[2048,8192]{1,0:T(8,128)}), f32[64,8192]{1,0:T(8,128)}) %reduce-scatter.5.cloned.1.call-update) | async-done | bytes 2097168 | tf_op jit(solution)/shard_map/reduce_scatter | solution.py:309
  3834.1 1938.4 %reduce-scatter.9.cloned.1.call-done = f32[64,11264]{1,0:T(8,128)} async-done(((f32[2048,11264]{1,0:T(8,128)}), f32[64,11264]{1,0:T(8,128)}) %reduce-scatter.9.cloned.1.call-update) | async-done | bytes 2883600 | tf_op jit(solution)/shard_map/reduce_scatter | solution.py:263
  (566 shorter events, 338.8 us)
Async XLA Ops:
  7.2 51.0 copy-start.56
  7.2 202.3 %all-gather.9.cloned.1.call-start = ((), (), s32[]{:S(2)}) async-start(), calls=%async_computation.4 | async-start | bytes 34603008 | tf_op jit(solution)/shard_map/all_gather | solution.py:197
  7.9 412.8 %all-gather.17.cloned.1.call-start = ((), (), s32[]{:S(2)}) async-start(), calls=%async_computation.12 | async-start | bytes 5242880 | tf_op jit(solution)/shard_map/all_gather | solution.py:19
  55.9 181.0 %copy-start.105 = (bf16[2048]{0:T(1024)(128)(2,1)}, bf16[2048]{0:T(1024)(128)(2,1)S(1)}, u32[]{:S(2)}) copy-start(bf16[2048]{0:T(1024)(128)(2,1)S(1)} %get-tuple-element.1357) | copy-start | bytes 12292
  55.9 181.0 %copy-start.94 = (f32[2048]{0:T(1024)}, f32[2048]{0:T(1024)S(1)}, u32[]{:S(2)}) copy-start(f32[2048]{0:T(1024)S(1)} %convert_element_type.192) | copy-start | bytes 24580
  58.2 178.8 %copy-start.103 = (f32[1,2,2,128]{3,1,2,0:T(2,128)}, f32[1,2,2,128]{3,1,2,0:T(2,128)S(1)}, u32[]{:S(2)}) copy-start(f32[1,2,2,128]{3,1,2,0:T(2,128)S(1)} %copy.270) | copy-start | bytes 6148
  58.2 178.8 %copy-start.96 = (f32[2048]{0:T(1024)}, f32[2048]{0:T(1024)S(1)}, u32[]{:S(2)}) copy-start(f32[2048]{0:T(1024)S(1)} %get-tuple-element.1405) | copy-start | bytes 24580
  58.2 178.8 %copy-start.98 = (f32[2048]{0:T(1024)}, f32[2048]{0:T(1024)S(1)}, u32[]{:S(2)}) copy-start(f32[2048]{0:T(1024)S(1)} %get-tuple-element.1406) | copy-start | bytes 24580
  261.2 11.9 copy-start.22
  341.2 158.5 %all-gather.11.cloned.1.call-start = ((), (), s32[]{:S(2)}) async-start(), calls=%async_computation.5 | async-start | bytes 8650752 | tf_op jit(solution)/shard_map/all_gather | solution.py:198
  341.9 414.3 %all-gather.13.cloned.1.call-start = ((), (), s32[]{:S(2)}) async-start(), calls=%async_computation.6 | async-start | bytes 47579136 | tf_op jit(solution)/shard_map/all_gather | solution.py:229
  342.5 559.3 %all-gather.15.cloned.1.call-start = ((), (), s32[]{:S(2)}) async-start(), calls=%async_computation.7 | async-start | bytes 23789568 | tf_op jit(solution)/shard_map/all_gather | solution.py:230
  343.1 777.9 %all-gather.19.cloned.1.call-start = ((), (), s32[]{:S(2)}) async-start(), calls=%async_computation.13 | async-start | bytes 5242880 | tf_op jit(solution)/shard_map/all_gather | solution.py:44
  344.3 23.9 copy-start.100
  344.4 619.2 %copy-start.79 = (f32[2048]{0:T(1024)}, f32[2048]{0:T(1024)S(1)}, u32[]{:S(2)}) copy-start(f32[2048]{0:T(1024)S(1)} %convert_element_type.201) | copy-start | bytes 24580
  344.4 10.5 copy-start.108
  344.4 96.6 %copy-start.89 = (f32[2048]{0:T(1024)}, f32[2048]{0:T(1024)S(1)}, u32[]{:S(2)}) copy-start(f32[2048]{0:T(1024)S(1)} %broadcast_bitcast_fusion) | copy-start | bytes 24580
  349.1 19.1 copy-start.37
  353.3 15.0 copy-start.23
  354.9 17.0 copy-start.87
  442.9 56.7 copy-start.57
  510.4 453.2 %copy-start.81 = (f32[512]{0:T(512)}, f32[512]{0:T(512)S(1)}, u32[]{:S(2)}) copy-start(f32[512]{0:T(512)S(1)} %add_rsqrt_fusion.1) | copy-start | bytes 6148
  756.2 145.5 %copy-start.77 = (bf16[2,256,2048]{2,1,0:T(8,128)(2,1)S(1)}, bf16[2,256,2048]{2,1,0:T(8,128)(2,1)}, u32[]{:S(2)}) copy-start(bf16[2,256,2048]{2,1,0:T(8,128)(2,1)} %param.23) | copy-start | bytes 6291460
  968.3 8.8 copy-start.72
  968.3 10.8 copy-start.90
  1001.1 528.0 %reduce-scatter.7.cloned.1.call-start = ((), (), s32[]{:S(2)}) async-start(), calls=%async_computation.9 | async-start | bytes 17301504 | tf_op jit(solution)/shard_map/reduce_scatter | solution.py:310
  1012.0 1408.1 %reduce-scatter.11.cloned.1.call-start = ((), (), s32[]{:S(2)}) async-start(), calls=%async_computation.11 | async-start | bytes 47579136 | tf_op jit(solution)/shard_map/reduce_scatter | solution.py:264
  1034.8 2799.3 %reduce-scatter.5.cloned.1.call-start = ((), (), s32[]{:S(2)}) async-start(), calls=%async_computation.8 | async-start | bytes 69206016 | tf_op jit(solution)/shard_map/reduce_scatter | solution.py:309
  1045.9 8.8 copy-start.47
  1045.9 8.8 copy-start.50
  1070.9 10.8 copy-start.47
  1070.9 10.8 copy-start.50
  1162.3 8.8 copy-start.11
  1196.2 8.6 copy-start.12
  1196.2 8.6 copy-start.14
  1243.2 9.0 copy-start.11
  1277.0 8.6 copy-start.12
  1277.0 8.6 copy-start.14
  1324.5 15.2 slice-start
  1324.5 15.2 slice-start.1
  1331.4 8.3 copy-start.97
  1331.4 8.3 copy-start.99
  1385.3 4387.2 %reduce-scatter.9.cloned.1.call-start = ((), (), s32[]{:S(2)}) async-start(), calls=%async_computation.10 | async-start | bytes 95158272 | tf_op jit(solution)/shard_map/reduce_scatter | solution.py:263
  1427.4 20.1 copy-start.106
  1427.4 20.1 copy-start.58
  1427.5 20.1 copy-start.95
  1427.5 20.1 copy-start.104
  1447.5 27.8 copy-start.107
  (125 other events, 570.3 us)
Sparse Core Ops, SparseCore 0:
  11.0 198.5 all-gather.8
  341.3 79.3 all-gather.16
  423.6 75.9 all-gather.10
  502.3 253.8 all-gather.12
  758.9 142.7 all-gather.14
  1001.2 78.9 all-gather.18
  1083.1 362.7 reduce-scatter.6
  1448.7 971.3 reduce-scatter.10
  2423.0 1411.0 reduce-scatter.4
  3836.9 1935.5 reduce-scatter.8
where the time goes:
time: 5790 us; the launch traced here: 5780 us
  waiting for transfers between devices  4850 us (84%)
  matrix products  461 us (8%)
  other arithmetic  189 us (3%)
  local copies, waits for them, and re-layouts  146 us (3%)
  blocking collectives  102 us (2%)
    reduce_scatter x1, waiting for transfers between devices, local(): lax.psum_scatter(grad_gu, ('dp', 'seq'), scatter_dimension=0, tiled=True)  1940 us
    reduce_scatter x1, waiting for transfers between devices, local(): lax.psum_scatter(grad_mix, ('dp', 'seq'), scatter_dimension=0, tiled=True)  1410 us
    reduce_scatter x1, waiting for transfers between devices, local(): lax.psum_scatter(grad_down, ('dp', 'seq'), scatter_dimension=0, tiled=True)  891 us
    all_gather x1, waiting for transfers between devices, local(): lax.all_gather(w_gu, ('dp', 'seq'), axis=0, tiled=True)  246 us
    all_gather x1, waiting for transfers between devices, local(): lax.all_gather(w_mix, ('dp', 'seq'), axis=0, tiled=True)  149 us
  transfers between devices with their start and end apart: 10, of which 8 were waited for; matrix products, arithmetic and copies ran while one was open for 9% of the time, Pallas kernels for 0%

commit v1 on v0

v1 whole, which is shorter than its diff:
```python
import jax
import jax.numpy as jnp
from jax import lax
from jax.experimental import pallas as pl
from jax.experimental.pallas import tpu as pltpu
from jax.sharding import PartitionSpec as P

HEAD = 128
TEAM = 4
EPSILON = 1e-06
SCALE = HEAD**-0.5
F32 = jnp.float32
BF16 = jnp.bfloat16
VMEM_LIMIT = 60 * 1024 * 1024


class Places:
    def __init__(self, n_dp, n_seq):
        self.n_dp, self.ny, self.nz = n_dp, n_dp // TEAM, n_seq
        place = lax.axis_index("dp")
        self.rank, self.y, self.z = place % TEAM, place // TEAM, lax.axis_index("seq")

    def swap(self, value, bits):
        return lax.ppermute(value, "dp", [(i, i ^ bits) for i in range(self.n_dp)])

    def hop(self, value, axis, pairs):
        if axis == "z":
            return lax.ppermute(value, "seq", pairs)
        spread = [(a * TEAM + r, b * TEAM + r) for a, b in pairs for r in range(TEAM)]
        return lax.ppermute(value, "dp", spread)

    def along(self, axis):
        return (self.ny, self.y) if axis == "y" else (self.nz, self.z)

    def by_rank(self, stack):
        odd, high = (self.rank & 1) == 1, (self.rank & 2) == 2
        stack = jnp.where(odd, jnp.concatenate([stack[1:2], stack[0:1], stack[3:4], stack[2:3]]), stack)
        return jnp.where(high, jnp.concatenate([stack[2:], stack[:2]]), stack)

    def team_gather(self, own):
        one, two = self.swap(own, 1), self.swap(own, 2)
        return [own, one, two, self.swap(two, 1)]

    def team_sum(self, parts):
        near = self.swap(jnp.stack([parts[1], parts[3]]), 1)
        far = (parts[2].astype(F32) + near[1].astype(F32)).astype(BF16)
        mine = parts[0].astype(F32) + near[0].astype(F32)
        return mine + self.swap(far, 2).astype(F32)

    def team_trade(self, stack):
        sent = self.by_rank(stack)
        got = [sent[0]] + [self.swap(sent[j], j) for j in range(1, TEAM)]
        return self.by_rank(jnp.stack(got))

    def gather_line(self, own, axis):
        n, here = self.along(axis)
        found = [(here, own)]
        if n == 2:
            return found + [(1 - here, self.hop(own, axis, [(0, 1), (1, 0)]))]
        ups, downs, up, down = [], [], own, own
        for _ in range(n - 1):
            up = self.hop(up, axis, [(i, i + 1) for i in range(n - 1)])
            down = self.hop(down, axis, [(i + 1, i) for i in range(n - 1)])
            ups.append(up)
            downs.append(down)
        for k in range(n - 1):
            found.append(((here + n - 1 - k) % n, ups[k] + downs[n - 2 - k]))
        return found

    def sum_line(self, piece, axis):
        n, here = self.along(axis)
        if n == 2:
            other = self.hop(piece(1 - here), axis, [(0, 1), (1, 0)])
            return piece(here).astype(F32) + other.astype(F32)
        total = None
        for sign in (1, -1):
            place = here if sign == 1 else n - 1 - here
            moving = None
            for k in range(n - 1):
                slot = (n - 1 - k + place) % n
                share = piece(slot if sign == 1 else n - 1 - slot)
                if moving is not None:
                    share = (share.astype(F32) + moving.astype(F32)).astype(BF16)
                pairs = [(i, i + 1) for i in range(min(k + 1, n - 1))]
                if sign == -1:
                    pairs = [(n - 1 - a, n - 1 - b) for a, b in pairs]
                moving = self.hop(share.astype(BF16), axis, pairs)
            total = moving.astype(F32) if total is None else total + moving.astype(F32)
        return piece(here).astype(F32) + total

    def gather_rows(self, own):
        s, rows, n = own.shape
        whole = jnp.zeros((self.ny, s, self.nz, rows, n), own.dtype)
        for z, value in self.gather_line(own, "z"):
            for y, there in self.gather_line(value, "y"):
                whole = lax.dynamic_update_slice(whole, there[None, :, None], (y, 0, z, 0, 0))
        return whole


def nn(a, b):
    return jnp.dot(a, b, preferred_element_type=F32)


def nt(a, b):
    return lax.dot_general(a, b, (((1,), (1,)), ((), ())), preferred_element_type=F32)


def tn(a, b):
    return lax.dot_general(a, b, (((0,), (0,)), ((), ())), preferred_element_type=F32)


def add_up(matrix, value):
    high = value.astype(BF16)
    rest = value - high.astype(F32)
    mid = rest.astype(BF16)
    low = (rest - mid.astype(F32)).astype(BF16)
    return nn(matrix, high) + nn(matrix, mid) + nn(matrix, low)


def triangle(n, lower):
    row = lax.broadcasted_iota(jnp.int32, (n, n), 0)
    col = lax.broadcasted_iota(jnp.int32, (n, n), 1)
    return row >= col if lower else row <= col


def sigmoid(z):
    return 1.0 / (1.0 + jnp.exp(-z))


def gates(f_pre, lower):
    small = jnp.exp(-jnp.abs(f_pre))
    big_part = 1.0 / (1.0 + small)
    small_part = small * big_part
    positive = f_pre >= 0
    opened = jnp.where(positive, big_part, small_part)
    closed = jnp.where(positive, small_part, big_part)
    return opened, closed, lower + (1.0 - lower) * opened


def wide_blocks(width):
    step = 512
    return [(a, min(a + step, width)) for a in range(0, width, step)]


def mix_kernel(x_ref, gain_ref, w_ref, lower_ref, row_ref, col_ref, *refs):
    normed_ref, proj_ref, run_ref, qd_ref, kg_ref, ins_ref, leave_ref, fade_ref = refs[-8:]
    channels = lower_ref.shape[1]
    x = x_ref[0].astype(F32)
    scale = lax.rsqrt(jnp.mean(x * x, axis=-1, keepdims=True) + EPSILON)
    normed_ref[0] = (x * scale * gain_ref[...]).astype(BF16)
    for a, b in wide_blocks(4 * channels):
        proj_ref[0, :, a:b] = nn(normed_ref[0], w_ref[:, a:b])
    lower = lower_ref[...]
    q_pre = proj_ref[0, :, 0:channels]
    f_pre = proj_ref[0, :, channels : 2 * channels]
    _, closed, decays = gates(f_pre, lower)
    keys = (1.0 - lower) * closed
    length = x.shape[0]
    causal = triangle(length, True)
    running = add_up(causal.astype(BF16), jnp.log(decays))
    run_ref[0] = running
    row, col = row_ref[0], col_ref[0]
    alive = (col[length - 1 :] == 0).astype(F32)
    tail = (col == col[length - 1 :]).astype(F32)
    final = running[length - 1 :]
    fade_ref[0] = jnp.exp(final) * alive
    qd_ref[0] = (q_pre * sigmoid(q_pre) * jnp.exp(running)).astype(BF16)
    kg_ref[0] = (keys * jnp.exp(-running)).astype(BF16)
    last = (keys * jnp.exp(final - running) * tail).astype(BF16)
    mask = jnp.where(causal & (col == row), 1.0, 0.0)
    for h in range(channels // HEAD):
        cut = slice(h * HEAD, (h + 1) * HEAD)
        values = proj_ref[0, :, 2 * channels + h * HEAD : 2 * channels + (h + 1) * HEAD].astype(BF16)
        scores = (nt(qd_ref[0, :, cut], kg_ref[0, :, cut]) * mask).astype(BF16)
        ins_ref[0, :, cut] = nn(scores, values) * SCALE
        leave_ref[0, h] = tn(last[:, cut], values)


def out_kernel(ins_ref, qd_ref, o_ref, state_ref, col_ref, group_ref, w_ref, *refs):
    mixed_ref, gated_ref, part_ref = refs[-3:]
    channels = ins_ref.shape[2]
    alive = (col_ref[0] == 0).astype(F32) * SCALE
    for h in range(channels // HEAD):
        cut = slice(h * HEAD, (h + 1) * HEAD)
        mixed = ins_ref[0, :, cut] + alive * nn(qd_ref[0, :, cut], state_ref[0, h])
        mixed_ref[0, :, cut] = mixed
        scale = lax.rsqrt(jnp.mean(mixed * mixed, axis=-1, keepdims=True) + EPSILON)
        o_pre = o_ref[0, :, cut]
        gated_ref[0, :, cut] = (mixed * scale * group_ref[...] * (o_pre * sigmoid(o_pre))).astype(BF16)
    for a, b in wide_blocks(w_ref.shape[1]):
        part_ref[0, :, a:b] = nn(gated_ref[0], w_ref[:, a:b]).astype(BF16)


def up_kernel(x_ref, w_ref, *refs):
    hidden_ref, first_ref, second_ref = refs[-3:]
    width = hidden_ref.shape[2]
    for a, b in wide_blocks(width):
        gate = nn(x_ref[0], w_ref[:, a:b])
        up = nn(x_ref[0], w_ref[:, width + a : width + b])
        s = sigmoid(gate)
        silu = gate * s
        hidden_ref[0, :, a:b] = (silu * up).astype(BF16)
        first_ref[0, :, a:b] = (up * (s * (1.0 + gate * (1.0 - s)))).astype(BF16)
        second_ref[0, :, a:b] = silu.astype(BF16)


def down_back_kernel(cot_ref, down_ref, w_ref, first_ref, second_ref, *refs):
    both_ref, part_ref = refs[-2:]
    width = first_ref.shape[2]
    for a, b in wide_blocks(width):
        d_hidden = nt(cot_ref[0], down_ref[a:b, :])
        both_ref[0, :, a:b] = (d_hidden * first_ref[0, :, a:b].astype(F32)).astype(BF16)
        both_ref[0, :, width + a : width + b] = (d_hidden * second_ref[0, :, a:b].astype(F32)).astype(BF16)
    for a, b in wide_blocks(part_ref.shape[2]):
        part_ref[0, :, a:b] = nt(both_ref[0], w_ref[a:b, :]).astype(BF16)


def out_back_kernel(branch_ref, w_ref, mixed_ref, o_ref, qd_ref, col_ref, group_ref, *refs):
    d_o_ref, g_ref, toward_ref, sum_ref = refs[-4:]
    channels = mixed_ref.shape[2]
    alive = (col_ref[0] == 0).astype(F32)
    group = group_ref[...]
    d_gated_all = nt(branch_ref[0], w_ref[...])
    for h in range(channels // HEAD):
        cut = slice(h * HEAD, (h + 1) * HEAD)
        d_gated = d_gated_all[:, cut]
        mixed = mixed_ref[0, :, cut]
        scale = lax.rsqrt(jnp.mean(mixed * mixed, axis=-1, keepdims=True) + EPSILON)
        unit = mixed * scale
        o_pre = o_ref[0, :, cut]
        s = sigmoid(o_pre)
        silu = o_pre * s
        both = d_gated * unit
        d_o_ref[0, :, cut] = (both * group * (s * (1.0 + o_pre * (1.0 - s)))).astype(BF16)
        sum_ref[0, :, cut] = jnp.sum(both * silu, axis=0, keepdims=True)
        d_unit = d_gated * group * silu
        d_mixed = scale * (d_unit - unit * jnp.mean(d_unit * unit, axis=-1, keepdims=True))
        g = (d_mixed * SCALE).astype(BF16)
        g_ref[0, :, cut] = g
        reach = (qd_ref[0, :, cut].astype(F32) * alive).astype(BF16)
        toward_ref[0, h] = tn(reach, g)


def mix_back_kernel(
    q_ref, f_ref, v_ref, run_ref, qd_ref, kg_ref, g_ref, state_ref, adjoint_ref, d_o_ref, lower_ref, row_ref, col_ref, *refs
):
    proj_ref, sum_ref = refs[-2:]
    channels = lower_ref.shape[1]
    length = row_ref.shape[2]
    lower = lower_ref[...]
    row, col = row_ref[0], col_ref[0]
    alive = (col == 0).astype(F32)
    alive_end = alive[length - 1 :]
    tail = (col == col[length - 1 :]).astype(F32)
    mask = jnp.where(triangle(length, True) & (col == row), 1.0, 0.0)
    later = triangle(length, False).astype(BF16)
    eye = lax.broadcasted_iota(jnp.int32, (HEAD, HEAD), 0) == lax.broadcasted_iota(jnp.int32, (HEAD, HEAD), 1)
    for h in range(channels // HEAD):
        cut = slice(h * HEAD, (h + 1) * HEAD)
        q_pre, f_pre = q_ref[0, :, cut], f_ref[0, :, cut]
        values = v_ref[0, :, cut].astype(BF16)
        running = run_ref[0, :, cut]
        qd, kg, g = qd_ref[0, :, cut], kg_ref[0, :, cut], g_ref[0, :, cut]
        state, adjoint = state_ref[0, h], adjoint_ref[0, h]
        low = lower[:, cut]
        opened, closed, decays = gates(f_pre, low)
        keys = (1.0 - low) * closed
        final = running[length - 1 :]
        last_factor = jnp.exp(final - running) * tail
        last = (keys * last_factor).astype(BF16)
        scores = (nt(qd, kg) * mask).astype(BF16)
        d_values = tn(scores, g) + nn(last, adjoint)
        d_scores = (nt(g, values) * mask).astype(BF16)
        d_qd = nn(d_scores, kg) + alive * nt(g, state)
        d_kg = tn(d_scores, qd)
        d_last = nt(values, adjoint)
        part_last = d_last * last.astype(F32)
        moved = d_qd * qd.astype(F32) - d_kg * kg.astype(F32) - part_last
        passed = jnp.sum(adjoint.astype(F32) * state.astype(F32), axis=1, keepdims=True)
        passed = jnp.sum(jnp.where(eye, passed, 0.0), axis=0, keepdims=True)
        d_final = jnp.sum(part_last, axis=0, keepdims=True) + passed * jnp.exp(final) * alive_end
        d_log = add_up(later, moved) + d_final
        d_queries = d_qd * jnp.exp(running)
        d_keys = d_kg * jnp.exp(-running) + d_last * last_factor
        common = d_log / decays - d_keys
        s = sigmoid(q_pre)
        proj_ref[0, :, cut] = (d_queries * (s * (1.0 + q_pre * (1.0 - s)))).astype(BF16)
        proj_ref[0, :, channels + h * HEAD : channels + (h + 1) * HEAD] = (
            (1.0 - low) * opened * closed * common
        ).astype(BF16)
        proj_ref[0, :, 2 * channels + h * HEAD : 2 * channels + (h + 1) * HEAD] = d_values.astype(BF16)
        sum_ref[0, :, cut] = jnp.sum(closed * common, axis=0, keepdims=True)
    proj_ref[0, :, 3 * channels :] = d_o_ref[0]


def over_sequences(kernel, name, chunk, count, total, ins, outs, shared, flops):
    del name

    def spec(shape, kind):
        if kind == "whole":
            return pl.BlockSpec(shape, lambda j: (0,) * len(shape), pipeline_mode=pl.Buffered(1))
        offset = chunk * count if kind == "all" or isinstance(kind, tuple) and kind[0] == "all" else 0
        if isinstance(kind, tuple):
            _, width, at = kind
            return pl.BlockSpec((1, shape[1], width), lambda j: (offset + j, 0, at))
        return pl.BlockSpec((1,) + shape[1:], lambda j: (offset + j,) + (0,) * (len(shape) - 1))

    arrays = [a for a, _ in ins]
    in_specs = [spec(a.shape, kind) for a, kind in ins]
    aliases = {}
    for i, held in enumerate(shared):
        if held is not None:
            aliases[len(arrays)] = i
            arrays.append(held)
            in_specs.append(pl.BlockSpec(memory_space=pl.ANY))
    size = sum(a.size * a.dtype.itemsize for a in arrays)
    return pl.pallas_call(
        kernel,
        grid=(count,),
        in_specs=in_specs,
        out_specs=[spec(shape, kind) for shape, _, kind in outs],
        out_shape=[jax.ShapeDtypeStruct(shape, kind) for shape, kind, _ in outs],
        input_output_aliases=aliases,
        compiler_params=pltpu.CompilerParams(vmem_limit_bytes=VMEM_LIMIT),
        cost_estimate=pl.CostEstimate(flops=flops, bytes_accessed=size, transcendentals=0),
    )(*arrays)


def build(n_dp, n_seq):
    def local(block_in, doc_starts, out_grad, w_mix, w_out, w_gu, w_down, attn_gain, ffn_gain, group_gain, lower_logit):
        at = Places(n_dp, n_seq)
        ny, nz = at.ny, at.nz
        micro, length, features = block_in.shape
        rows = w_mix.shape[0]
        own_channels = ny * nz * rows
        heads = own_channels // HEAD
        strip = own_channels // ny
        ff_rows = w_down.shape[0]
        own_ff = ny * nz * ff_rows
        ff_strip = nz * ff_rows
        total = micro * TEAM
        tokens = total * length

        mix_parts = jnp.transpose(w_mix.reshape(rows, 4, ny, TEAM, strip), (3, 0, 1, 2, 4))
        mix_own = at.team_trade(mix_parts.reshape(TEAM, rows, 4 * own_channels))
        gu_parts = jnp.transpose(w_gu.reshape(rows, 2, ny, TEAM, ff_strip), (3, 0, 1, 2, 4))
        gu_own = at.team_trade(gu_parts.reshape(TEAM, rows, 2 * own_ff))
        whole_mix = at.gather_rows(mix_own).reshape(features, 4 * own_channels)

        scales = jnp.concatenate([attn_gain, ffn_gain, lower_logit, group_gain])
        scales = jnp.pad(scales, (0, -scales.shape[0] % HEAD))
        scales = at.by_rank(jnp.stack(at.team_gather(scales)))
        scales = at.gather_rows(scales[:, None, :]).reshape(ny * TEAM * nz, -1).astype(F32)
        attn_scale = scales[:, :rows].reshape(1, features)
        ffn_scale = scales[:, rows : 2 * rows].reshape(1, features)
        logits = scales[:, 2 * rows : 3 * rows].reshape(ny, TEAM, nz * rows)
        own_logit = lax.dynamic_index_in_dim(logits, at.rank, 1, False).reshape(1, own_channels)
        group_scale = scales[:, 3 * rows : 3 * rows + group_gain.shape[0]].reshape(1, HEAD)
        bound = jax.nn.sigmoid(own_logit)

        starts = jnp.stack(at.team_gather(doc_starts.astype(BF16)), axis=1)
        upto = (jnp.arange(length)[:, None] <= jnp.arange(length)[None, :]).astype(BF16)
        counts = jnp.dot(starts.reshape(total, length), upto, preferred_element_type=F32)
        count_row = counts.reshape(total, 1, length)
        count_col = counts.reshape(total, length, 1)

        inputs = [jnp.stack(at.team_gather(block_in[c])) for c in range(micro)]
        whole_out = at.gather_rows(w_out[None]).reshape(own_channels, features)
        cotangent = jnp.concatenate([jnp.stack(at.team_gather(out_grad[c])) for c in range(micro)])
        whole_gu = at.gather_rows(gu_own).reshape(features, 2 * own_ff)
        whole_down = at.gather_rows(w_down[None]).reshape(own_ff, features)

        def run(kernel, name, chunk, ins, outs, shared, flops):
            return over_sequences(kernel, name, chunk, TEAM, total, ins, outs, shared, flops)

        def pass_on(leaving, fade, sign):
            factor = fade.reshape(TEAM, heads, HEAD)[..., None]
            entering = jnp.zeros(leaving.shape, F32)
            for k in range(nz - 1):
                pair = (k, k + 1) if sign == 1 else (nz - 1 - k, nz - 2 - k)
                entering = entering + at.hop((factor * entering + leaving).astype(BF16), "z", [pair]).astype(F32)
            return entering.astype(BF16)

        span = (total, length)
        part = (TEAM, length)
        wide = 4 * own_channels
        per_matmul = 2 * TEAM * length * features

        normed = gated = hidden = first = second = None
        proj = running = qd = kg = mixed = None
        entering, residual, normed2 = [], [], []
        fades = []
        for c in range(micro):
            rows_c, cols_c = (a[c * TEAM : (c + 1) * TEAM] for a in (count_row, count_col))
            normed, proj, running, qd, kg, inside, leaving, fade = run(
                mix_kernel, "mix", c,
                [(inputs[c], "part"), (attn_scale, "whole"), (whole_mix, "whole"), (bound, "whole"), (rows_c, "part"), (cols_c, "part")],
                [
                    (span + (features,), BF16, "all"),
                    (span + (wide,), F32, "all"),
                    (span + (own_channels,), F32, "all"),
                    (span + (own_channels,), BF16, "all"),
                    (span + (own_channels,), BF16, "all"),
                    (part + (own_channels,), F32, "part"),
                    (TEAM_STATES := (TEAM, heads, HEAD, HEAD), F32, "part"),
                    ((TEAM, 1, own_channels), F32, "part"),
                ],
                [normed, proj, running, qd, kg],
                per_matmul * wide,
            )
            fades.append(fade)
            entering.append(pass_on(leaving, fade, 1))
            mixed, gated, partial = run(
                out_kernel, "out", c,
                [
                    (inside, "part"), (qd, "all"), (proj, ("all", own_channels, 3)), (entering[c], "part"), (cols_c, "part"),
                    (group_scale, "whole"), (whole_out, "whole"),
                ],
                [(span + (own_channels,), F32, "all"), (span + (own_channels,), BF16, "all"), (part + (features,), BF16, "part")],
                [mixed, gated],
                per_matmul * own_channels,
            )
            residual.append(block_in[c].astype(F32) + at.team_sum(partial))
            rms_two = lax.rsqrt(jnp.mean(residual[c] * residual[c], axis=-1, keepdims=True) + EPSILON)
            normed2.append(jnp.stack(at.team_gather((residual[c] * rms_two * ffn_scale).astype(BF16))))
            hidden, first, second = run(
                up_kernel, "up", c,
                [(normed2[c], "part"), (whole_gu, "whole")],
                [(span + (own_ff,), BF16, "all")] * 3,
                [hidden, first, second],
                per_matmul * 2 * own_ff,
            )

        both = d_proj = None
        d_residual, d_branch, gain_sums = [], [], []
        for c in range(micro):
            both, partial = run(
                down_back_kernel, "down_back", c,
                [(cotangent, "all"), (whole_down, "whole"), (whole_gu, "whole"), (first, "all"), (second, "all")],
                [(span + (2 * own_ff,), BF16, "all"), (part + (features,), BF16, "part")],
                [both],
                per_matmul * 3 * own_ff,
            )
            d_normed2 = at.team_sum(partial)
            res = residual[c]
            rms_two = lax.rsqrt(jnp.mean(res * res, axis=-1, keepdims=True) + EPSILON)
            gain_sums.append(jnp.sum(d_normed2 * res * rms_two, axis=0))
            scaled = d_normed2 * ffn_scale
            d_residual.append(
                out_grad[c].astype(F32)
                + rms_two * (scaled - res * rms_two * rms_two * jnp.mean(scaled * res, axis=-1, keepdims=True))
            )
            d_branch.append(jnp.stack(at.team_gather(d_residual[c].astype(BF16))))

        def flat(a):
            return a.reshape(tokens, a.shape[-1])

        def column_piece(left, right, count):
            size = left.shape[1] // count
            if count == 2:
                return lambda j: tn(lax.dynamic_slice_in_dim(left, j * size, size, 1), right)
            product = tn(left, right).reshape(count, size, right.shape[1])
            return lambda j: lax.dynamic_index_in_dim(product, j, 0, False)

        def weight_sum(left, right, blocks):
            piece = column_piece(left, right, ny)
            sent = at.sum_line(lambda j: piece(j).astype(BF16), "y") if ny != 2 else None
            if sent is None:
                other = at.hop(piece(1 - at.y).astype(BF16), "y", [(0, 1), (1, 0)])
                sent = piece(at.y) + other.astype(F32)
            sent = sent.astype(BF16).reshape(blocks, nz, -1, right.shape[1])
            return at.sum_line(lambda j: lax.dynamic_index_in_dim(sent, j, 1, False), "z")

        grad_down = weight_sum(flat(hidden), flat(cotangent), 1)[0]
        gu_sum = weight_sum(flat(jnp.concatenate(normed2)), flat(both), TEAM)

        group_sums, logit_sums = [], []
        for c in range(micro):
            rows_c, cols_c = (a[c * TEAM : (c + 1) * TEAM] for a in (count_row, count_col))
            d_o, g, toward, group_sum = run(
                out_back_kernel, "out_back", c,
                [
                    (d_branch[c], "part"), (whole_out, "whole"), (mixed, "all"), (proj, ("all", own_channels, 3)), (qd, "all"),
                    (cols_c, "part"), (group_scale, "whole"),
                ],
                [
                    (part + (own_channels,), BF16, "part"), (part + (own_channels,), BF16, "part"),
                    (TEAM_STATES, F32, "part"), ((TEAM, 1, own_channels), F32, "part"),
                ],
                [],
                per_matmul * own_channels,
            )
            group_sums.append(group_sum)
            adjoint = pass_on(toward, fades[c], -1)
            d_proj, logit_sum = run(
                mix_back_kernel, "mix_back", c,
                [
                    (proj, ("all", own_channels, 0)), (proj, ("all", own_channels, 1)), (proj, ("all", own_channels, 2)),
                    (running, "all"), (qd, "all"), (kg, "all"), (g, "part"), (entering[c], "part"), (adjoint, "part"),
                    (d_o, "part"), (bound, "whole"), (rows_c, "part"), (cols_c, "part"),
                ],
                [(span + (wide,), BF16, "all"), ((TEAM, 1, own_channels), F32, "part")],
                [d_proj],
                per_matmul * own_channels,
            )
            logit_sums.append(logit_sum)

        mix_sum = weight_sum(flat(normed), flat(d_proj), TEAM)
        grad_out = weight_sum(flat(gated), flat(jnp.concatenate(d_branch)), 1)[0]
        d_normed_parts = times_transpose(flat(d_proj), whole_mix).astype(BF16).reshape(micro, TEAM, length, features)
        ffn_parts = nn(flat(hidden), whole_down).astype(BF16).reshape(micro, TEAM, length, features)

        def out_of_team(summed, count):
            got = at.team_trade(summed.astype(BF16)).astype(F32)
            width = got.shape[2] // (count * ny)
            got = got.reshape(TEAM, rows, count, ny, width)
            return jnp.transpose(got, (1, 2, 3, 0, 4)).reshape(rows, -1)

        grad_mix = out_of_team(mix_sum, 4)
        grad_gu = out_of_team(gu_sum, 2)

        d_normed = at.team_sum([d_normed_parts[:, j] for j in range(TEAM)])
        ffn_out = at.team_sum([ffn_parts[:, j] for j in range(TEAM)])
        block_out = (jnp.stack(residual) + ffn_out).astype(BF16)
        x = block_in.astype(F32)
        rms_one = lax.rsqrt(jnp.mean(x * x, axis=-1, keepdims=True) + EPSILON)
        attn_sum = jnp.sum(d_normed * x * rms_one, axis=(0, 1))
        scaled = d_normed * attn_scale
        in_grad = jnp.stack(d_residual) + rms_one * (
            scaled - x * rms_one * rms_one * jnp.mean(scaled * x, axis=-1, keepdims=True)
        )

        logit_sum = bound[0] * (1.0 - bound[0]) * sum(jnp.sum(a, axis=(0, 1)) for a in logit_sums)
        logit_all = jnp.where(
            jnp.arange(TEAM)[None, :, None] == at.rank, logit_sum.reshape(ny, 1, strip), 0.0
        ).reshape(features)
        group_all = jnp.sum(sum(jnp.sum(a, axis=(0, 1)) for a in group_sums).reshape(heads, HEAD), axis=0)
        sums = lax.psum(jnp.concatenate([attn_sum, sum(gain_sums), logit_all, group_all]), ("dp", "seq"))
        here = lax.axis_index("dp") * nz + at.z

        def mine(start, size):
            return lax.dynamic_slice_in_dim(sums, start + here * size, size)

        return (
            block_out,
            in_grad,
            grad_mix,
            grad_out,
            grad_gu,
            grad_down,
            mine(0, rows),
            mine(features, rows),
            mine(3 * features, group_gain.shape[0]),
            mine(2 * features, rows),
        )

    return local


def times_transpose(left, right):
    return nt(left, right)


def solution(mesh):
    tokens = P("dp", "seq", None)
    matrix = P(("dp", "seq"), None)
    vector = P(("dp", "seq"))
    return jax.shard_map(
        build(mesh.shape["dp"], mesh.shape["seq"]),
        mesh=mesh,
        in_specs=(tokens, P("dp", "seq"), tokens) + (matrix,) * 4 + (vector,) * 4,
        out_specs=(tokens, tokens) + (matrix,) * 4 + (vector,) * 4,
        check_vma=False,
    )
```

time: 5790 us -> 1560 us (0.27)
  waiting for transfers between devices: 4850 us -> 519 us
  matrix products: 461 us -> 136 us
  starting transfers between devices: 0.4 us -> 321 us
  Pallas kernels: 0 us -> 207 us
  blocking collectives: 102 us -> 42.5 us
    reduce_scatter x4 -> x0, waiting for transfers between devices: 4240 us -> none  [the longest x1 1940 us: local(): lax.psum_scatter(grad_gu, ('dp', 'seq'), scatter_dimension=0, tiled=True)]
    all_gather x6 -> x0, waiting for transfers between devices: 607 us -> none  [the longest x1 246 us: local(): lax.all_gather(w_gu, ('dp', 'seq'), axis=0, tiled=True)]
    ppermute x0 -> x144, waiting for transfers between devices: none -> 519 us  [the longest x24 244 us: hop(): return lax.ppermute(value, 'dp', spread)]
    dot_general x43 -> x11, matrix products: 461 us -> 136 us  [the longest x8 97.5 us: tn(): lax.dot_general(a, b, (((0,), (0,)), ((), ())), preferred_element_type=F32)]
    ppermute x0 -> x144, starting transfers between devices: none -> 321 us  [the longest x66 269 us: hop(): return lax.ppermute(value, 'seq', pairs)]
    pallas_call x0 -> x12, Pallas kernels: none -> 207 us  [over_sequences(): pl.pallas_call(kernel, grid=(count,), in_specs=in_specs, out_specs=[spec(...]
    unnamed x2 -> x0, blocking collectives: 89.2 us -> none
  transfers between devices with their start and end apart: 10 -> 144, of which waited for: 8 -> 43; matrix products, arithmetic and copies ran while one was open for 9% -> 27% of each run, Pallas kernels for 0% -> 12%
where the time goes in v1:
time: 1560 us; the launch traced here: 1550 us
  waiting for transfers between devices  519 us (33%)
  starting transfers between devices  321 us (21%)
  Pallas kernels  207 us (13%)
  other arithmetic  164 us (11%)
  local copies, waits for them, and re-layouts  161 us (10%)
  matrix products  136 us (9%)
  blocking collectives  42.5 us (3%)
    ppermute x66, starting transfers between devices, hop(): return lax.ppermute(value, 'seq', pairs)  269 us
    ppermute x24, waiting for transfers between devices, hop(): return lax.ppermute(value, 'dp', spread)  244 us
    pallas_call x12, Pallas kernels, over_sequences(): pl.pallas_call(kernel, grid=(count,), in_specs=in_specs, out_specs=[spec(...  207 us
    ppermute x66, waiting for transfers between devices, hop(): return lax.ppermute(value, 'seq', pairs)  193 us
    dot_general x8, matrix products, tn(): lax.dot_general(a, b, (((0,), (0,)), ((), ())), preferred_element_type=F32)  97.5 us
    ppermute x54, waiting for transfers between devices, swap(): return lax.ppermute(value, 'dp', [(i, i ^ bits) for i in range(self.n_dp)])  81.9 us
    psum x1, blocking collectives, local(): lax.psum(jnp.concatenate([attn_sum, sum(gain_sums), logit_all, group_all]...  42.5 us
    unnamed x190, local copies, waits for them, and re-layouts  31.7 us
  transfers between devices with their start and end apart: 144, of which 43 were waited for; matrix products, arithmetic and copies ran while one was open for 27% of the time, Pallas kernels for 12%

profile of v1, /device:TPU:0, one launch (start us, length us, event | category | flops | bytes accessed | tf_op | source)
XLA Modules:
  0.0 1554.2 jit_solution(9531756462252028319)
XLA Ops:
  142.8 38.3 %collective-permute-done.21 = bf16[4,64,2048]{2,1,0:T(8,128)(2,1)S(1)} collective-permute-done((bf16[4,64,2048]{2,1,0:T(8,128)(2,1)S(1)}, bf16[4,64,2048]{2,1,0:T(8,128)(2,1)S(1)}, u32[]{:S(2)}, u32[]{:S(2)}) %collective-permute-start.21) | collective-permute-done | bytes 1048608 | tf_op jit(solution)/shard_map/ppermute | solution.py:28
  197.4 17.2 %collective-permute-done.39 = bf16[1,64,2048]{2,1,0:T(8,128)(2,1)S(1)} collective-permute-done((bf16[1,64,2048]{2,1,0:T(8,128)(2,1)}, bf16[1,64,2048]{2,1,0:T(8,128)(2,1)S(1)}, u32[]{:S(2)}, u32[]{:S(2)}) %collective-permute-start.39) | collective-permute-done | bytes 262176 | tf_op jit(solution)/shard_map/ppermute | solution.py:28
  220.6 24.6 %collective-permute-done.40 = bf16[1,64,2048]{2,1,0:T(8,128)(2,1)S(1)} collective-permute-done((bf16[1,64,2048]{2,1,0:T(8,128)(2,1)S(1)}, bf16[1,64,2048]{2,1,0:T(8,128)(2,1)S(1)}, u32[]{:S(2)}, u32[]{:S(2)}) %collective-permute-start.40) | collective-permute-done | bytes 262176 | tf_op jit(solution)/shard_map/ppermute | solution.py:30
  265.7 17.8 %collective-permute-done.42 = bf16[1,64,2048]{2,1,0:T(8,128)(2,1)S(1)} collective-permute-done((bf16[1,64,2048]{2,1,0:T(8,128)(2,1)S(1)}, bf16[1,64,2048]{2,1,0:T(8,128)(2,1)S(1)}, u32[]{:S(2)}, u32[]{:S(2)}) %collective-permute-start.42) | collective-permute-done | bytes 262176 | tf_op jit(solution)/shard_map/ppermute | solution.py:30
  302.5 17.8 %collective-permute-done.44 = bf16[1,64,2048]{2,1,0:T(8,128)(2,1)S(1)} collective-permute-done((bf16[1,64,2048]{2,1,0:T(8,128)(2,1)S(1)}, bf16[1,64,2048]{2,1,0:T(8,128)(2,1)S(1)}, u32[]{:S(2)}, u32[]{:S(2)}) %collective-permute-start.44) | collective-permute-done | bytes 262176 | tf_op jit(solution)/shard_map/ppermute | solution.py:30
  328.2 23.8 %collective-permute-done.61 = bf16[4,64,2816]{2,1,0:T(8,128)(2,1)S(1)} collective-permute-done((bf16[4,64,2816]{2,1,0:T(8,128)(2,1)S(1)}, bf16[4,64,2816]{2,1,0:T(8,128)(2,1)S(1)}, u32[]{:S(2)}, u32[]{:S(2)}) %collective-permute-start.61) | collective-permute-done | bytes 1441824 | tf_op jit(solution)/shard_map/ppermute | solution.py:30
  357.5 16.4 %collective-permute-done.28 = bf16[4,64,2048]{2,1,0:T(8,128)(2,1)S(1)} collective-permute-done((bf16[4,64,2048]{2,1,0:T(8,128)(2,1)S(1)}, bf16[4,64,2048]{2,1,0:T(8,128)(2,1)S(1)}, u32[]{:S(2)}, u32[]{:S(2)}) %collective-permute-start.28) | collective-permute-done | bytes 1048608 | tf_op jit(solution)/shard_map/ppermute | solution.py:30
  374.9 21.2 %shard_map.186 = (bf16[8,256,2048]{2,1,0:T(8,128)(2,1)}, f32[8,256,2048]{2,1,0:T(8,128)}, f32[8,256,512]{2,1,0:T(8,128)}, bf16[8,256,512]{2,1,0:T(8,128)(2,1)}, ...) custom-call(bf16[4,256,2048]{2,1,0:T(8,128)(2,1)} %pad_maximum_fusion., ...), custom_call_target="tpu_custom_call" | custom-call | flops 8589934592 | bytes 12601344 | tf_op jit(solution)/shard_map/pallas_call | solution.py:317
  414.8 9.8 collective-permute-done.48
  430.3 24.5 %collective-permute-done.77 = bf16[1,176,2048]{2,1,0:T(8,128)(2,1)S(1)} collective-permute-done((bf16[1,176,2048]{2,1,0:T(8,128)(2,1)}, bf16[1,176,2048]{2,1,0:T(8,128)(2,1)S(1)}, u32[]{:S(2)}, u32[]{:S(2)}) %collective-permute-start.77) | collective-permute-done | bytes 720928 | tf_op jit(solution)/shard_map/ppermute | solution.py:28
  464.4 10.7 collective-permute-done.80
  475.1 12.8 collective-permute-start.82
  500.0 10.8 collective-permute-done.64
  513.2 8.7 shard_map.187
  521.9 21.5 %shard_map.188 = (bf16[8,256,2048]{2,1,0:T(8,128)(2,1)}, f32[8,256,2048]{2,1,0:T(8,128)}, f32[8,256,512]{2,1,0:T(8,128)}, bf16[8,256,512]{2,1,0:T(8,128)(2,1)}, ...) custom-call(bf16[4,256,2048]{2,1,0:T(8,128)(2,1)} %pad_maximum_fusio, ...), custom_call_target="tpu_custom_call", output_to_operand_aliasing={{0}: (6, {}), {1}: (7, {}), {2}: (8, {}), {3}: (9, {}), {4}... | custom-call | flops 8589934592 | bytes 46155776 | tf_op jit(solution)/shard_map/pallas_call | solution.py:317
  589.4 16.0 %collective-permute-done.66 = bf16[4,64,2816]{2,1,0:T(8,128)(2,1)} collective-permute-done((bf16[4,64,2816]{2,1,0:T(8,128)(2,1)}, bf16[4,64,2816]{2,1,0:T(8,128)(2,1)}, u32[]{:S(2)}, u32[]{:S(2)}) %collective-permute-start.66) | collective-permute-done | bytes 1441824 | tf_op jit(solution)/shard_map/ppermute | solution.py:30
  621.7 14.2 collective-permute-done.46
  635.9 16.6 %collective-permute-done.54 = bf16[256,2048]{1,0:T(8,128)(2,1)S(1)} collective-permute-done((bf16[256,2048]{1,0:T(8,128)(2,1)S(1)}, bf16[256,2048]{1,0:T(8,128)(2,1)S(1)}, u32[]{:S(2)}, u32[]{:S(2)}) %collective-permute-start.54) | collective-permute-done | bytes 1048608 | tf_op jit(solution)/shard_map/ppermute | solution.py:24
  662.4 13.4 collective-permute-done.72
  679.9 15.6 %collective-permute-done.70 = bf16[4,64,2816]{2,1,0:T(8,128)(2,1)S(1)} collective-permute-done((bf16[4,64,2816]{2,1,0:T(8,128)(2,1)S(1)}, bf16[4,64,2816]{2,1,0:T(8,128)(2,1)S(1)}, u32[]{:S(2)}, u32[]{:S(2)}) %collective-permute-start.70) | collective-permute-done | bytes 1441824 | tf_op jit(solution)/shard_map/ppermute | solution.py:30
  704.1 20.2 %shard_map.190 = (bf16[8,256,1408]{2,1,0:T(8,128)(2,1)}, bf16[8,256,1408]{2,1,0:T(8,128)(2,1)}, bf16[8,256,1408]{2,1,0:T(8,128)(2,1)}) custom-call(bf16[4,256,2048]{2,1,0:T(8,128)(2,1)} %pad_maximum_fusion.3.x_ref, bf16[2048,2816]{1,0:T(8,128)(2,1)} %bitcast.112.w_ref), custom_call_target="tpu_custom_call" | custom-call | flops 11811160064 | bytes 15728640 | tf_op jit(solution)/shard_map/pallas_call | solution.py:317
  731.0 20.5 %shard_map.191 = (bf16[8,256,1408]{2,1,0:T(8,128)(2,1)}, bf16[8,256,1408]{2,1,0:T(8,128)(2,1)}, bf16[8,256,1408]{2,1,0:T(8,128)(2,1)}) custom-call(bf16[4,256,2048]{2,1,0:T(8,128)(2,1)} %pad_maximum_fusion.2.x_ref, bf16[2048,2816]{1,0:T(8,128)(2,1)} %bitcast.112.w_ref, ...), custom_call_target="tpu_custom_call", output_to_operand_aliasing={{0}: (2, {}), {1}: (3, {}), {2}: (4, {})} | custom-call | flops 11811160064 | bytes 33030144 | tf_op jit(solution)/shard_map/pallas_call | solution.py:317
  751.5 11.3 convolution_convert_fusion.3
  763.8 16.0 %convolution_convert_fusion.1 = bf16[2048,2048]{1,0:T(8,128)(2,1)S(1)} fusion(bf16[2048,1408]{1,0:T(8,128)(2,1)S(1)} %bitcast.664, bf16[1408,2048]{1,0:T(8,128)(2,1)} %bitcast.135.down_ref), kind=kOutput, calls=%fused_computation.3 | convolution fusion | flops 11815354368 | bytes 19922944 | tf_op jit(solution)/shard_map/dot_general | solution.py:101
  785.6 27.5 %shard_map.192 = (bf16[8,256,2816]{2,1,0:T(8,128)(2,1)}, bf16[4,256,2048]{2,1,0:T(8,128)(2,1)}) custom-call(bf16[8,256,2048]{2,1,0:T(8,128)(2,1)} %bitcast_dynamic-update-slice_fusion.14.cot_ref, bf16[1408,2048]{1,0:T(8,128)(2,1)} %bitcast.135.down_ref, bf16[2048,2816]{1,0:T(8,128)(2,1)} %bitcast.112.w_ref, ...), custom_call_target="tpu_custom_call" | custom-call | flops 17716740096 | bytes 37224448 | tf_op jit(solution)/shard_map/pallas_call | solution.py:317
  813.1 27.7 %shard_map.193 = (bf16[8,256,2816]{2,1,0:T(8,128)(2,1)}, bf16[4,256,2048]{2,1,0:T(8,128)(2,1)}) custom-call(bf16[8,256,2048]{2,1,0:T(8,128)(2,1)} %bitcast_dynamic-update-slice_fusion.14.cot_ref, bf16[1408,2048]{1,0:T(8,128)(2,1)} %bitcast.135.down_ref, bf16[2048,2816]{1,0:T(8,128)(2,1)} %bitcast.112.w_ref, ...), custom_call_target="tpu_custom_call", output_to_operand_aliasing={{0}: (5, {})} | custom-call | flops 17716740096 | bytes 48758784 | tf_op jit(solution)/shard_map/pallas_call | solution.py:317
  845.9 19.3 %convolution_convert_fusion.2 = bf16[1024,2816]{1,0:T(8,128)(2,1)} fusion(bf16[2048,2816]{1,0:T(8,128)(2,1)} %bitcast.661, bf16[2048,2048]{1,0:T(8,128)(2,1)} %bitcast.651, s32[]{:T(128)S(6)} %select_n.509), kind=kOutput, calls=%fused_computation.9 | convolution fusion | flops 11814043648 | bytes 21495812 | tf_op jit(solution)/shard_map/dot_general | solution.py:109
  869.3 9.8 add_convert_fusion.2
  879.3 55.9 %collective-permute-start.138 = (bf16[1,176,2048]{2,1,0:T(8,128)(2,1)S(1)}, bf16[1,176,2048]{2,1,0:T(8,128)(2,1)S(1)}, u32[]{:S(2)}, u32[]{:S(2)}) collective-permute-start(bf16[1,176,2048]{2,1,0:T(8,128)(2,1)S(1)} %get-tuple-element.174), channel_id=1, source_target_pairs={{0,1},{4,5},{8,9},{12,13},{16,17},{20,21},{24,25},{28,29}} | collective-permute-start | bytes 2162696 | tf_op jit(solution)/shard_map/ppermute | solution.py:28
  950.4 26.6 %collective-permute-start.139 = (bf16[1,176,2048]{2,1,0:T(8,128)(2,1)S(1)}, bf16[1,176,2048]{2,1,0:T(8,128)(2,1)S(1)}, u32[]{:S(2)}, u32[]{:S(2)}) collective-permute-start(bf16[1,176,2048]{2,1,0:T(8,128)(2,1)S(1)} %fusion.43), channel_id=1, source_target_pairs={{0,1},{1,2},{4,5},{5,6},{8,9},{9,10},{12,13},{13,14},{16,17},{17,1... | collective-permute-start | bytes 2162696 | tf_op jit(solution)/shard_map/ppermute | solution.py:28
  982.9 8.6 collective-permute-done.139
  995.8 13.3 collective-permute-start.140
  1019.3 9.4 shard_map.195
  1031.1 17.9 %collective-permute-done.143 = bf16[1,176,2048]{2,1,0:T(8,128)(2,1)} collective-permute-done((bf16[1,176,2048]{2,1,0:T(8,128)(2,1)}, bf16[1,176,2048]{2,1,0:T(8,128)(2,1)}, u32[]{:S(2)}, u32[]{:S(2)}) %collective-permute-start.143) | collective-permute-done | bytes 720928 | tf_op jit(solution)/shard_map/ppermute | solution.py:28
  1052.7 18.3 %add_convert_fusion = bf16[1024,2816]{1,0:T(8,128)(2,1)S(1)} fusion(bf16[1024,2816]{1,0:T(8,128)(2,1)} %collective-permute-done.127, bf16[2048,2816]{1,0:T(8,128)(2,1)} %bitcast.662, bf16[2048,2048]{1,0:T(8,128)(2,1)} %bitcast.652, s32[]{:T(128)S(6)} %select_n.508), kind=kOutput, calls=%fused_computation | convolution fusion | flops 11819810816 | bytes 27262980 | tf_op jit(solution)/shard_map/dot_general | solution.py:109
  1093.0 17.9 %collective-permute-done.107 = bf16[4,4,128,128]{3,2,1,0:T(8,128)(2,1)S(1)} collective-permute-done((bf16[4,4,128,128]{3,2,1,0:T(8,128)(2,1)S(1)}, bf16[4,4,128,128]{3,2,1,0:T(8,128)(2,1)S(1)}, u32[]{:S(2)}, u32[]{:S(2)}) %collective-permute-start.107) | collective-permute-done | bytes 524320 | tf_op jit(solution)/shard_map/ppermute | solution.py:28
  1111.9 16.1 %shard_map.196 = (bf16[8,256,2048]{2,1,0:T(8,128)(2,1)}, f32[4,1,512]{2,1,0:T(1,128)}) custom-call(f32[8,256,2048]{2,1,0:T(8,128)} %get-tuple-element.65.o_ref.q_ref.f_ref.v_ref, f32[8,256,2048]{2,1,0:T(8,128)} %get-tuple-element.65.o_ref.q_ref.f_ref.v_ref, f32[8,256,2048]{2,1,0:T(8,128)} %get-tuple-element.65.o_ref.q_ref.f_ref.v_ref, ...), custom_call_target="tpu_custom_call" | custom-call | flops 2147483648 | bytes 61876224 | tf_op jit(solution)/shard_map/pallas_call | solution.py:317
  1132.4 9.4 shard_map.194
  1168.4 11.7 collective-permute-done.120
  1198.7 15.3 collective-permute-start.122
  1229.7 15.9 %shard_map.197 = (bf16[8,256,2048]{2,1,0:T(8,128)(2,1)}, f32[4,1,512]{2,1,0:T(1,128)}) custom-call(f32[8,256,2048]{2,1,0:T(8,128)} %get-tuple-element.65.o_ref.q_ref.f_ref.v_ref, f32[8,256,2048]{2,1,0:T(8,128)} %get-tuple-element.65.o_ref.q_ref.f_ref.v_ref, ...), custom_call_target="tpu_custom_call", output_to_operand_aliasing={{0}: (13, {})} | custom-call | flops 2147483648 | bytes 70264832 | tf_op jit(solution)/shard_map/pallas_call | solution.py:317
  1245.6 22.5 %convolution_convert_fusion = bf16[2048,2048]{1,0:T(8,128)(2,1)S(1)} fusion(bf16[2048,2048]{1,0:T(8,128)(2,1)} %bitcast.588, bf16[2048,2048]{1,0:T(8,128)(2,1)} %bitcast.43.w_ref), kind=kOutput, calls=%fused_computation.2 | convolution fusion | flops 17184063488 | bytes 25165824 | tf_op jit(solution)/shard_map/dot_general | solution.py:105
  1268.1 14.5 fusion.20
  1293.6 86.6 %collective-permute-done.110 = bf16[1024,2048]{1,0:T(8,128)(2,1)S(1)} collective-permute-done((bf16[1024,2048]{1,0:T(8,128)(2,1)}, bf16[1024,2048]{1,0:T(8,128)(2,1)S(1)}, u32[]{:S(2)}, u32[]{:S(2)}) %collective-permute-start.110) | collective-permute-done | bytes 4194336 | tf_op jit(solution)/shard_map/ppermute | solution.py:30
  1380.2 11.5 add_convert_fusion.1
  1440.8 9.2 collective-permute-done.112
  1453.7 11.2 collective-permute-start.113
  1502.1 42.5 %psum.7 = f32[6272]{0:T(1024)S(1)} all-reduce(f32[6272]{0:T(1024)S(1)} %pad_maximum_fusion.12), channel_id=1, replica_groups=mesh['dp'=8,'seq'=4] {'dp','seq'}, use_global_device_ids=true, to_apply=%region_14.15 | all-reduce | flops 6272 | bytes 50176 | tf_op jit(solution)/shard_map/psum | solution.py:538
  (698 shorter events, 612.7 us)
Async XLA Ops:
  1.9 62.4 %collective-permute-start.4 = (bf16[256]{0:T(256)(128)(2,1)}, bf16[256]{0:T(256)(128)(2,1)}, u32[]{:S(2)}, u32[]{:S(2)}) collective-permute-start(bf16[256]{0:T(256)(128)(2,1)} %fusion.86), channel_id=1, source_target_pairs={{0,8},{4,12},{8,0},{12,4},{16,24},{20,28},{24,16},{28,20},{1,9},{5... | collective-permute-start | bytes 1544 | tf_op jit(solution)/shard_map/ppermute | solution.py:24
  4.9 62.1 %collective-permute-start.3 = (bf16[256]{0:T(256)(128)(2,1)}, bf16[256]{0:T(256)(128)(2,1)}, u32[]{:S(2)}, u32[]{:S(2)}) collective-permute-start(bf16[256]{0:T(256)(128)(2,1)} %fusion.86), channel_id=1, source_target_pairs={{0,4},{4,0},{8,12},{12,8},{16,20},{20,16},{24,28},{28,24},{1,5},{5... | collective-permute-start | bytes 1544 | tf_op jit(solution)/shard_map/ppermute | solution.py:24
  5.6 83.7 %collective-permute-start.29 = (bf16[2,256]{1,0:T(2,128)(2,1)S(1)}, bf16[2,256]{1,0:T(2,128)(2,1)S(1)}, u32[]{:S(2)}, u32[]{:S(2)}) collective-permute-start(bf16[2,256]{1,0:T(2,128)(2,1)S(1)} %convert_element_type.661), channel_id=1, source_target_pairs={{0,4},{4,0},{8,12},{12,8},{16,20},{20,16},{24,28},{28,24},{1,5},{5... | collective-permute-start | bytes 3080 | tf_op jit(solution)/shard_map/ppermute | solution.py:24
  6.1 76.3 %collective-permute-start.30 = (bf16[2,256]{1,0:T(2,128)(2,1)S(1)}, bf16[2,256]{1,0:T(2,128)(2,1)}, u32[]{:S(2)}, u32[]{:S(2)}) collective-permute-start(bf16[2,256]{1,0:T(2,128)(2,1)S(1)} %convert_element_type.661), channel_id=1, source_target_pairs={{0,8},{4,12},{8,0},{12,4},{16,24},{20,28},{24,16},{28,20},{1,9},{5... | collective-permute-start | bytes 3080 | tf_op jit(solution)/shard_map/ppermute | solution.py:24
  6.1 131.1 %collective-permute-start.37 = (bf16[1,64,2048]{2,1,0:T(8,128)(2,1)}, bf16[1,64,2048]{2,1,0:T(8,128)(2,1)}, u32[]{:S(2)}, u32[]{:S(2)}) collective-permute-start(bf16[1,64,2048]{2,1,0:T(8,128)(2,1)} %bitcast.52), channel_id=1, source_target_pairs={{1,0},{2,1},{3,2},{5,4},{6,5},{7,6},{9,8},{10,9},{11,10},{13,12},{... | collective-permute-start | bytes 786440 | tf_op jit(solution)/shard_map/ppermute | solution.py:28
  82.4 109.0 %collective-permute-start.36 = (bf16[1,64,2048]{2,1,0:T(8,128)(2,1)}, bf16[1,64,2048]{2,1,0:T(8,128)(2,1)}, u32[]{:S(2)}, u32[]{:S(2)}) collective-permute-start(bf16[1,64,2048]{2,1,0:T(8,128)(2,1)} %bitcast.52), channel_id=1, source_target_pairs={{0,1},{1,2},{2,3},{4,5},{5,6},{6,7},{8,9},{9,10},{10,11},{12,13},{... | collective-permute-start | bytes 786440 | tf_op jit(solution)/shard_map/ppermute | solution.py:28
  137.2 261.5 %collective-permute-start.76 = (bf16[1,176,2048]{2,1,0:T(8,128)(2,1)}, bf16[1,176,2048]{2,1,0:T(8,128)(2,1)}, u32[]{:S(2)}, u32[]{:S(2)}) collective-permute-start(bf16[1,176,2048]{2,1,0:T(8,128)(2,1)} %bitcast.120), channel_id=1, source_target_pairs={{1,0},{2,1},{3,2},{5,4},{6,5},{7,6},{9,8},{10,9},{11,10},{13,12},{... | collective-permute-start | bytes 2162696 | tf_op jit(solution)/shard_map/ppermute | solution.py:28
  138.5 78.3 %collective-permute-start.74 = (bf16[1,176,2048]{2,1,0:T(8,128)(2,1)}, bf16[1,176,2048]{2,1,0:T(8,128)(2,1)S(1)}, u32[]{:S(2)}, u32[]{:S(2)}) collective-permute-start(bf16[1,176,2048]{2,1,0:T(8,128)(2,1)} %bitcast.120), channel_id=1, source_target_pairs={{0,16},{4,20},{8,24},{12,28},{16,0},{20,4},{24,8},{28,12},{1,17},{... | collective-permute-start | bytes 2162696 | tf_op jit(solution)/shard_map/ppermute | solution.py:30
  140.8 48.7 %collective-permute-start.38 = (bf16[1,64,2048]{2,1,0:T(8,128)(2,1)}, bf16[1,64,2048]{2,1,0:T(8,128)(2,1)}, u32[]{:S(2)}, u32[]{:S(2)}) collective-permute-start(bf16[1,64,2048]{2,1,0:T(8,128)(2,1)} %collective-permute-done.37), channel_id=1, source_target_pairs={{1,0},{2,1},{3,2},{5,4},{6,5},{7,6},{9,8},{10,9},{11,10},{13,12},{... | collective-permute-start | bytes 786440 | tf_op jit(solution)/shard_map/ppermute | solution.py:28
  192.0 55.9 %collective-permute-start.20 = (bf16[4,64,2048]{2,1,0:T(8,128)(2,1)S(1)}, bf16[4,64,2048]{2,1,0:T(8,128)(2,1)S(1)}, u32[]{:S(2)}, u32[]{:S(2)}) collective-permute-start(bf16[4,64,2048]{2,1,0:T(8,128)(2,1)S(1)} %copy-done.53), channel_id=1, source_target_pairs={{0,1},{1,2},{2,3},{4,5},{5,6},{6,7},{8,9},{9,10},{10,11},{12,13},{... | collective-permute-start | bytes 3145736 | tf_op jit(solution)/shard_map/ppermute | solution.py:28
  245.9 49.8 %collective-permute-start.87 = (bf16[256,2048]{1,0:T(8,128)(2,1)S(1)}, bf16[256,2048]{1,0:T(8,128)(2,1)}, u32[]{:S(2)}, u32[]{:S(2)}) collective-permute-start(bf16[256,2048]{1,0:T(8,128)(2,1)S(1)} %copy-done.51), channel_id=1, source_target_pairs={{0,8},{4,12},{8,0},{12,4},{16,24},{20,28},{24,16},{28,20},{1,9},{5... | collective-permute-start | bytes 3145736 | tf_op jit(solution)/shard_map/ppermute | solution.py:24
  321.8 78.0 %collective-permute-start.75 = (bf16[1,176,2048]{2,1,0:T(8,128)(2,1)}, bf16[1,176,2048]{2,1,0:T(8,128)(2,1)}, u32[]{:S(2)}, u32[]{:S(2)}) collective-permute-start(bf16[1,176,2048]{2,1,0:T(8,128)(2,1)} %bitcast.120), channel_id=1, source_target_pairs={{0,1},{1,2},{2,3},{4,5},{5,6},{6,7},{8,9},{9,10},{10,11},{12,13},{... | collective-permute-start | bytes 2162696 | tf_op jit(solution)/shard_map/ppermute | solution.py:28
  354.1 49.8 %collective-permute-start.47 = (bf16[256,2048]{1,0:T(8,128)(2,1)}, bf16[256,2048]{1,0:T(8,128)(2,1)}, u32[]{:S(2)}, u32[]{:S(2)}) collective-permute-start(bf16[256,2048]{1,0:T(8,128)(2,1)} %get-tuple-element.182), channel_id=1, source_target_pairs={{0,4},{4,0},{8,12},{12,8},{16,20},{20,16},{24,28},{28,24},{1,5},{5... | collective-permute-start | bytes 3145736 | tf_op jit(solution)/shard_map/ppermute | solution.py:24
  354.1 52.2 %collective-permute-start.90 = (bf16[256,2048]{1,0:T(8,128)(2,1)}, bf16[256,2048]{1,0:T(8,128)(2,1)}, u32[]{:S(2)}, u32[]{:S(2)}) collective-permute-start(bf16[256,2048]{1,0:T(8,128)(2,1)} %get-tuple-element.176), channel_id=1, source_target_pairs={{0,8},{4,12},{8,0},{12,4},{16,24},{20,28},{24,16},{28,20},{1,9},{5... | collective-permute-start | bytes 3145736 | tf_op jit(solution)/shard_map/ppermute | solution.py:24
  403.9 53.4 %collective-permute-start.63 = (bf16[4,64,2816]{2,1,0:T(8,128)(2,1)S(1)}, bf16[4,64,2816]{2,1,0:T(8,128)(2,1)S(1)}, u32[]{:S(2)}, u32[]{:S(2)}) collective-permute-start(bf16[4,64,2816]{2,1,0:T(8,128)(2,1)S(1)} %copy-done.49), channel_id=1, source_target_pairs={{1,0},{2,1},{3,2},{5,4},{6,5},{7,6},{9,8},{10,9},{11,10},{13,12},{... | collective-permute-start | bytes 4325384 | tf_op jit(solution)/shard_map/ppermute | solution.py:28
  406.3 48.5 %collective-permute-start.77 = (bf16[1,176,2048]{2,1,0:T(8,128)(2,1)}, bf16[1,176,2048]{2,1,0:T(8,128)(2,1)S(1)}, u32[]{:S(2)}, u32[]{:S(2)}) collective-permute-start(bf16[1,176,2048]{2,1,0:T(8,128)(2,1)} %collective-permute-done.76), channel_id=1, source_target_pairs={{1,0},{2,1},{3,2},{5,4},{6,5},{7,6},{9,8},{10,9},{11,10},{13,12},{... | collective-permute-start | bytes 2162696 | tf_op jit(solution)/shard_map/ppermute | solution.py:28
  424.6 63.4 %collective-permute-start.62 = (bf16[4,64,2816]{2,1,0:T(8,128)(2,1)S(1)}, bf16[4,64,2816]{2,1,0:T(8,128)(2,1)}, u32[]{:S(2)}, u32[]{:S(2)}) collective-permute-start(bf16[4,64,2816]{2,1,0:T(8,128)(2,1)S(1)} %copy-done.49), channel_id=1, source_target_pairs={{0,1},{1,2},{2,3},{4,5},{5,6},{6,7},{8,9},{9,10},{10,11},{12,13},{... | collective-permute-start | bytes 4325384 | tf_op jit(solution)/shard_map/ppermute | solution.py:28
  461.2 49.6 %collective-permute-start.64 = (bf16[4,64,2816]{2,1,0:T(8,128)(2,1)S(1)}, bf16[4,64,2816]{2,1,0:T(8,128)(2,1)}, u32[]{:S(2)}, u32[]{:S(2)}) collective-permute-start(bf16[4,64,2816]{2,1,0:T(8,128)(2,1)S(1)} %collective-permute-done.63), channel_id=1, source_target_pairs={{1,0},{2,1},{3,2},{5,4},{6,5},{7,6},{9,8},{10,9},{11,10},{13,12},{... | collective-permute-start | bytes 4325384 | tf_op jit(solution)/shard_map/ppermute | solution.py:28
  475.1 110.5 %collective-permute-start.82 = (bf16[1,176,2048]{2,1,0:T(8,128)(2,1)}, bf16[1,176,2048]{2,1,0:T(8,128)(2,1)}, u32[]{:S(2)}, u32[]{:S(2)}) collective-permute-start(bf16[1,176,2048]{2,1,0:T(8,128)(2,1)} %collective-permute-done.80), channel_id=1, source_target_pairs={{0,1},{1,2},{2,3},{4,5},{5,6},{6,7},{8,9},{9,10},{10,11},{12,13},{... | collective-permute-start | bytes 2162696 | tf_op jit(solution)/shard_map/ppermute | solution.py:28
  488.0 68.0 %collective-permute-start.67 = (bf16[4,64,2816]{2,1,0:T(8,128)(2,1)}, bf16[4,64,2816]{2,1,0:T(8,128)(2,1)}, u32[]{:S(2)}, u32[]{:S(2)}) collective-permute-start(bf16[4,64,2816]{2,1,0:T(8,128)(2,1)} %collective-permute-done.62), channel_id=1, source_target_pairs={{0,1},{1,2},{2,3},{4,5},{5,6},{6,7},{8,9},{9,10},{10,11},{12,13},{... | collective-permute-start | bytes 4325384 | tf_op jit(solution)/shard_map/ppermute | solution.py:28
  499.1 51.2 %collective-permute-start.79 = (bf16[1,176,2048]{2,1,0:T(8,128)(2,1)}, bf16[1,176,2048]{2,1,0:T(8,128)(2,1)}, u32[]{:S(2)}, u32[]{:S(2)}) collective-permute-start(bf16[1,176,2048]{2,1,0:T(8,128)(2,1)} %get-tuple-element.119), channel_id=1, source_target_pairs={{0,16},{4,20},{8,24},{12,28},{16,0},{20,4},{24,8},{28,12},{1,17},{... | collective-permute-start | bytes 2162696 | tf_op jit(solution)/shard_map/ppermute | solution.py:30
  510.8 52.9 %collective-permute-start.65 = (bf16[4,64,2816]{2,1,0:T(8,128)(2,1)}, bf16[4,64,2816]{2,1,0:T(8,128)(2,1)}, u32[]{:S(2)}, u32[]{:S(2)}) collective-permute-start(bf16[4,64,2816]{2,1,0:T(8,128)(2,1)} %collective-permute-done.64), channel_id=1, source_target_pairs={{1,0},{2,1},{3,2},{5,4},{6,5},{7,6},{9,8},{10,9},{11,10},{13,12},{... | collective-permute-start | bytes 4325384 | tf_op jit(solution)/shard_map/ppermute | solution.py:28
  556.0 102.6 %collective-permute-start.69 = (bf16[4,64,2816]{2,1,0:T(8,128)(2,1)}, bf16[4,64,2816]{2,1,0:T(8,128)(2,1)}, u32[]{:S(2)}, u32[]{:S(2)}) collective-permute-start(bf16[4,64,2816]{2,1,0:T(8,128)(2,1)} %collective-permute-done.67), channel_id=1, source_target_pairs={{0,1},{1,2},{2,3},{4,5},{5,6},{6,7},{8,9},{9,10},{10,11},{12,13},{... | collective-permute-start | bytes 4325384 | tf_op jit(solution)/shard_map/ppermute | solution.py:28
  762.8 106.4 %collective-permute-start.137 = (bf16[704,2048]{1,0:T(8,128)(2,1)}, bf16[704,2048]{1,0:T(8,128)(2,1)}, u32[]{:S(2)}, u32[]{:S(2)}) collective-permute-start(bf16[704,2048]{1,0:T(8,128)(2,1)} %convolution_convert_fusion.3), channel_id=1, source_target_pairs={{0,16},{4,20},{8,24},{12,28},{16,0},{20,4},{24,8},{28,12},{1,17},{... | collective-permute-start | bytes 8650760 | tf_op jit(solution)/shard_map/ppermute | solution.py:30
  785.4 191.6 %collective-permute-start.84 = (bf16[2,2,256,2048]{3,2,1,0:T(8,128)(2,1)}, bf16[2,2,256,2048]{3,2,1,0:T(8,128)(2,1)}, u32[]{:S(2)}, u32[]{:S(2)}) collective-permute-start(bf16[2,2,256,2048]{3,2,1,0:T(8,128)(2,1)} %pad_maximum_fusion.4), channel_id=1, source_target_pairs={{0,4},{4,0},{8,12},{12,8},{16,20},{20,16},{24,28},{28,24},{1,5},{5... | collective-permute-start | bytes 12582920 | tf_op jit(solution)/shard_map/ppermute | solution.py:24
  865.2 187.5 %collective-permute-start.127 = (bf16[1024,2816]{1,0:T(8,128)(2,1)}, bf16[1024,2816]{1,0:T(8,128)(2,1)}, u32[]{:S(2)}, u32[]{:S(2)}) collective-permute-start(bf16[1024,2816]{1,0:T(8,128)(2,1)} %convolution_convert_fusion.2), channel_id=1, source_target_pairs={{0,16},{4,20},{8,24},{12,28},{16,0},{20,4},{24,8},{28,12},{1,17},{... | collective-permute-start | bytes 17301512 | tf_op jit(solution)/shard_map/ppermute | solution.py:30
  866.7 68.5 %collective-permute-start.93 = (bf16[256,2048]{1,0:T(8,128)(2,1)S(1)}, bf16[256,2048]{1,0:T(8,128)(2,1)S(1)}, u32[]{:S(2)}, u32[]{:S(2)}) collective-permute-start(bf16[256,2048]{1,0:T(8,128)(2,1)S(1)} %fusion.56), channel_id=1, source_target_pairs={{0,8},{4,12},{8,0},{12,4},{16,24},{20,28},{24,16},{28,20},{1,9},{5... | collective-permute-start | bytes 3145736 | tf_op jit(solution)/shard_map/ppermute | solution.py:24
  868.2 67.9 %collective-permute-start.95 = (bf16[256,2048]{1,0:T(8,128)(2,1)S(1)}, bf16[256,2048]{1,0:T(8,128)(2,1)S(1)}, u32[]{:S(2)}, u32[]{:S(2)}) collective-permute-start(bf16[256,2048]{1,0:T(8,128)(2,1)S(1)} %fusion.57), channel_id=1, source_target_pairs={{0,8},{4,12},{8,0},{12,4},{16,24},{20,28},{24,16},{28,20},{1,9},{5... | collective-permute-start | bytes 3145736 | tf_op jit(solution)/shard_map/ppermute | solution.py:24
  879.3 70.9 %collective-permute-start.138 = (bf16[1,176,2048]{2,1,0:T(8,128)(2,1)S(1)}, bf16[1,176,2048]{2,1,0:T(8,128)(2,1)S(1)}, u32[]{:S(2)}, u32[]{:S(2)}) collective-permute-start(bf16[1,176,2048]{2,1,0:T(8,128)(2,1)S(1)} %get-tuple-element.174), channel_id=1, source_target_pairs={{0,1},{4,5},{8,9},{12,13},{16,17},{20,21},{24,25},{28,29}} | collective-permute-start | bytes 2162696 | tf_op jit(solution)/shard_map/ppermute | solution.py:28
  935.2 46.4 %collective-permute-start.141 = (bf16[1,176,2048]{2,1,0:T(8,128)(2,1)S(1)}, bf16[1,176,2048]{2,1,0:T(8,128)(2,1)S(1)}, u32[]{:S(2)}, u32[]{:S(2)}) collective-permute-start(bf16[1,176,2048]{2,1,0:T(8,128)(2,1)S(1)} %get-tuple-element.175), channel_id=1, source_target_pairs={{3,2},{7,6},{11,10},{15,14},{19,18},{23,22},{27,26},{31,30}} | collective-permute-start | bytes 2162696 | tf_op jit(solution)/shard_map/ppermute | solution.py:28
  981.6 100.8 %collective-permute-start.85 = (bf16[2,256,2048]{2,1,0:T(8,128)(2,1)}, bf16[2,256,2048]{2,1,0:T(8,128)(2,1)}, u32[]{:S(2)}, u32[]{:S(2)}) collective-permute-start(bf16[2,256,2048]{2,1,0:T(8,128)(2,1)} %fusion.12), channel_id=1, source_target_pairs={{0,8},{4,12},{8,0},{12,4},{16,24},{20,28},{24,16},{28,20},{1,9},{5... | collective-permute-start | bytes 6291464 | tf_op jit(solution)/shard_map/ppermute | solution.py:24
  1015.5 73.8 %collective-permute-start.97 = (bf16[256,2048]{1,0:T(8,128)(2,1)S(1)}, bf16[256,2048]{1,0:T(8,128)(2,1)}, u32[]{:S(2)}, u32[]{:S(2)}) collective-permute-start(bf16[256,2048]{1,0:T(8,128)(2,1)S(1)} %get-tuple-element.109), channel_id=1, source_target_pairs={{0,8},{4,12},{8,0},{12,4},{16,24},{20,28},{24,16},{28,20},{1,9},{5... | collective-permute-start | bytes 3145736 | tf_op jit(solution)/shard_map/ppermute | solution.py:24
  1031.0 58.6 %collective-permute-start.96 = (bf16[256,2048]{1,0:T(8,128)(2,1)S(1)}, bf16[256,2048]{1,0:T(8,128)(2,1)S(1)}, u32[]{:S(2)}, u32[]{:S(2)}) collective-permute-start(bf16[256,2048]{1,0:T(8,128)(2,1)S(1)} %get-tuple-element.109), channel_id=1, source_target_pairs={{0,4},{4,0},{8,12},{12,8},{16,20},{20,16},{24,28},{28,24},{1,5},{5... | collective-permute-start | bytes 3145736 | tf_op jit(solution)/shard_map/ppermute | solution.py:24
  1074.2 82.7 %collective-permute-start.128 = (bf16[4,64,2816]{2,1,0:T(8,128)(2,1)}, bf16[4,64,2816]{2,1,0:T(8,128)(2,1)}, u32[]{:S(2)}, u32[]{:S(2)}) collective-permute-start(bf16[4,64,2816]{2,1,0:T(8,128)(2,1)} %get-tuple-element.156), channel_id=1, source_target_pairs={{0,1},{4,5},{8,9},{12,13},{16,17},{20,21},{24,25},{28,29}} | collective-permute-start | bytes 4325384 | tf_op jit(solution)/shard_map/ppermute | solution.py:28
  1080.3 76.7 %collective-permute-start.131 = (bf16[4,64,2816]{2,1,0:T(8,128)(2,1)}, bf16[4,64,2816]{2,1,0:T(8,128)(2,1)}, u32[]{:S(2)}, u32[]{:S(2)}) collective-permute-start(bf16[4,64,2816]{2,1,0:T(8,128)(2,1)} %get-tuple-element.157), channel_id=1, source_target_pairs={{3,2},{7,6},{11,10},{15,14},{19,18},{23,22},{27,26},{31,30}} | collective-permute-start | bytes 4325384 | tf_op jit(solution)/shard_map/ppermute | solution.py:28
  1161.1 52.9 %collective-permute-start.129 = (bf16[4,64,2816]{2,1,0:T(8,128)(2,1)}, bf16[4,64,2816]{2,1,0:T(8,128)(2,1)}, u32[]{:S(2)}, u32[]{:S(2)}) collective-permute-start(bf16[4,64,2816]{2,1,0:T(8,128)(2,1)} %get-tuple-element.154), channel_id=1, source_target_pairs={{0,1},{1,2},{4,5},{5,6},{8,9},{9,10},{12,13},{13,14},{16,17},{17,1... | collective-permute-start | bytes 4325384 | tf_op jit(solution)/shard_map/ppermute | solution.py:28
  1163.7 50.3 %collective-permute-start.132 = (bf16[4,64,2816]{2,1,0:T(8,128)(2,1)}, bf16[4,64,2816]{2,1,0:T(8,128)(2,1)}, u32[]{:S(2)}, u32[]{:S(2)}) collective-permute-start(bf16[4,64,2816]{2,1,0:T(8,128)(2,1)} %get-tuple-element.155), channel_id=1, source_target_pairs={{3,2},{2,1},{7,6},{6,5},{11,10},{10,9},{15,14},{14,13},{19,18},{18... | collective-permute-start | bytes 4325384 | tf_op jit(solution)/shard_map/ppermute | solution.py:28
  1217.6 69.9 %collective-permute-start.130 = (bf16[4,64,2816]{2,1,0:T(8,128)(2,1)}, bf16[4,64,2816]{2,1,0:T(8,128)(2,1)}, u32[]{:S(2)}, u32[]{:S(2)}) collective-permute-start(bf16[4,64,2816]{2,1,0:T(8,128)(2,1)} %get-tuple-element.152), channel_id=1, source_target_pairs={{0,1},{1,2},{2,3},{4,5},{5,6},{6,7},{8,9},{9,10},{10,11},{12,13},{... | collective-permute-start | bytes 4325384 | tf_op jit(solution)/shard_map/ppermute | solution.py:28
  1220.6 68.2 %collective-permute-start.133 = (bf16[4,64,2816]{2,1,0:T(8,128)(2,1)S(1)}, bf16[4,64,2816]{2,1,0:T(8,128)(2,1)}, u32[]{:S(2)}, u32[]{:S(2)}) collective-permute-start(bf16[4,64,2816]{2,1,0:T(8,128)(2,1)S(1)} %get-tuple-element.153), channel_id=1, source_target_pairs={{3,2},{2,1},{1,0},{7,6},{6,5},{5,4},{11,10},{10,9},{9,8},{15,14},{... | collective-permute-start | bytes 4325384 | tf_op jit(solution)/shard_map/ppermute | solution.py:28
  1222.1 175.7 %collective-permute-start.123 = (bf16[1,64,2048]{2,1,0:T(8,128)(2,1)S(1)}, bf16[1,64,2048]{2,1,0:T(8,128)(2,1)S(1)}, u32[]{:S(2)}, u32[]{:S(2)}) collective-permute-start(bf16[1,64,2048]{2,1,0:T(8,128)(2,1)S(1)} %get-tuple-element.212), channel_id=1, source_target_pairs={{0,1},{1,2},{2,3},{4,5},{5,6},{6,7},{8,9},{9,10},{10,11},{12,13},{... | collective-permute-start | bytes 786440 | tf_op jit(solution)/shard_map/ppermute | solution.py:28
  1226.7 60.2 %collective-permute-start.125 = (bf16[1,64,2048]{2,1,0:T(8,128)(2,1)S(1)}, bf16[1,64,2048]{2,1,0:T(8,128)(2,1)S(1)}, u32[]{:S(2)}, u32[]{:S(2)}) collective-permute-start(bf16[1,64,2048]{2,1,0:T(8,128)(2,1)S(1)} %get-tuple-element.213), channel_id=1, source_target_pairs={{3,2},{2,1},{7,6},{6,5},{11,10},{10,9},{15,14},{14,13},{19,18},{18... | collective-permute-start | bytes 786440 | tf_op jit(solution)/shard_map/ppermute | solution.py:28
  1286.9 148.3 %collective-permute-start.108 = (bf16[2,2,256,2048]{3,2,1,0:T(8,128)(2,1)}, bf16[2,2,256,2048]{3,2,1,0:T(8,128)(2,1)}, u32[]{:S(2)}, u32[]{:S(2)}) collective-permute-start(bf16[2,2,256,2048]{3,2,1,0:T(8,128)(2,1)} %pad_maximum_fusion.7), channel_id=1, source_target_pairs={{0,4},{4,0},{8,12},{12,8},{16,20},{20,16},{24,28},{28,24},{1,5},{5... | collective-permute-start | bytes 12582920 | tf_op jit(solution)/shard_map/ppermute | solution.py:24
  1286.9 93.3 %collective-permute-start.110 = (bf16[1024,2048]{1,0:T(8,128)(2,1)}, bf16[1024,2048]{1,0:T(8,128)(2,1)S(1)}, u32[]{:S(2)}, u32[]{:S(2)}) collective-permute-start(bf16[1024,2048]{1,0:T(8,128)(2,1)} %fusion.20), channel_id=1, source_target_pairs={{0,16},{4,20},{8,24},{12,28},{16,0},{20,4},{24,8},{28,12},{1,17},{... | collective-permute-start | bytes 12582920 | tf_op jit(solution)/shard_map/ppermute | solution.py:30
  1287.5 112.1 %collective-permute-start.126 = (bf16[1,64,2048]{2,1,0:T(8,128)(2,1)S(1)}, bf16[1,64,2048]{2,1,0:T(8,128)(2,1)S(1)}, u32[]{:S(2)}, u32[]{:S(2)}) collective-permute-start(bf16[1,64,2048]{2,1,0:T(8,128)(2,1)S(1)} %fusion.62), channel_id=1, source_target_pairs={{3,2},{2,1},{1,0},{7,6},{6,5},{5,4},{11,10},{10,9},{9,8},{15,14},{... | collective-permute-start | bytes 786440 | tf_op jit(solution)/shard_map/ppermute | solution.py:28
  1293.3 107.3 %collective-permute-start.134 = (bf16[64,2816]{1,0:T(8,128)(2,1)S(1)}, bf16[64,2816]{1,0:T(8,128)(2,1)S(1)}, u32[]{:S(2)}, u32[]{:S(2)}) collective-permute-start(bf16[64,2816]{1,0:T(8,128)(2,1)S(1)} %get-tuple-element.191), channel_id=1, source_target_pairs={{0,4},{4,0},{8,12},{12,8},{16,20},{20,16},{24,28},{28,24},{1,5},{5... | collective-permute-start | bytes 1081352 | tf_op jit(solution)/shard_map/ppermute | solution.py:24
  1494.9 51.1 %collective-permute-start.117 = (bf16[64,2048]{1,0:T(8,128)(2,1)}, bf16[64,2048]{1,0:T(8,128)(2,1)S(1)}, u32[]{:S(2)}, u32[]{:S(2)}) collective-permute-start(bf16[64,2048]{1,0:T(8,128)(2,1)} %get-tuple-element.218), channel_id=1, source_target_pairs={{0,4},{4,0},{8,12},{12,8},{16,20},{20,16},{24,28},{28,24},{1,5},{5... | collective-permute-start | bytes 786440 | tf_op jit(solution)/shard_map/ppermute | solution.py:24
  1494.9 51.1 %collective-permute-start.119 = (bf16[64,2048]{1,0:T(8,128)(2,1)}, bf16[64,2048]{1,0:T(8,128)(2,1)S(1)}, u32[]{:S(2)}, u32[]{:S(2)}) collective-permute-start(bf16[64,2048]{1,0:T(8,128)(2,1)} %get-tuple-element.219), channel_id=1, source_target_pairs={{0,8},{4,12},{8,0},{12,4},{16,24},{20,28},{24,16},{28,20},{1,9},{5... | collective-permute-start | bytes 786440 | tf_op jit(solution)/shard_map/ppermute | solution.py:24
  1495.9 50.1 %collective-permute-start.118 = (bf16[64,2048]{1,0:T(8,128)(2,1)S(1)}, bf16[64,2048]{1,0:T(8,128)(2,1)S(1)}, u32[]{:S(2)}, u32[]{:S(2)}) collective-permute-start(bf16[64,2048]{1,0:T(8,128)(2,1)S(1)} %get-tuple-element.220), channel_id=1, source_target_pairs={{0,12},{4,8},{8,4},{12,0},{16,28},{20,24},{24,20},{28,16},{1,13},{... | collective-permute-start | bytes 786440 | tf_op jit(solution)/shard_map/ppermute | solution.py:24
  (182 other events, 3742.3 us)

commit v2 on v1

v2 whole, which is shorter than its diff:
```python
from functools import partial

import jax
import jax.numpy as jnp
from jax import lax
from jax.experimental import pallas as pl
from jax.experimental.pallas import tpu as pltpu
from jax.sharding import Mesh, PartitionSpec as P

HEAD = 128
TEAM = 4
EPSILON = 1e-06
SCALE = HEAD**-0.5
F32 = jnp.float32
BF16 = jnp.bfloat16
VMEM_LIMIT = 60 * 1024 * 1024


class Places:
    def __init__(self, ny, nz):
        self.ny, self.nz = ny, nz
        self.rank, self.y, self.z = lax.axis_index("team"), lax.axis_index("y"), lax.axis_index("seq")

    def swap(self, value, bits):
        return lax.ppermute(value, "team", [(i, i ^ bits) for i in range(TEAM)])

    def swap_y(self, value, bits):
        return lax.ppermute(value, "y", [(i, i ^ bits) for i in range(self.ny)])

    def swap_z(self, value, bits):
        return lax.ppermute(value, "seq", [(i, i ^ bits) for i in range(self.nz)])

    def by_rank(self, stack):
        odd, high = (self.rank & 1) == 1, (self.rank & 2) == 2
        stack = jnp.where(odd, jnp.concatenate([stack[1:2], stack[0:1], stack[3:4], stack[2:3]]), stack)
        return jnp.where(high, jnp.concatenate([stack[2:], stack[:2]]), stack)

    def team_gather(self, own):
        one, two = self.swap(own, 1), self.swap(own, 2)
        return [own, one, two, self.swap(two, 1)]

    def team_sum(self, even, odd, first_held, *held):
        near = self.swap(after(odd, *first_held), 1)
        sent = (even[:, 1].astype(F32) + after(near, *held)[:, 1].astype(F32)).astype(BF16)
        return even[:, 0].astype(F32) + near[:, 0].astype(F32) + self.swap(sent, 2).astype(F32), sent


    def gather_blocks(self, own):
        found = {(0, 0): own}
        for step in [1 << i for i in reversed(range(self.nz.bit_length() - 1))]:
            found.update({(0, dz ^ step): self.swap_z(v, step) for (_, dz), v in list(found.items())})
        for step in [1 << i for i in range(self.ny.bit_length() - 1)]:
            found.update({(dy ^ step, dz): self.swap_y(v, step) for (dy, dz), v in list(found.items())})
        return found

    def everyone_sum(self, value):
        for step in (2, 1):
            value = value + self.swap(value, step)
        for step in [1 << i for i in reversed(range(self.ny.bit_length() - 1))]:
            value = value + self.swap_y(value, step)
        for step in [1 << i for i in reversed(range(self.nz.bit_length() - 1))]:
            value = value + self.swap_z(value, step)
        return value


class Weight:
    def __init__(self, at, found):
        self.ny, self.nz = at.ny, at.nz
        if isinstance(found, dict):
            self.s, self.rows, self.n = found[0, 0].shape
            self.keys, self.blocks = list(found), list(found.values())
        else:
            self.s, self.rows, self.n = found.shape[1:]
            self.keys, self.blocks = None, [found]
        self.height = self.ny * self.nz * self.s * self.rows
        self.split = self.rows % 16 == 0
        if not self.split:
            if self.keys:
                found = jnp.zeros((self.ny, self.nz) + self.blocks[0].shape, BF16)
                for (dy, dz), block in zip(self.keys, self.blocks):
                    found = lax.dynamic_update_slice(found, block[None, None], (at.y ^ dy, at.z ^ dz, 0, 0, 0))
            found = found.reshape(self.ny, self.nz, self.s, self.rows, self.n)
            self.blocks = [jnp.swapaxes(found, 1, 2).reshape(self.height, self.n)]

    @property
    def copies(self):
        return self.ny * self.nz * self.s if self.split else 1

    def load(self, refs, place_ref, into, sems):
        for copy in self.copies_of(refs, place_ref, into, sems):
            copy.start()

    def copies_of(self, refs, place_ref, into, sems):
        if not self.split:
            return [pltpu.make_async_copy(refs[0], into, sems.at[0])]
        rank, y, z = place_ref[0], place_ref[1], place_ref[2]
        if self.keys:
            blocks = [(y ^ dy, z ^ dz, ref) for (dy, dz), ref in zip(self.keys, refs)]
        else:
            blocks = [(i // self.nz, i % self.nz, refs[0].at[i]) for i in range(self.ny * self.nz)]
        copies = []
        for there_y, there_z, ref in blocks:
            for j in range(self.s):
                s = rank ^ j if self.s > 1 else 0
                row = ((there_y * self.s + s) * self.nz + there_z) * self.rows
                if not isinstance(row, int):
                    row = pl.multiple_of(row, self.rows)
                copies.append(pltpu.make_async_copy(ref.at[j], into.at[pl.ds(row, self.rows)], sems.at[len(copies)]))
        return copies


def nn(a, b):
    return jnp.dot(a, b, preferred_element_type=F32)


def nt(a, b):
    return lax.dot_general(a, b, (((1,), (1,)), ((), ())), preferred_element_type=F32)


def tn(a, b):
    return lax.dot_general(a, b, (((0,), (0,)), ((), ())), preferred_element_type=F32)


def add_up(matrix, value):
    high = value.astype(BF16)
    rest = value - high.astype(F32)
    mid = rest.astype(BF16)
    low = (rest - mid.astype(F32)).astype(BF16)
    return nn(matrix, high) + nn(matrix, mid) + nn(matrix, low)


def triangle(n, lower):
    row = lax.broadcasted_iota(jnp.int32, (n, n), 0)
    col = lax.broadcasted_iota(jnp.int32, (n, n), 1)
    return row >= col if lower else row <= col


def sigmoid(z):
    return 1.0 / (1.0 + jnp.exp(-z))


def gates(f_pre, lower):
    small = jnp.exp(-jnp.abs(f_pre))
    big_part = 1.0 / (1.0 + small)
    small_part = small * big_part
    positive = f_pre >= 0
    opened = jnp.where(positive, big_part, small_part)
    closed = jnp.where(positive, small_part, big_part)
    return opened, closed, lower + (1.0 - lower) * opened


def wide_blocks(width):
    step = 512
    return [(a, min(a + step, width)) for a in range(0, width, step)]


def take_piece(step, piece_refs, into_ref):
    for j, ref in enumerate(piece_refs):

        @pl.when(step == j)
        def _(ref=ref):
            into_ref[0] = ref[...]


def put_share(step, even_ref, odd_ref, a, b, value):
    value = value.astype(BF16)

    @pl.when(step % 2 == 0)
    def _():
        even_ref[0, :, a:b] = value

    @pl.when(step % 2 == 1)
    def _():
        odd_ref[0, :, a:b] = value


def pick_kernel(strip, place_ref, w_ref, extra_ref, *out_refs):
    rank = place_ref[0]
    count = w_ref.shape[1] // (TEAM * strip)
    for j, out_ref in enumerate(out_refs):
        for k in range(count):
            at = pl.multiple_of((k * TEAM + (rank ^ j)) * strip, strip)
            out_ref[:, k * strip : (k + 1) * strip] = w_ref[:, pl.ds(at, strip)]
        out_ref[:, count * strip :] = extra_ref[...]


def mix_kernel(strip, step, fetch, piece_refs, place_ref, row_ref, col_ref, *refs):
    normed_ref, proj_ref, run_ref, qd_ref, kg_ref, ins_ref, leave_ref, fade_ref, scales_ref, lower_ref = refs
    channels = lower_ref.shape[1]
    (w_ref,) = fetch()

    @pl.when(step == 0)
    def _():
        row = lax.broadcasted_iota(jnp.int32, (8, HEAD), 0)
        col = lax.broadcasted_iota(jnp.int32, (8, HEAD), 1)
        pick = jnp.where(row == col, 1.0, 0.0).astype(BF16)
        scales_ref[...] = nt(pick, w_ref[:, 4 * channels :])
        for k in range(channels // strip):
            at = pl.multiple_of((k * TEAM + place_ref[0]) * strip, strip)
            lower_ref[:, k * strip : (k + 1) * strip] = sigmoid(scales_ref[2:3, pl.ds(at, strip)])

    gain = scales_ref[0:1]
    take_piece(step, piece_refs, normed_ref)
    x = normed_ref[0].astype(F32)
    scale = lax.rsqrt(jnp.mean(x * x, axis=-1, keepdims=True) + EPSILON)
    normed_ref[0] = (x * scale * gain).astype(BF16)
    for a, b in wide_blocks(4 * channels):
        proj_ref[0, :, a:b] = nn(normed_ref[0], w_ref[:, a:b])
    lower = lower_ref[...]
    q_pre = proj_ref[0, :, 0:channels]
    f_pre = proj_ref[0, :, channels : 2 * channels]
    _, closed, decays = gates(f_pre, lower)
    keys = (1.0 - lower) * closed
    length = x.shape[0]
    causal = triangle(length, True)
    running = add_up(causal.astype(BF16), jnp.log(decays))
    run_ref[0] = running
    row, col = row_ref[0], col_ref[0]
    alive = (col[length - 1 :] == 0).astype(F32)
    tail = (col == col[length - 1 :]).astype(F32)
    final = running[length - 1 :]
    fade_ref[0] = jnp.exp(final) * alive
    qd_ref[0] = (q_pre * sigmoid(q_pre) * jnp.exp(running)).astype(BF16)
    kg_ref[0] = (keys * jnp.exp(-running)).astype(BF16)
    last = (keys * jnp.exp(final - running) * tail).astype(BF16)
    mask = jnp.where(causal & (col == row), 1.0, 0.0)
    for h in range(channels // HEAD):
        cut = slice(h * HEAD, (h + 1) * HEAD)
        values = proj_ref[0, :, 2 * channels + h * HEAD : 2 * channels + (h + 1) * HEAD].astype(BF16)
        scores = (nt(qd_ref[0, :, cut], kg_ref[0, :, cut]) * mask).astype(BF16)
        ins_ref[0, :, cut] = nn(scores, values) * SCALE
        leave_ref[0, h] = tn(last[:, cut], values)


def out_kernel(step, fetch, piece_refs, ins_ref, qd_ref, o_ref, state_ref, col_ref, group_ref, *refs):
    mixed_ref, gated_ref, even_ref, odd_ref = refs
    channels = ins_ref.shape[2]
    alive = (col_ref[0] == 0).astype(F32) * SCALE
    for h in range(channels // HEAD):
        cut = slice(h * HEAD, (h + 1) * HEAD)
        mixed = ins_ref[0, :, cut] + alive * nn(qd_ref[0, :, cut], state_ref[0, h])
        mixed_ref[0, :, cut] = mixed
        scale = lax.rsqrt(jnp.mean(mixed * mixed, axis=-1, keepdims=True) + EPSILON)
        o_pre = o_ref[0, :, cut]
        gated_ref[0, :, cut] = (mixed * scale * group_ref[...] * (o_pre * sigmoid(o_pre))).astype(BF16)
    (w_ref,) = fetch()
    for a, b in wide_blocks(w_ref.shape[1]):
        put_share(step, even_ref, odd_ref, a, b, nn(gated_ref[0], w_ref[:, a:b]))


def up_kernel(step, fetch, piece_refs, normed_ref, hidden_ref, first_ref, second_ref):
    width = hidden_ref.shape[2]
    take_piece(step, piece_refs, normed_ref)
    (w_ref,) = fetch()
    for a, b in wide_blocks(width):
        gate = nn(normed_ref[0], w_ref[:, a:b])
        up = nn(normed_ref[0], w_ref[:, width + a : width + b])
        s = sigmoid(gate)
        silu = gate * s
        hidden_ref[0, :, a:b] = (silu * up).astype(BF16)
        first_ref[0, :, a:b] = (up * (s * (1.0 + gate * (1.0 - s)))).astype(BF16)
        second_ref[0, :, a:b] = silu.astype(BF16)


def down_back_kernel(step, fetch, piece_refs, cot_ref, first_ref, second_ref, both_ref, even_ref, odd_ref):
    width = first_ref.shape[2]
    down_ref, w_ref = fetch()
    for a, b in wide_blocks(width):
        d_hidden = nt(cot_ref[0], down_ref[a:b, :])
        both_ref[0, :, a:b] = (d_hidden * first_ref[0, :, a:b].astype(F32)).astype(BF16)
        both_ref[0, :, width + a : width + b] = (d_hidden * second_ref[0, :, a:b].astype(F32)).astype(BF16)
    for a, b in wide_blocks(w_ref.shape[0]):
        put_share(step, even_ref, odd_ref, a, b, nt(both_ref[0], w_ref[a:b, :]))


def out_back_kernel(step, fetch, piece_refs, mixed_ref, o_ref, qd_ref, col_ref, group_ref, *refs):
    branch_ref, d_o_ref, g_ref, toward_ref, sum_ref = refs
    channels = mixed_ref.shape[2]
    take_piece(step, piece_refs, branch_ref)
    alive = (col_ref[0] == 0).astype(F32)
    group = group_ref[...]
    (w_ref,) = fetch()
    d_gated_all = nt(branch_ref[0], w_ref[...])
    for h in range(channels // HEAD):
        cut = slice(h * HEAD, (h + 1) * HEAD)
        d_gated = d_gated_all[:, cut]
        mixed = mixed_ref[0, :, cut]
        scale = lax.rsqrt(jnp.mean(mixed * mixed, axis=-1, keepdims=True) + EPSILON)
        unit = mixed * scale
        o_pre = o_ref[0, :, cut]
        s = sigmoid(o_pre)
        silu = o_pre * s
        both = d_gated * unit
        d_o_ref[0, :, cut] = (both * group * (s * (1.0 + o_pre * (1.0 - s)))).astype(BF16)
        sum_ref[0, :, cut] = jnp.sum(both * silu, axis=0, keepdims=True)
        d_unit = d_gated * group * silu
        d_mixed = scale * (d_unit - unit * jnp.mean(d_unit * unit, axis=-1, keepdims=True))
        g = (d_mixed * SCALE).astype(BF16)
        g_ref[0, :, cut] = g
        reach = (qd_ref[0, :, cut].astype(F32) * alive).astype(BF16)
        toward_ref[0, h] = tn(reach, g)


def mix_back_kernel(
    step, fetch, piece_refs, q_ref, f_ref, v_ref, run_ref, qd_ref, kg_ref, g_ref, state_ref, adjoint_ref, lower_ref,
    row_ref, col_ref, d_o_ref, d_q_ref, d_fv_ref, sum_ref, even_ref, odd_ref,
):
    channels = lower_ref.shape[1]
    length = row_ref.shape[2]
    lower = lower_ref[...]
    row, col = row_ref[0], col_ref[0]
    alive = (col == 0).astype(F32)
    alive_end = alive[length - 1 :]
    tail = (col == col[length - 1 :]).astype(F32)
    mask = jnp.where(triangle(length, True) & (col == row), 1.0, 0.0)
    later = triangle(length, False).astype(BF16)
    eye = lax.broadcasted_iota(jnp.int32, (HEAD, HEAD), 0) == lax.broadcasted_iota(jnp.int32, (HEAD, HEAD), 1)
    for h in range(channels // HEAD):
        cut = slice(h * HEAD, (h + 1) * HEAD)
        q_pre, f_pre = q_ref[0, :, cut], f_ref[0, :, cut]
        values = v_ref[0, :, cut].astype(BF16)
        running = run_ref[0, :, cut]
        qd, kg, g = qd_ref[0, :, cut], kg_ref[0, :, cut], g_ref[0, :, cut]
        state, adjoint = state_ref[0, h], adjoint_ref[0, h]
        low = lower[:, cut]
        opened, closed, decays = gates(f_pre, low)
        keys = (1.0 - low) * closed
        final = running[length - 1 :]
        last_factor = jnp.exp(final - running) * tail
        last = (keys * last_factor).astype(BF16)
        scores = (nt(qd, kg) * mask).astype(BF16)
        d_values = tn(scores, g) + nn(last, adjoint)
        d_scores = (nt(g, values) * mask).astype(BF16)
        d_qd = nn(d_scores, kg) + alive * nt(g, state)
        d_kg = tn(d_scores, qd)
        d_last = nt(values, adjoint)
        part_last = d_last * last.astype(F32)
        moved = d_qd * qd.astype(F32) - d_kg * kg.astype(F32) - part_last
        passed = jnp.sum(adjoint.astype(F32) * state.astype(F32), axis=1, keepdims=True)
        passed = jnp.sum(jnp.where(eye, passed, 0.0), axis=0, keepdims=True)
        d_final = jnp.sum(part_last, axis=0, keepdims=True) + passed * jnp.exp(final) * alive_end
        d_log = add_up(later, moved) + d_final
        d_queries = d_qd * jnp.exp(running)
        d_keys = d_kg * jnp.exp(-running) + d_last * last_factor
        common = d_log / decays - d_keys
        s = sigmoid(q_pre)
        d_q_ref[0, :, cut] = (d_queries * (s * (1.0 + q_pre * (1.0 - s)))).astype(BF16)
        d_fv_ref[0, :, cut] = ((1.0 - low) * opened * closed * common).astype(BF16)
        d_fv_ref[0, :, channels + h * HEAD : channels + (h + 1) * HEAD] = d_values.astype(BF16)
        sum_ref[0, :, cut] = jnp.sum(closed * common, axis=0, keepdims=True)
    (w_ref,) = fetch()
    parts = [(0, d_q_ref), (channels, d_fv_ref), (3 * channels, d_o_ref)]
    for a, b in wide_blocks(w_ref.shape[0]):
        value = sum(nt(ref[0], w_ref[a:b, k : k + ref.shape[2]]) for k, ref in parts)
        put_share(step, even_ref, odd_ref, a, b, value)


def share_kernel(step, fetch, piece_refs, left_ref, even_ref, odd_ref):
    (w_ref,) = fetch()
    for a, b in wide_blocks(w_ref.shape[1]):
        put_share(step, even_ref, odd_ref, a, b, nn(left_ref[0], w_ref[:, a:b]))


def over_sequences(kernel, place, chunk, count, ins, outs, held=(), weights=(), pieces=(), flops=0):
    def spec(shape, kind):
        if kind == "scalars":
            return pl.BlockSpec(memory_space=pltpu.SMEM)
        if kind == "whole":
            return pl.BlockSpec(shape, lambda i: (0,) * len(shape), pipeline_mode=pl.Buffered(1))
        if kind == "pair":
            return pl.BlockSpec((1,) + shape[1:], lambda i: (i // 2,) + (0,) * (len(shape) - 1))
        offset = 0 if kind == "part" else chunk * count
        if isinstance(kind, tuple):
            _, width, at = kind
            return pl.BlockSpec((1, shape[1], width), lambda i: (offset + i, 0, at))
        return pl.BlockSpec((1,) + shape[1:], lambda i: (offset + i,) + (0,) * (len(shape) - 1))

    anywhere = pl.BlockSpec(memory_space=pl.ANY)
    arrays, specs = [place], [pl.BlockSpec(memory_space=pltpu.SMEM)]
    for w in weights:
        arrays += w.blocks
        specs += [anywhere] * len(w.blocks)
    for piece in pieces:
        arrays.append(piece)
        specs.append(spec(piece.shape, "whole"))
    arrays += [a for a, _ in ins]
    specs += [spec(a.shape, kind) for a, kind in ins]
    aliases = {}
    for i, array in enumerate(held):
        if array is not None:
            aliases[len(arrays)] = i
            arrays.append(array)
            specs.append(anywhere)

    def body(*refs):
        refs = list(refs)
        place_ref = refs.pop(0)
        block_refs = [[refs.pop(0) for _ in w.blocks] for w in weights]
        piece_refs = [refs.pop(0) for _ in pieces]
        in_refs = [refs.pop(0) for _ in ins]
        del refs[: len(aliases)]
        out_refs = [refs.pop(0) for _ in outs]
        into, sems = refs[: len(weights)], refs[len(weights) :]
        step = pl.program_id(0)

        @pl.when(step == 0)
        def _():
            for w, blocks, ref, sem in zip(weights, block_refs, into, sems):
                w.load(blocks, place_ref, ref, sem)

        def fetch():
            @pl.when(step == 0)
            def _():
                for w, blocks, ref, sem in zip(weights, block_refs, into, sems):
                    for copy in w.copies_of(blocks, place_ref, ref, sem):
                        copy.wait()

            return into

        kernel(step, fetch, piece_refs, *in_refs, *out_refs)

    size = sum(a.size * a.dtype.itemsize for a in arrays)
    return pl.pallas_call(
        body,
        grid=(count,),
        in_specs=specs,
        out_specs=[spec(shape, kind) for shape, _, kind in outs],
        out_shape=[jax.ShapeDtypeStruct(shape, kind) for shape, kind, _ in outs],
        scratch_shapes=[pltpu.VMEM((w.height, w.n), BF16) for w in weights]
        + [pltpu.SemaphoreType.DMA((w.copies,)) for w in weights],
        input_output_aliases=aliases,
        compiler_params=pltpu.CompilerParams(vmem_limit_bytes=VMEM_LIMIT),
        cost_estimate=pl.CostEstimate(flops=flops, bytes_accessed=size // 4, transcendentals=0),
    )(*arrays)


def after(value, *others):
    return lax.optimization_barrier((value,) + others)[0] if others else value


def build(ny, nz):
    def local(block_in, doc_starts, out_grad, w_mix, w_out, w_gu, w_down, attn_gain, ffn_gain, group_gain, lower_logit):
        at = Places(ny, nz)
        micro, length, features = block_in.shape
        rows = w_mix.shape[0]
        own_channels = ny * nz * rows
        heads = own_channels // HEAD
        strip = own_channels // ny
        ff_rows = w_down.shape[0]
        own_ff = ny * nz * ff_rows
        ff_strip = nz * ff_rows
        total = micro * TEAM
        tokens = total * length
        place = jnp.stack([at.rank, at.y, at.z]).astype(jnp.int32)
        team = ("y", "seq")

        def trade(parts, *held):
            return jnp.stack([parts[0]] + [at.swap(after(parts[j], *held), j) for j in range(1, TEAM)])

        def columns_of(matrix, count, width):
            parts = matrix.reshape(rows, count * ny, TEAM, width)
            return [lax.dynamic_index_in_dim(parts, at.rank ^ j, 2, False).reshape(rows, -1) for j in range(TEAM)]

        group_share = jnp.pad(group_gain, (0, rows - group_gain.shape[0]))
        extra = jnp.stack([attn_gain, ffn_gain, lower_logit, group_share], axis=1).astype(BF16)
        extra = jnp.pad(extra, ((0, 0), (0, HEAD - extra.shape[1])))
        mix_width = 4 * own_channels + HEAD
        mix_parts = pl.pallas_call(
            partial(pick_kernel, strip),
            in_specs=[pl.BlockSpec(memory_space=pltpu.SMEM)] + [pl.BlockSpec(memory_space=pltpu.VMEM)] * 2,
            out_specs=[pl.BlockSpec(memory_space=pltpu.VMEM)] * TEAM,
            out_shape=[jax.ShapeDtypeStruct((rows, mix_width), BF16)] * TEAM,
        )(place, w_mix, extra)
        mix_own, out_own = trade(mix_parts), w_out[None]
        starts = doc_starts.astype(BF16)[:, None]
        starts = jnp.concatenate([starts, at.swap(starts, 1)], axis=1)
        starts = jnp.concatenate([starts, at.swap(starts, 2)], axis=1)
        waits = {}
        if (ny, nz) == (2, 4) and micro == 2:
            z1, z2 = (lambda v: at.swap_z(v, 1)), (lambda v: at.swap_z(v, 2))
            cross = lambda v: at.swap_y(v, 1)
            far = lambda v: at.swap(v, 2)
            m1, m2, my = z1(mix_own), z2(mix_own), cross(mix_own)
            oy = cross(after(out_own, mix_own))
            in0 = far(after(block_in[0], mix_own))
            gu_own = trade(columns_of(after(w_gu, mix_own), 2, ff_strip), mix_own)
            done = (m1, m2, my, oy, in0)
            m12, my1, my2 = z1(after(m2, *done)), cross(after(m1, *done)), cross(after(m2, *done))
            o1, o2 = z1(after(out_own, *done)), z2(after(out_own, *done))
            in1 = far(after(block_in[1], *done, gu_own))
            done = (m12, my1, my2, in1, o1, o2)
            my12 = cross(after(m12, *done))
            o12, oy1, oy2 = z1(after(o2, *done)), cross(after(o1, *done)), cross(after(o2, *done))
            g1, g2 = z1(after(gu_own, *done)), z2(after(gu_own, *done))
            gy = cross(after(gu_own, my12))
            cot0 = far(after(out_grad[0], *done))
            oy12 = cross(o12)
            gy1, gy2 = cross(g1), cross(g2)
            cot1 = far(after(out_grad[1], cot0))
            g12 = z1(g2)
            waits["mix", 0] = (o12, g1)
            waits["mix", 1] = (g2, gy, oy1, oy2, oy12)
            waits["hop", 0] = (g12,)
            waits["hop", 1] = (gy1, cot1)
            waits["out", 0] = (gy2,)

            def later(*held):
                found_gu = found(gu_own, g1, g2, g12, gy, gy1, gy2, cross(g12))
                return Weight(at, found_gu), Weight(at, lax.all_gather(after(w_down, *held), team)[:, None])

            def found(own, a1, a2, a12, y, y1, y2, y12):
                near = {(0, 0): own, (0, 1): a1, (0, 2): a2, (0, 3): a12}
                return {**near, (1, 0): y, (1, 1): y1, (1, 2): y2, (1, 3): y12}

            mix = Weight(at, found(mix_own, m1, m2, m12, my, my1, my2, my12))
            out = Weight(at, found(out_own, o1, o2, o12, oy, oy1, oy2, oy12))
            inputs, cotangent = (
                [[own, at.swap(own, 1), far_own, at.swap(far_own, 1)] for own, far_own in zip(here, there)]
                for here, there in ((block_in, (in0, in1)), (out_grad, (cot0, cot1)))
            )
        else:
            gu_own = trade(columns_of(w_gu, 2, ff_strip))
            mix, out = (Weight(at, at.gather_blocks(v)) for v in (mix_own, out_own))

            def later(*held):
                return Weight(at, at.gather_blocks(gu_own)), Weight(at, lax.all_gather(w_down, team)[:, None])

            inputs = [at.team_gather(block_in[c]) for c in range(micro)]
            cotangent = [at.team_gather(out_grad[c]) for c in range(micro)]

        def turn(name, c, *others):
            return after(place, *waits.get((name, c), ()), *others)

        upto = (jnp.arange(length)[:, None] <= jnp.arange(length)[None, :]).astype(BF16)
        counts = jnp.dot(starts.reshape(total, length), upto, preferred_element_type=F32)
        count_row = counts.reshape(total, 1, length)
        count_col = counts.reshape(total, length, 1)

        def pass_on(leaving, fade, sign, *held):
            factor = fade.reshape(TEAM, heads, HEAD)[..., None]
            entering = jnp.zeros(leaving.shape, F32)
            hops = []
            for k in range(nz - 1):
                pair = (k, k + 1) if sign == 1 else (nz - 1 - k, nz - 2 - k)
                moved = (factor * entering + leaving).astype(BF16)
                moved = lax.ppermute(after(moved, *held) if k == 1 else moved, "seq", [pair])
                hops.append(moved)
                entering = entering + moved.astype(F32)
            return entering.astype(BF16), hops

        span, part, pair = (total, length), (TEAM, length), (TEAM // 2, length, features)
        states = (TEAM, heads, HEAD, HEAD)
        wide = 4 * own_channels
        per_matmul = 2 * TEAM * length * features

        normed = proj = running = qd = kg = mixed = gated = None
        normed2 = hidden = first = second = None
        entering, residual, fades, team_normed2 = [], [], [], []
        insides, leavings = [], []
        for c in range(micro):
            rows_c, cols_c = (a[c * TEAM : (c + 1) * TEAM] for a in (count_row, count_col))
            normed, proj, running, qd, kg, inside, leaving, fade, scales, bound = over_sequences(
                partial(mix_kernel, strip), turn("mix", c), c, TEAM,
                [(place, "scalars"), (rows_c, "part"), (cols_c, "part")],
                [
                    (span + (features,), BF16, "all"),
                    (span + (wide,), F32, "all"),
                    (span + (own_channels,), F32, "all"),
                    (span + (own_channels,), BF16, "all"),
                    (span + (own_channels,), BF16, "all"),
                    (part + (own_channels,), F32, "part"),
                    (states, F32, "part"),
                    ((TEAM, 1, own_channels), F32, "part"),
                    ((8, features), F32, "whole"),
                    ((1, own_channels), F32, "whole"),
                ],
                [normed, proj, running, qd, kg], [mix], inputs[c], per_matmul * wide,
            )
            if c == 0:
                attn_scale, ffn_scale = scales[0:1], scales[1:2]
                group_scale = scales[3].reshape(-1, rows)[:, : group_gain.shape[0]].reshape(1, HEAD)
            fades.append(fade)
            insides.append(inside)
            leavings.append(leaving)
            entering.append(pass_on(leaving, fade, 1, *waits.get(("hop", c), ()))[0])
        gu, down = later(*entering)
        for c in range(micro):
            cols_c = count_col[c * TEAM : (c + 1) * TEAM]
            mixed, gated, even, odd = over_sequences(
                out_kernel, turn("out", c, *leavings), c, TEAM,
                [
                    (insides[c], "part"), (qd, "all"), (proj, ("all", own_channels, 3)), (entering[c], "part"), (cols_c, "part"),
                    (group_scale, "whole"),
                ],
                [
                    (span + (own_channels,), F32, "all"), (span + (own_channels,), BF16, "all"),
                    (pair, BF16, "pair"), (pair, BF16, "pair"),
                ],
                [mixed, gated], [out], (), per_matmul * own_channels,
            )
            residual.append(block_in[c].astype(F32) + at.team_sum(even[None], odd[None], ())[0][0])
            rms_two = lax.rsqrt(jnp.mean(residual[c] * residual[c], axis=-1, keepdims=True) + EPSILON)
            team_normed2.append(at.team_gather((residual[c] * rms_two * ffn_scale).astype(BF16)))

        def flat(a):
            return a.reshape(tokens, a.shape[-1])

        def team_share(left, right, s):
            product = tn(left, right).astype(BF16).reshape(ny, s, nz, -1, right.shape[1])
            product = jnp.swapaxes(product, 1, 2).reshape(ny * nz, -1, right.shape[1])
            return lax.psum_scatter(product, team, scatter_dimension=0, tiled=False).reshape(s, -1, right.shape[1]), product

        def weight_half(left, right, k):
            size = left.shape[1] // ny
            if ny == 2:
                y = 1 - at.y if k == 0 else at.y
                return tn(lax.dynamic_slice_in_dim(left, y * size, size, 1), right).astype(BF16)
            return tn(left, right).astype(BF16).reshape(ny, size, right.shape[1])

        def weight_halves(left, right):
            return [weight_half(left, right, k) for k in range(2 if ny == 2 else 1)]

        def weight_sum(parts, s, held=(), first_held=()):
            width = parts[0].shape[-1]
            if ny == 2:
                send, keep = parts
                terms = [keep, after(at.swap_y(after(send, *first_held), 1), *held)]
            else:
                terms = parts
                for step in [1 << i for i in reversed(range(ny.bit_length() - 1))]:
                    halves = [t.reshape((t.shape[0] // 2 // step, 2, step) + t.shape[1:])[0] for t in terms]
                    bit = (at.y // step) % 2
                    pick = lambda k: [lax.dynamic_index_in_dim(t, k, 0, False) for t in halves]
                    send = sum(t.astype(F32) for t in pick(1 - bit)).astype(BF16)
                    terms = pick(bit) + [at.swap_y(send, step)]
                terms = [t[0] for t in terms]
            terms = [t.reshape(s, nz, -1, width) for t in terms]
            count = nz
            for i in range(nz.bit_length() - 1):
                count //= 2
                halves = [t.reshape((s, count, 2) + t.shape[2:]) for t in terms]
                bit = (at.z // (1 << i)) % 2
                pick = lambda k: [lax.dynamic_index_in_dim(t, k, 2, False) for t in halves]
                send = sum(t.astype(F32) for t in pick(1 - bit)).astype(BF16)
                terms = pick(bit) + [at.swap_z(send, 1 << i)]
            return (lambda i: sum(lax.dynamic_index_in_dim(t[:, 0], i, 0, False).astype(F32) for t in terms)), send

        def out_of_team(summed, count, *held):
            got = at.by_rank(trade([summed(at.rank ^ j).astype(BF16) for j in range(TEAM)], *held)).astype(F32)
            width = got.shape[2] // (count * ny)
            got = got.reshape(TEAM, rows, count, ny, width)
            return jnp.transpose(got, (1, 2, 3, 0, 4)).reshape(rows, -1)

        both = whole_branch = None
        all_cot = jnp.concatenate([jnp.stack(pieces) for pieces in cotangent])
        for c in range(micro):
            normed2, hidden, first, second = over_sequences(
                up_kernel, turn("up", c), c, TEAM,
                [],
                [(span + (features,), BF16, "all")] + [(span + (own_ff,), BF16, "all")] * 3,
                [normed2, hidden, first, second], [gu], team_normed2[c], per_matmul * 2 * own_ff,
            )
        d_residual, d_branch, branch_own, gain_sums, sents = [], [], [], [], []
        held, branch_sum = (), ()
        for c in range(micro):
            both, even, odd = over_sequences(
                down_back_kernel, turn("down_back", c, *held), c, TEAM,
                [(all_cot, "all"), (first, "all"), (second, "all")],
                [(span + (2 * own_ff,), BF16, "all"), (pair, BF16, "pair"), (pair, BF16, "pair")],
                [both], [down, gu], (), per_matmul * 3 * own_ff,
            )
            if c == 0:
                grad_down, down_product = team_share(after(flat(hidden), even), flat(all_cot), 1)
                grad_down = grad_down[0].astype(F32)
            d_normed2, sent = at.team_sum(even[None], odd[None], branch_sum, *((down_product,) if c == 0 else branch_own))
            held = (down_product, sent)
            d_normed2 = d_normed2[0]
            branch_sum = (d_normed2,)
            sents.append(sent)
            res = residual[c]
            rms_two = lax.rsqrt(jnp.mean(res * res, axis=-1, keepdims=True) + EPSILON)
            gain_sums.append(jnp.sum(d_normed2 * res * rms_two, axis=0))
            scaled = d_normed2 * ffn_scale
            d_residual.append(
                out_grad[c].astype(F32)
                + rms_two * (scaled - res * rms_two * rms_two * jnp.mean(scaled * res, axis=-1, keepdims=True))
            )
            branch_own.append(d_residual[c].astype(BF16))
            d_branch.append(at.team_gather(branch_own[c]))

        d_q = d_fv = d_o = None
        gs, group_sums, logit_sums, adjoints = [], [], [], []

        def enter_back(c, whole_branch, d_o, *held):
            cols_c = count_col[c * TEAM : (c + 1) * TEAM]
            whole_branch, d_o, g, toward, group_sum = over_sequences(
                out_back_kernel, turn("out_back", c, *held), c, TEAM,
                [
                    (mixed, "all"), (proj, ("all", own_channels, 3)), (qd, "all"), (cols_c, "part"), (group_scale, "whole"),
                ],
                [
                    (span + (features,), BF16, "all"), (span + (own_channels,), BF16, "all"),
                    (part + (own_channels,), BF16, "part"), (states, F32, "part"), ((TEAM, 1, own_channels), F32, "part"),
                ],
                [whole_branch, d_o], [out], d_branch[c], per_matmul * own_channels,
            )
            gs.append(g)
            group_sums.append(group_sum)
            adjoint, hops = pass_on(toward, fades[c], -1)
            adjoints.append(adjoint)
            return whole_branch, d_o, toward, hops

        toward = place
        gu_send = weight_half(after(flat(normed2), branch_own[0]), flat(both), 0)
        hops = []
        for c in range(micro - 1):
            whole_branch, d_o, toward, hops = enter_back(c, whole_branch, d_o, gu_send, sents[c + 1])
        gu_halves = [gu_send] + ([weight_half(after(flat(normed2), toward), flat(both), 1)] if ny == 2 else [])
        even, odd = over_sequences(
            share_kernel, after(place, gu_halves[-1], branch_own[-1], *hops[:1]), 0, total, [(hidden, "part")],
            [((micro * TEAM // 2, length, features), BF16, "pair")] * 2, (), [down], (), 2 * tokens * own_ff * features,
        )
        whole_branch, d_o, toward, last_hops = enter_back(micro - 1, whole_branch, d_o, even, *hops[1:2])
        paired = (micro, TEAM // 2, length, features)
        ffn_near = after(at.swap(odd, 1), toward).reshape(paired)
        even = even.reshape(paired)
        ffn_sent = [(even[c, 1].astype(F32) + ffn_near[c, 1].astype(F32)).astype(BF16) for c in range(micro)]
        block_out = [
            (residual[c] + (even[c, 0].astype(F32) + ffn_near[c, 0].astype(F32) + at.swap(ffn_sent[c], 2).astype(F32))).astype(BF16)
            for c in range(micro)
        ]
        out_halves = weight_halves(flat(gated), flat(whole_branch))
        mix_halves = {"o": weight_halves(after(flat(normed), *last_hops[:1]), flat(d_o))}
        gu_sum, gu_sent = weight_sum(gu_halves, TEAM, adjoints)

        d_normed, dn_sent = [], []
        for c in range(micro):
            rows_c, cols_c = (a[c * TEAM : (c + 1) * TEAM] for a in (count_row, count_col))
            held = (*ffn_sent, *last_hops[1:2], *out_halves, *mix_halves["o"]) if c == 0 else (gu_sent, block_out[0])
            d_q, d_fv, logit_sum, even, odd = over_sequences(
                mix_back_kernel, turn("mix_back", c, *held), c, TEAM,
                [
                    (proj, ("all", own_channels, 0)), (proj, ("all", own_channels, 1)), (proj, ("all", own_channels, 2)),
                    (running, "all"), (qd, "all"), (kg, "all"), (gs[c], "part"), (entering[c], "part"), (adjoints[c], "part"),
                    (bound, "whole"), (rows_c, "part"), (cols_c, "part"), (d_o, "all"),
                ],
                [
                    (span + (own_channels,), BF16, "all"), (span + (2 * own_channels,), BF16, "all"),
                    ((TEAM, 1, own_channels), F32, "part"), (pair, BF16, "pair"), (pair, BF16, "pair"),
                ],
                [d_q, d_fv], [mix], (), per_matmul * wide,
            )
            logit_sums.append(logit_sum)
            summed, sent = at.team_sum(even[None], odd[None], ())
            d_normed.append(summed[0])
            dn_sent.append(sent)
        last, d_q = d_fv, after(d_q, d_fv)
        fv_sum, fv_product = team_share(flat(normed), flat(d_fv), TEAM)
        mix_halves["q"] = [weight_half(after(flat(normed), fv_product), flat(d_q), 0)]
        if ny == 2:
            q_left = after(flat(normed), *dn_sent, *mix_halves["q"])
            mix_halves["q"].append(weight_half(q_left, flat(d_q), 1))
        d_normed, block_out = jnp.stack(d_normed), jnp.stack(block_out)
        x = block_in.astype(F32)
        rms_one = lax.rsqrt(jnp.mean(x * x, axis=-1, keepdims=True) + EPSILON)
        attn_sum = jnp.sum(d_normed * x * rms_one, axis=(0, 1))
        scaled = d_normed * attn_scale
        in_grad = jnp.stack(d_residual) + rms_one * (
            scaled - x * rms_one * rms_one * jnp.mean(scaled * x, axis=-1, keepdims=True)
        )

        logit_sum = bound[0] * (1.0 - bound[0]) * sum(jnp.sum(a, axis=(0, 1)) for a in logit_sums)
        logit_all = jnp.where(
            jnp.arange(TEAM)[None, :, None] == at.rank, logit_sum.reshape(ny, 1, strip), 0.0
        ).reshape(features)
        group_all = jnp.sum(sum(jnp.sum(a, axis=(0, 1)) for a in group_sums).reshape(heads, HEAD), axis=0)
        sums = at.everyone_sum(jnp.concatenate([attn_sum, sum(gain_sums), logit_all, group_all]))

        grad_gu = out_of_team(gu_sum, 2)
        grad_out = weight_sum(out_halves, 1, (last,), adjoints)[0](0)
        grads = [
            out_of_team(weight_sum(mix_halves[name], TEAM, (last, fv_product), adjoints)[0], 1) for name in ("q", "o")
        ]
        grad_fv = out_of_team(
            lambda i: lax.dynamic_index_in_dim(fv_sum, i, 0, False), 2, sums, grad_gu, grad_out, *grads
        )
        grad_mix = jnp.concatenate([grads[0], grad_fv, grads[1]], axis=1)
        here = (at.y * TEAM + at.rank) * nz + at.z

        def mine(start, size):
            return lax.dynamic_slice_in_dim(sums, start + here * size, size)

        return (
            block_out,
            in_grad,
            grad_mix,
            grad_out,
            grad_gu,
            grad_down,
            mine(0, rows),
            mine(features, rows),
            mine(3 * features, group_gain.shape[0]),
            mine(2 * features, rows),
        )

    return local


def solution(mesh):
    devices = mesh.devices.reshape(-1, TEAM, mesh.shape["seq"])
    tokens = P(("y", "team"), "seq", None)
    matrix = P(("y", "team", "seq"), None)
    vector = P(("y", "team", "seq"))
    return jax.shard_map(
        build(devices.shape[0], devices.shape[2]),
        mesh=Mesh(devices, ("y", "team", "seq")),
        in_specs=(tokens, P(("y", "team"), "seq"), tokens) + (matrix,) * 4 + (vector,) * 4,
        out_specs=(tokens, tokens) + (matrix,) * 4 + (vector,) * 4,
        check_vma=False,
    )
```

time: 1560 us -> 1140 us (0.73)
  starting transfers between devices: 321 us -> 84.3 us
  waiting for transfers between devices: 519 us -> 380 us
  Pallas kernels: 207 us -> 305 us
  local copies, waits for them, and re-layouts: 161 us -> 107 us
  blocking collectives: 42.5 us -> 0 us
  matrix products: 136 us -> 97.9 us
  other arithmetic: 164 us -> 143 us
    ppermute x144 -> x109, starting transfers between devices: 321 us -> 84.2 us  [the longest x61 36.1 us: swap(): return lax.ppermute(value, 'team', [(i, i ^ bits) for i in range(TEAM)])]
    ppermute x144 -> x109, waiting for transfers between devices: 519 us -> 380 us  [the longest x61 157 us: swap(): return lax.ppermute(value, 'team', [(i, i ^ bits) for i in range(TEAM)])]
    pallas_call x12 -> x14, Pallas kernels: 207 us -> 305 us  [the longest x13 303 us: over_sequences(): pl.pallas_call(body, grid=(count,), in_specs=specs, out_specs=[spec(shape...]
    psum x1 -> x0, blocking collectives: 42.5 us -> none  [local(): lax.psum(jnp.concatenate([attn_sum, sum(gain_sums), logit_all, group_all]...]
    dot_general x2 -> x0, matrix products: 38.5 us -> none  [the longest x1 22.5 us: nt(): lax.dot_general(a, b, (((1,), (1,)), ((), ())), preferred_element_type=F32)]
    convert_element_type x36 -> x51, other arithmetic: 58.6 us -> 88.9 us  [the longest x8 18.2 us: weight_sum(): send = sum((t.astype(F32) for t in pick(1 - bit))).astype(BF16)]
    dynamic_update_slice x18 -> x0, other arithmetic: 29.9 us -> none  [gather_rows(): lax.dynamic_update_slice(whole, there[None, :, None], (y, 0, z, 0, 0))]
    slice x19 -> x1, local copies, waits for them, and re-layouts: 28.7 us -> 1.57 us  [local(): attn_scale, ffn_scale = (scales[0:1], scales[1:2])]
  transfers between devices with their start and end apart: 144 -> 112, of which waited for: 43 -> 39; matrix products, arithmetic and copies ran while one was open for 27% -> 29% of each run, Pallas kernels for 12% -> 24%
where the time goes in v2:
time: 1140 us; the launch traced here: 1130 us
  waiting for transfers between devices  380 us (33%)
  Pallas kernels  305 us (27%)
  other arithmetic  143 us (13%)
  local copies, waits for them, and re-layouts  107 us (9%)
  matrix products  97.9 us (9%)
  starting transfers between devices  84.3 us (7%)
  between operations  15.8 us (1%)
    pallas_call x13, Pallas kernels, over_sequences(): pl.pallas_call(body, grid=(count,), in_specs=specs, out_specs=[spec(shape...  303 us
    ppermute x61, waiting for transfers between devices, swap(): return lax.ppermute(value, 'team', [(i, i ^ bits) for i in range(TEAM)])  157 us
    ppermute x19, waiting for transfers between devices, swap_z(): return lax.ppermute(value, 'seq', [(i, i ^ bits) for i in range(self.nz)])  131 us
    dot_general x10, matrix products, tn(): lax.dot_general(a, b, (((0,), (0,)), ((), ())), preferred_element_type=F32)  97.7 us
    ppermute x17, waiting for transfers between devices, swap_y(): return lax.ppermute(value, 'y', [(i, i ^ bits) for i in range(self.ny)])  49.1 us
    ppermute x12, waiting for transfers between devices, pass_on(): lax.ppermute(after(moved, *held) if k == 1 else moved, 'seq', [pair])  42.8 us
    ppermute x61, starting transfers between devices, swap(): return lax.ppermute(value, 'team', [(i, i ^ bits) for i in range(TEAM)])  36.1 us
  transfers between devices with their start and end apart: 112, of which 39 were waited for; matrix products, arithmetic and copies ran while one was open for 29% of the time, Pallas kernels for 24%

profile of v2, /device:TPU:0, one launch (start us, length us, event | category | flops | bytes accessed | tf_op | source)
XLA Modules:
  0.0 1132.6 jit_solution(3525652307990848301)
XLA Ops:
  15.5 7.6 collective-permute-done.1
  23.1 5.6 collective-permute-done.2
  39.2 4.9 reshape.1788
  44.1 14.4 %dynamic-slice_reduce_fusion.3 = (bf16[64,4,704]{2,1,0:T(4,128)(2,1)}, bf16[64,4,704]{2,1,0:T(4,128)(2,1)}, bf16[64,4,704]{2,1,0:T(4,128)(2,1)}, bf16[64,4,704]{2,1,0:T(4,128)(2,1)}) fusion(bf16[64,4,4,704]{3,2,1,0:T(4,128)(2,1)} %reshape.1788, s32[]{:T(128)S(6)} %select_n.307, s32[]{:T(128)S(6)} %select_n.309, s32[]{:T(128)S(6)} %select_n.308, ...), kind=kLoop, calls=%fused_computation.147 | loop fusion | bytes 2883600 | tf_op jit(solution)/shard_map/jit(dynamic_index_in_dim)/dynamic_slice | solution.py:462
  69.0 15.5 %collective-permute-done.7.refs_2_ = bf16[4,64,2176]{2,1,0:T(8,128)(2,1)} collective-permute-done((bf16[4,64,2176]{2,1,0:T(8,128)(2,1)S(1)}, bf16[4,64,2176]{2,1,0:T(8,128)(2,1)}, u32[]{:S(2)}, u32[]{:S(2)}) %collective-permute-start.7) | collective-permute-done | bytes 1114144 | tf_op jit(solution)/shard_map/ppermute | solution.py:31
  93.6 6.3 collective-permute-done.16.refs_3_
  104.0 11.6 %collective-permute-done.14.refs_11_ = bf16[256,2048]{1,0:T(8,128)(2,1)S(1)} collective-permute-done((bf16[256,2048]{1,0:T(8,128)(2,1)}, bf16[256,2048]{1,0:T(8,128)(2,1)S(1)}, u32[]{:S(2)}, u32[]{:S(2)}) %collective-permute-start.14) | collective-permute-done | bytes 1048608 | tf_op jit(solution)/shard_map/ppermute | solution.py:25
  120.3 5.7 collective-permute-done.11.refs_4_
  125.9 14.8 %collective-permute-done.12.refs_6_ = bf16[4,64,2176]{2,1,0:T(8,128)(2,1)} collective-permute-done((bf16[4,64,2176]{2,1,0:T(8,128)(2,1)}, bf16[4,64,2176]{2,1,0:T(8,128)(2,1)}, u32[]{:S(2)}, u32[]{:S(2)}) %collective-permute-start.12) | collective-permute-done | bytes 1114144 | tf_op jit(solution)/shard_map/ppermute | solution.py:28
  148.0 14.8 %collective-permute-done.41 = bf16[256,2048]{1,0:T(8,128)(2,1)} collective-permute-done((bf16[256,2048]{1,0:T(8,128)(2,1)}, bf16[256,2048]{1,0:T(8,128)(2,1)}, u32[]{:S(2)}, u32[]{:S(2)}) %collective-permute-start.41) | collective-permute-done | bytes 1048608 | tf_op jit(solution)/shard_map/ppermute | solution.py:25
  169.1 8.8 collective-permute-done.19.refs_4_
  181.6 23.8 %shard_map.187 = (bf16[8,256,2048]{2,1,0:T(8,128)(2,1)}, f32[8,256,2048]{2,1,0:T(8,128)}, f32[8,256,512]{2,1,0:T(8,128)}, bf16[8,256,512]{2,1,0:T(8,128)(2,1)}, ...) custom-call(s32[3]{0:T(128)} %pad_add_fusion.place_ref.refs_0_.refs_, ...), custom_call_target="tpu_custom_call" | custom-call | flops 8589934592 | bytes 3278854 | tf_op jit(solution)/shard_map/pallas_call | solution.py:423
  211.5 9.3 collective-permute-done.27.refs_6_
  223.1 5.1 collective-permute-done.29.refs_8_
  230.8 7.7 collective-permute-done.17.refs_3_.refs_4_
  242.1 24.3 %shard_map.188 = (bf16[8,256,2048]{2,1,0:T(8,128)(2,1)}, f32[8,256,2048]{2,1,0:T(8,128)}, f32[8,256,512]{2,1,0:T(8,128)}, bf16[8,256,512]{2,1,0:T(8,128)(2,1)}, ...) custom-call(s32[3]{0:T(128)} %pad_add_fusion.place_ref.refs_0_.refs_, ...), custom_call_target="tpu_custom_call", output_to_operand_aliasing={{0}: (16, {}), {1}: (17, {}), {2}: (18, {}), {3}: (19, {}),... | custom-call | flops 8589934592 | bytes 11667462 | tf_op jit(solution)/shard_map/pallas_call | solution.py:423
  273.9 9.5 collective-permute-done.40
  291.7 10.9 collective-permute-done.18.refs_7_.refs_8_
  307.7 12.2 %shard_map.189 = (f32[8,256,512]{2,1,0:T(8,128)}, bf16[8,256,512]{2,1,0:T(8,128)(2,1)}, bf16[2,256,2048]{2,1,0:T(8,128)(2,1)}, bf16[2,256,2048]{2,1,0:T(8,128)(2,1)}) custom-call(s32[3]{0:T(128)} %pad_add_fusion.place_ref.refs_0_.refs_13_, bf16[1,64,2048]{2,1,0:T(8,128)(2,1)} %bitcast.456, bf16[1,64,2048]{2,1,0:T(8,128)(2,1)} %copy-done.35, ...), custom_call_target="tpu_custom_call" | custom-call | flops 2147483648 | bytes 5899395 | tf_op jit(solution)/shard_map/pallas_call | solution.py:423
  322.2 12.6 %shard_map.190 = (f32[8,256,512]{2,1,0:T(8,128)}, bf16[8,256,512]{2,1,0:T(8,128)(2,1)}, bf16[2,256,2048]{2,1,0:T(8,128)(2,1)}, bf16[2,256,2048]{2,1,0:T(8,128)(2,1)}) custom-call(s32[3]{0:T(128)} %pad_add_fusion.place_ref.refs_0_.refs_13_, bf16[1,64,2048]{2,1,0:T(8,128)(2,1)} %bitcast.457, ...), custom_call_target="tpu_custom_call", output_to_operand_aliasing={{0}: (15, {}), {1}: (16, {})} | custom-call | flops 2147483648 | bytes 7472259 | tf_op jit(solution)/shard_map/pallas_call | solution.py:423
  341.5 22.1 %collective-permute-done.37 = bf16[1,256,2048]{2,1,0:T(8,128)(2,1)S(1)} collective-permute-done((bf16[1,256,2048]{2,1,0:T(8,128)(2,1)S(1)}, bf16[1,256,2048]{2,1,0:T(8,128)(2,1)S(1)}, u32[]{:S(2)}, u32[]{:S(2)}) %collective-permute-start.37) | collective-permute-done | bytes 1048608 | tf_op jit(solution)/shard_map/ppermute | solution.py:25
  363.5 21.6 %collective-permute-done.46 = bf16[1,256,2048]{2,1,0:T(8,128)(2,1)S(1)} collective-permute-done((bf16[1,256,2048]{2,1,0:T(8,128)(2,1)S(1)}, bf16[1,256,2048]{2,1,0:T(8,128)(2,1)S(1)}, u32[]{:S(2)}, u32[]{:S(2)}) %collective-permute-start.46) | collective-permute-done | bytes 1048608 | tf_op jit(solution)/shard_map/ppermute | solution.py:25
  394.1 22.1 %collective-permute-done.51.refs_11_ = bf16[256,2048]{1,0:T(8,128)(2,1)S(1)} collective-permute-done((bf16[256,2048]{1,0:T(8,128)(2,1)S(1)}, bf16[256,2048]{1,0:T(8,128)(2,1)S(1)}, u32[]{:S(2)}, u32[]{:S(2)}) %collective-permute-start.51) | collective-permute-done | bytes 1048608 | tf_op jit(solution)/shard_map/ppermute | solution.py:25
  421.2 15.9 %collective-permute-done.48.refs_11_ = bf16[256,2048]{1,0:T(8,128)(2,1)} collective-permute-done((bf16[256,2048]{1,0:T(8,128)(2,1)S(1)}, bf16[256,2048]{1,0:T(8,128)(2,1)}, u32[]{:S(2)}, u32[]{:S(2)}) %collective-permute-start.48) | collective-permute-done | bytes 1048608 | tf_op jit(solution)/shard_map/ppermute | solution.py:25
  439.2 22.5 %shard_map.191 = (bf16[8,256,2048]{2,1,0:T(8,128)(2,1)}, bf16[8,256,1408]{2,1,0:T(8,128)(2,1)}, bf16[8,256,1408]{2,1,0:T(8,128)(2,1)}, bf16[8,256,1408]{2,1,0:T(8,128)(2,1)}) custom-call(s32[3]{0:T(128)} %pad_add_fusion.place_ref.refs_0_.refs_13_, bf16[4,64,2816]{2,1,0:T(8,128)(2,1)} %pad_maximum_fusion.3.refs_1_.refs_2_, ...), custom_call_target="tpu_custom_call" | custom-call | flops 11811160064 | bytes 3932163 | tf_op jit(solution)/shard_map/pallas_call | solution.py:423
  461.8 22.8 %shard_map.192 = (bf16[8,256,2048]{2,1,0:T(8,128)(2,1)}, bf16[8,256,1408]{2,1,0:T(8,128)(2,1)}, bf16[8,256,1408]{2,1,0:T(8,128)(2,1)}, bf16[8,256,1408]{2,1,0:T(8,128)(2,1)}) custom-call(s32[3]{0:T(128)} %pad_add_fusion.place_ref.refs_0_.refs_13_, ...), custom_call_target="tpu_custom_call", output_to_operand_aliasing={{0}: (13, {}), {1}: (14, {}), {2}: (15, {}), {3}: (16, {})} | custom-call | flops 11811160064 | bytes 10354691 | tf_op jit(solution)/shard_map/pallas_call | solution.py:423
  484.6 32.3 %shard_map.193 = (bf16[8,256,2816]{2,1,0:T(8,128)(2,1)}, bf16[2,256,2048]{2,1,0:T(8,128)(2,1)}, bf16[2,256,2048]{2,1,0:T(8,128)(2,1)}) custom-call(s32[3]{0:T(128)} %pad_add_fusion.place_ref.refs_0_.refs_13_, bf16[8,1,176,2048]{3,2,1,0:T(8,128)(2,1)} %bitcast.527, bf16[4,64,2816]{2,1,0:T(8,128)(2,1)} %pad_maximum_fusion.3.refs_1_.refs_2_, ...), custom_call_target="tpu_custom_call" | custom-call | flops 17716740096 | bytes 9306115 | tf_op jit(solution)/shard_map/pallas_call | solution.py:423
  517.5 18.2 %convolution_convert_fusion = bf16[1408,2048]{1,0:T(8,128)(2,1)} fusion(bf16[2048,1408]{1,0:T(8,128)(2,1)} %bitcast.540, bf16[2048,2048]{1,0:T(8,128)(2,1)} %bitcast.518), kind=kOutput, calls=%fused_computation.1 | convolution fusion | flops 11814043648 | bytes 19922944 | tf_op jit(solution)/shard_map/dot_general | solution.py:121
  543.5 20.4 %collective-permute-done.58 = bf16[1,256,2048]{2,1,0:T(8,128)(2,1)S(1)} collective-permute-done((bf16[1,256,2048]{2,1,0:T(8,128)(2,1)}, bf16[1,256,2048]{2,1,0:T(8,128)(2,1)S(1)}, u32[]{:S(2)}, u32[]{:S(2)}) %collective-permute-start.58) | collective-permute-done | bytes 1048608 | tf_op jit(solution)/shard_map/ppermute | solution.py:25
  570.7 33.1 %shard_map.194 = (bf16[8,256,2816]{2,1,0:T(8,128)(2,1)}, bf16[2,256,2048]{2,1,0:T(8,128)(2,1)}, bf16[2,256,2048]{2,1,0:T(8,128)(2,1)}) custom-call(s32[3]{0:T(128)} %pad_add_fusion.place_ref.refs_0_.refs_13_, bf16[8,1,176,2048]{3,2,1,0:T(8,128)(2,1)} %bitcast.528, ...), custom_call_target="tpu_custom_call", output_to_operand_aliasing={{0}: (13, {})} | custom-call | flops 17716740096 | bytes 12189699 | tf_op jit(solution)/shard_map/pallas_call | solution.py:423
  604.5 19.4 %convolution_convert_fusion.2 = bf16[1024,2816]{1,0:T(8,128)(2,1)} fusion(bf16[2048,2816]{1,0:T(8,128)(2,1)} %bitcast.536, bf16[2048,2048]{1,0:T(8,128)(2,1)} %bitcast.538, s32[]{:T(128)S(6)} %select_n.311), kind=kOutput, calls=%fused_computation.8 | convolution fusion | flops 11814043648 | bytes 21495812 | tf_op jit(solution)/shard_map/dot_general | solution.py:121
  627.9 23.3 %shard_map.195 = (bf16[8,256,2048]{2,1,0:T(8,128)(2,1)}, bf16[8,256,512]{2,1,0:T(8,128)(2,1)}, bf16[4,256,512]{2,1,0:T(8,128)(2,1)}, f32[4,4,128,128]{3,2,1,0:T(8,128)}, f32[4,1,512]{2,1,0:T(1,128)}) custom-call(s32[3]{0:T(128)} %pad_add_fusion.place_ref.refs_0_.refs_13_, bf16[1,64,2048]{2,1,0:T(8,128)(2,1)} %bitcast.458, bf16[1,64,2048]{2,1,0:T(8,128)(2,1)} %copy-done.35, ...), custom_call_target="tpu_custom_call" | custom-call | flops 2147483648 | bytes 7341187 | tf_op jit(solution)/shard_map/pallas_call | solution.py:423
  666.6 18.9 %convolution_convert_fusion.1 = bf16[1024,2816]{1,0:T(8,128)(2,1)} fusion(bf16[2048,2816]{1,0:T(8,128)(2,1)} %bitcast.537, bf16[2048,2048]{1,0:T(8,128)(2,1)} %bitcast.539, s32[]{:T(128)S(6)} %select_n.312), kind=kOutput, calls=%fused_computation.7 | convolution fusion | flops 11814043648 | bytes 21495812 | tf_op jit(solution)/shard_map/dot_general | solution.py:121
  690.5 24.7 %shard_map.196 = (bf16[4,256,2048]{2,1,0:T(8,128)(2,1)}, bf16[4,256,2048]{2,1,0:T(8,128)(2,1)}) custom-call(s32[3]{0:T(128)} %pad_add_fusion.place_ref.refs_0_.refs_13_, bf16[8,1,176,2048]{3,2,1,0:T(8,128)(2,1)} %bitcast.529, bf16[8,256,1408]{2,1,0:T(8,128)(2,1)} %get-tuple-element.184.refs_2_), custom_call_target="tpu_custom_call" | custom-call | flops 11811160064 | bytes 2883587 | tf_op jit(solution)/shard_map/pallas_call | solution.py:423
  718.1 11.6 %shard_map.197 = (bf16[8,256,2048]{2,1,0:T(8,128)(2,1)}, bf16[8,256,512]{2,1,0:T(8,128)(2,1)}, bf16[4,256,512]{2,1,0:T(8,128)(2,1)}, f32[4,4,128,128]{3,2,1,0:T(8,128)}, f32[4,1,512]{2,1,0:T(1,128)}) custom-call(s32[3]{0:T(128)} %pad_add_fusion.place_ref.refs_0_.refs_13_, ...), custom_call_target="tpu_custom_call", output_to_operand_aliasing={{0}: (18, {}), {1}: (19, {})} | custom-call | flops 2147483648 | bytes 9962627 | tf_op jit(solution)/shard_map/pallas_call | solution.py:423
  732.6 7.3 convolution_convert_fusion.3
  753.6 33.3 %collective-permute-done.78 = bf16[4,4,128,128]{3,2,1,0:T(8,128)(2,1)S(1)} collective-permute-done((bf16[4,4,128,128]{3,2,1,0:T(8,128)(2,1)S(1)}, bf16[4,4,128,128]{3,2,1,0:T(8,128)(2,1)S(1)}, u32[]{:S(2)}, u32[]{:S(2)}) %collective-permute-start.78) | collective-permute-done | bytes 524320 | tf_op jit(solution)/shard_map/ppermute | solution.py:546
  797.9 29.5 %shard_map.198 = (bf16[8,256,512]{2,1,0:T(8,128)(2,1)}, bf16[8,256,1024]{2,1,0:T(8,128)(2,1)}, f32[4,1,512]{2,1,0:T(1,128)}, bf16[2,256,2048]{2,1,0:T(8,128)(2,1)}, bf16[2,256,2048]{2,1,0:T(8,128)(2,1)}) custom-call(s32[3]{0:T(128)} %pad_add_fusion.place_ref.refs_0_.refs_13_, bf16[4,64,2176]{2,1,0:T(8,128)(2,1)} %copy-done.12, ...), custom_call_target="tpu_custom_call" | custom-call | flops 8589934592 | bytes 17959428 | tf_op jit(solution)/shard_map/pallas_call | solution.py:423
  834.8 7.5 collective-permute-done.71
  842.3 5.5 fusion.24
  862.1 29.8 %shard_map.199 = (bf16[8,256,512]{2,1,0:T(8,128)(2,1)}, bf16[8,256,1024]{2,1,0:T(8,128)(2,1)}, f32[4,1,512]{2,1,0:T(1,128)}, bf16[2,256,2048]{2,1,0:T(8,128)(2,1)}, bf16[2,256,2048]{2,1,0:T(8,128)(2,1)}) custom-call(s32[3]{0:T(128)} %pad_add_fusion.place_ref.refs_0_.refs_13_, ...), custom_call_target="tpu_custom_call", output_to_operand_aliasing={{0}: (22, {}), {1}: (23, {})} | custom-call | flops 8589934592 | bytes 19532292 | tf_op jit(solution)/shard_map/pallas_call | solution.py:423
  896.3 13.1 %bitcast_convert_fusion = bf16[2048,1024]{1,0:T(8,128)(2,1)S(1)} fusion(bf16[8,256,2048]{2,1,0:T(8,128)(2,1)} %get-tuple-element.209, bf16[8,256,1024]{2,1,0:T(8,128)(2,1)} %get-tuple-element.226), kind=kOutput, calls=%fused_computation | convolution fusion | flops 8592031744 | bytes 16777216 | tf_op jit(solution)/shard_map/dot_general | solution.py:121
  914.3 6.2 fusion.33
  921.2 40.7 %collective-permute-done.98 = bf16[1,2,64,2048]{3,2,1,0:T(8,128)(2,1)} collective-permute-done((bf16[1,2,64,2048]{3,2,1,0:T(8,128)(2,1)}, bf16[1,2,64,2048]{3,2,1,0:T(8,128)(2,1)}, u32[]{:S(2)}, u32[]{:S(2)}) %collective-permute-start.98) | collective-permute-done | bytes 524320 | tf_op jit(solution)/shard_map/ppermute | solution.py:31
  963.8 23.3 %collective-permute-done.101 = bf16[4,2,64,512]{3,2,1,0:T(8,128)(2,1)S(1)} collective-permute-done((bf16[4,2,64,512]{3,2,1,0:T(8,128)(2,1)S(1)}, bf16[4,2,64,512]{3,2,1,0:T(8,128)(2,1)S(1)}, u32[]{:S(2)}, u32[]{:S(2)}) %collective-permute-start.101) | collective-permute-done | bytes 524320 | tf_op jit(solution)/shard_map/ppermute | solution.py:31
  993.1 9.9 collective-permute-done.102
  1073.2 5.4 reshape.1838
  1111.9 5.3 fusion.5
  (588 shorter events, 345.7 us)
Async XLA Ops:
  7.2 477.4 %all-gather.3.cloned.1.call-start = ((), (), s32[]{:S(2)}) async-start(), calls=%async_computation.4 | async-start | bytes 6488064 | tf_op jit(solution)/shard_map/all_gather | solution.py:509
  29.8 35.6 %collective-permute-start.8 = (bf16[4,64,2176]{2,1,0:T(8,128)(2,1)S(1)}, bf16[4,64,2176]{2,1,0:T(8,128)(2,1)}, u32[]{:S(2)}, u32[]{:S(2)}) collective-permute-start(bf16[4,64,2176]{2,1,0:T(8,128)(2,1)S(1)} %pad_maximum_fusion.4.refs_1_), channel_id=1, source_target_pairs={{0,16},{16,0},{1,17},{17,1},{2,18},{18,2},{3,19},{19,3},{4,20},{20... | collective-permute-start | bytes 3342344 | tf_op jit(solution)/shard_map/ppermute | solution.py:28
  33.0 31.7 %collective-permute-start.10 = (bf16[256,2048]{1,0:T(8,128)(2,1)}, bf16[256,2048]{1,0:T(8,128)(2,1)}, u32[]{:S(2)}, u32[]{:S(2)}) collective-permute-start(bf16[256,2048]{1,0:T(8,128)(2,1)} %get-tuple-element.136.refs_9_), channel_id=1, source_target_pairs={{0,8},{4,12},{8,0},{12,4},{1,9},{5,13},{9,1},{13,5},{2,10},{6,14},... | collective-permute-start | bytes 3145736 | tf_op jit(solution)/shard_map/ppermute | solution.py:25
  34.5 50.0 %collective-permute-start.7 = (bf16[4,64,2176]{2,1,0:T(8,128)(2,1)S(1)}, bf16[4,64,2176]{2,1,0:T(8,128)(2,1)}, u32[]{:S(2)}, u32[]{:S(2)}) collective-permute-start(bf16[4,64,2176]{2,1,0:T(8,128)(2,1)S(1)} %pad_maximum_fusion.4.refs_1_), channel_id=1, source_target_pairs={{0,1},{1,0},{2,3},{3,2},{4,5},{5,4},{6,7},{7,6},{8,9},{9,8},{10,11... | collective-permute-start | bytes 3342344 | tf_op jit(solution)/shard_map/ppermute | solution.py:31
  36.1 50.8 %collective-permute-start.6 = (bf16[4,64,2176]{2,1,0:T(8,128)(2,1)S(1)}, bf16[4,64,2176]{2,1,0:T(8,128)(2,1)}, u32[]{:S(2)}, u32[]{:S(2)}) collective-permute-start(bf16[4,64,2176]{2,1,0:T(8,128)(2,1)S(1)} %pad_maximum_fusion.4.refs_1_), channel_id=1, source_target_pairs={{0,2},{1,3},{2,0},{3,1},{4,6},{5,7},{6,4},{7,5},{8,10},{9,11},{10,... | collective-permute-start | bytes 3342344 | tf_op jit(solution)/shard_map/ppermute | solution.py:31
  93.0 32.9 %collective-permute-start.11 = (bf16[4,64,2176]{2,1,0:T(8,128)(2,1)}, bf16[4,64,2176]{2,1,0:T(8,128)(2,1)}, u32[]{:S(2)}, u32[]{:S(2)}) collective-permute-start(bf16[4,64,2176]{2,1,0:T(8,128)(2,1)} %collective-permute-done.6.refs_3_), channel_id=1, source_target_pairs={{0,1},{1,0},{2,3},{3,2},{4,5},{5,4},{6,7},{7,6},{8,9},{9,8},{10,11... | collective-permute-start | bytes 3342344 | tf_op jit(solution)/shard_map/ppermute | solution.py:31
  99.9 40.9 %collective-permute-start.12 = (bf16[4,64,2176]{2,1,0:T(8,128)(2,1)}, bf16[4,64,2176]{2,1,0:T(8,128)(2,1)}, u32[]{:S(2)}, u32[]{:S(2)}) collective-permute-start(bf16[4,64,2176]{2,1,0:T(8,128)(2,1)} %collective-permute-done.7.refs_2_), channel_id=1, source_target_pairs={{0,16},{16,0},{1,17},{17,1},{2,18},{18,2},{3,19},{19,3},{4,20},{20... | collective-permute-start | bytes 3342344 | tf_op jit(solution)/shard_map/ppermute | solution.py:28
  104.0 37.8 %collective-permute-start.53 = (bf16[256,2048]{1,0:T(8,128)(2,1)}, bf16[256,2048]{1,0:T(8,128)(2,1)}, u32[]{:S(2)}, u32[]{:S(2)}) collective-permute-start(bf16[256,2048]{1,0:T(8,128)(2,1)} %get-tuple-element.167), channel_id=1, source_target_pairs={{0,4},{4,0},{8,12},{12,8},{1,5},{5,1},{9,13},{13,9},{2,6},{6,2},{1... | collective-permute-start | bytes 3145736 | tf_op jit(solution)/shard_map/ppermute | solution.py:25
  120.2 59.4 %collective-permute-start.22 = (bf16[256,2048]{1,0:T(8,128)(2,1)}, bf16[256,2048]{1,0:T(8,128)(2,1)}, u32[]{:S(2)}, u32[]{:S(2)}) collective-permute-start(bf16[256,2048]{1,0:T(8,128)(2,1)} %get-tuple-element.136.refs_9_), channel_id=1, source_target_pairs={{0,4},{4,0},{8,12},{12,8},{1,5},{5,1},{9,13},{13,9},{2,6},{6,2},{1... | collective-permute-start | bytes 3145736 | tf_op jit(solution)/shard_map/ppermute | solution.py:25
  141.3 36.6 %collective-permute-start.20 = (bf16[4,64,2816]{2,1,0:T(8,128)(2,1)}, bf16[4,64,2816]{2,1,0:T(8,128)(2,1)}, u32[]{:S(2)}, u32[]{:S(2)}) collective-permute-start(bf16[4,64,2816]{2,1,0:T(8,128)(2,1)} %pad_maximum_fusion.3.refs_1_.refs_2_), channel_id=1, source_target_pairs={{0,1},{1,0},{2,3},{3,2},{4,5},{5,4},{6,7},{7,6},{8,9},{9,8},{10,11... | collective-permute-start | bytes 4325384 | tf_op jit(solution)/shard_map/ppermute | solution.py:31
  141.8 37.8 %collective-permute-start.23 = (bf16[256,2048]{1,0:T(8,128)(2,1)}, bf16[256,2048]{1,0:T(8,128)(2,1)}, u32[]{:S(2)}, u32[]{:S(2)}) collective-permute-start(bf16[256,2048]{1,0:T(8,128)(2,1)} %collective-permute-done.10.refs_11_), channel_id=1, source_target_pairs={{0,4},{4,0},{8,12},{12,8},{1,5},{5,1},{9,13},{13,9},{2,6},{6,2},{1... | collective-permute-start | bytes 3145736 | tf_op jit(solution)/shard_map/ppermute | solution.py:25
  169.1 70.9 %collective-permute-start.30 = (bf16[256,2048]{1,0:T(8,128)(2,1)}, bf16[256,2048]{1,0:T(8,128)(2,1)}, u32[]{:S(2)}, u32[]{:S(2)}) collective-permute-start(bf16[256,2048]{1,0:T(8,128)(2,1)} %get-tuple-element.139.refs_9_), channel_id=1, source_target_pairs={{0,4},{4,0},{8,12},{12,8},{1,5},{5,1},{9,13},{13,9},{2,6},{6,2},{1... | collective-permute-start | bytes 3145736 | tf_op jit(solution)/shard_map/ppermute | solution.py:25
  178.0 60.5 %collective-permute-start.17 = (bf16[4,64,2816]{2,1,0:T(8,128)(2,1)}, bf16[4,64,2816]{2,1,0:T(8,128)(2,1)}, u32[]{:S(2)}, u32[]{:S(2)}) collective-permute-start(bf16[4,64,2816]{2,1,0:T(8,128)(2,1)} %pad_maximum_fusion.3.refs_1_.refs_2_), channel_id=1, source_target_pairs={{0,2},{1,3},{2,0},{3,1},{4,6},{5,7},{6,4},{7,5},{8,10},{9,11},{10,... | collective-permute-start | bytes 4325384 | tf_op jit(solution)/shard_map/ppermute | solution.py:31
  179.6 29.3 %collective-permute-start.54 = (bf16[256,2048]{1,0:T(8,128)(2,1)}, bf16[256,2048]{1,0:T(8,128)(2,1)}, u32[]{:S(2)}, u32[]{:S(2)}) collective-permute-start(bf16[256,2048]{1,0:T(8,128)(2,1)} %collective-permute-done.41), channel_id=1, source_target_pairs={{0,4},{4,0},{8,12},{12,8},{1,5},{5,1},{9,13},{13,9},{2,6},{6,2},{1... | collective-permute-start | bytes 3145736 | tf_op jit(solution)/shard_map/ppermute | solution.py:25
  179.6 60.4 %collective-permute-start.26 = (bf16[4,64,2816]{2,1,0:T(8,128)(2,1)}, bf16[4,64,2816]{2,1,0:T(8,128)(2,1)}, u32[]{:S(2)}, u32[]{:S(2)}) collective-permute-start(bf16[4,64,2816]{2,1,0:T(8,128)(2,1)} %pad_maximum_fusion.3.refs_1_.refs_2_), channel_id=1, source_target_pairs={{0,16},{16,0},{1,17},{17,1},{2,18},{18,2},{3,19},{19,3},{4,20},{20... | collective-permute-start | bytes 4325384 | tf_op jit(solution)/shard_map/ppermute | solution.py:28
  206.3 34.3 %collective-permute-start.31 = (bf16[256,2048]{1,0:T(8,128)(2,1)}, bf16[256,2048]{1,0:T(8,128)(2,1)}, u32[]{:S(2)}, u32[]{:S(2)}) collective-permute-start(bf16[256,2048]{1,0:T(8,128)(2,1)} %copy-done.60), channel_id=1, source_target_pairs={{0,4},{4,0},{8,12},{12,8},{1,5},{5,1},{9,13},{13,9},{2,6},{6,2},{1... | collective-permute-start | bytes 3145736 | tf_op jit(solution)/shard_map/ppermute | solution.py:25
  228.1 40.7 %collective-permute-start.32 = (bf16[4,4,128,128]{3,2,1,0:T(8,128)(2,1)}, bf16[4,4,128,128]{3,2,1,0:T(8,128)(2,1)S(1)}, u32[]{:S(2)}, u32[]{:S(2)}) collective-permute-start(bf16[4,4,128,128]{3,2,1,0:T(8,128)(2,1)} %add_convert_fusion.25), channel_id=1, source_target_pairs={{0,1},{4,5},{8,9},{12,13},{16,17},{20,21},{24,25},{28,29}} | collective-permute-start | bytes 1572872 | tf_op jit(solution)/shard_map/ppermute | solution.py:546
  238.5 46.8 %collective-permute-start.38 = (bf16[4,64,2816]{2,1,0:T(8,128)(2,1)}, bf16[4,64,2816]{2,1,0:T(8,128)(2,1)}, u32[]{:S(2)}, u32[]{:S(2)}) collective-permute-start(bf16[4,64,2816]{2,1,0:T(8,128)(2,1)} %collective-permute-done.20.refs_2_.refs_3_), channel_id=1, source_target_pairs={{0,16},{16,0},{1,17},{17,1},{2,18},{18,2},{3,19},{19,3},{4,20},{20... | collective-permute-start | bytes 4325384 | tf_op jit(solution)/shard_map/ppermute | solution.py:28
  240.0 33.1 %collective-permute-start.33 = (bf16[4,64,2816]{2,1,0:T(8,128)(2,1)}, bf16[4,64,2816]{2,1,0:T(8,128)(2,1)}, u32[]{:S(2)}, u32[]{:S(2)}) collective-permute-start(bf16[4,64,2816]{2,1,0:T(8,128)(2,1)} %collective-permute-done.17.refs_3_.refs_4_), channel_id=1, source_target_pairs={{0,1},{1,0},{2,3},{3,2},{4,5},{5,4},{6,7},{7,6},{8,9},{9,8},{10,11... | collective-permute-start | bytes 4325384 | tf_op jit(solution)/shard_map/ppermute | solution.py:31
  240.0 62.6 %collective-permute-start.18 = (bf16[4,64,2816]{2,1,0:T(8,128)(2,1)}, bf16[4,64,2816]{2,1,0:T(8,128)(2,1)}, u32[]{:S(2)}, u32[]{:S(2)}) collective-permute-start(bf16[4,64,2816]{2,1,0:T(8,128)(2,1)} %collective-permute-done.17.refs_3_.refs_4_), channel_id=1, source_target_pairs={{0,16},{16,0},{1,17},{17,1},{2,18},{18,2},{3,19},{19,3},{4,20},{20... | collective-permute-start | bytes 4325384 | tf_op jit(solution)/shard_map/ppermute | solution.py:28
  240.6 44.7 %collective-permute-start.42 = (bf16[256,2048]{1,0:T(8,128)(2,1)}, bf16[256,2048]{1,0:T(8,128)(2,1)}, u32[]{:S(2)}, u32[]{:S(2)}) collective-permute-start(bf16[256,2048]{1,0:T(8,128)(2,1)} %get-tuple-element.168), channel_id=1, source_target_pairs={{0,8},{4,12},{8,0},{12,4},{1,9},{5,13},{9,1},{13,5},{2,10},{6,14},... | collective-permute-start | bytes 3145736 | tf_op jit(solution)/shard_map/ppermute | solution.py:25
  322.2 527.1 %reduce-scatter.5.cloned.1.call-start = ((), (), s32[]{:S(2)}) async-start(), calls=%async_computation.3 | async-start | bytes 6488064 | tf_op jit(solution)/shard_map/reduce_scatter | solution.py:611
  339.8 45.3 %collective-permute-start.46 = (bf16[1,256,2048]{2,1,0:T(8,128)(2,1)S(1)}, bf16[1,256,2048]{2,1,0:T(8,128)(2,1)S(1)}, u32[]{:S(2)}, u32[]{:S(2)}) collective-permute-start(bf16[1,256,2048]{2,1,0:T(8,128)(2,1)S(1)} %fusion.49), channel_id=1, source_target_pairs={{0,8},{4,12},{8,0},{12,4},{1,9},{5,13},{9,1},{13,5},{2,10},{6,14},... | collective-permute-start | bytes 3145736 | tf_op jit(solution)/shard_map/ppermute | solution.py:25
  341.4 52.2 %collective-permute-start.55 = (bf16[256,2048]{1,0:T(8,128)(2,1)}, bf16[256,2048]{1,0:T(8,128)(2,1)S(1)}, u32[]{:S(2)}, u32[]{:S(2)}) collective-permute-start(bf16[256,2048]{1,0:T(8,128)(2,1)} %get-tuple-element.168), channel_id=1, source_target_pairs={{0,4},{4,0},{8,12},{12,8},{1,5},{5,1},{9,13},{13,9},{2,6},{6,2},{1... | collective-permute-start | bytes 3145736 | tf_op jit(solution)/shard_map/ppermute | solution.py:25
  391.6 45.5 %collective-permute-start.39 = (bf16[4,64,2816]{2,1,0:T(8,128)(2,1)}, bf16[4,64,2816]{2,1,0:T(8,128)(2,1)S(1)}, u32[]{:S(2)}, u32[]{:S(2)}) collective-permute-start(bf16[4,64,2816]{2,1,0:T(8,128)(2,1)} %collective-permute-done.33.refs_4_.refs_5_), channel_id=1, source_target_pairs={{0,16},{16,0},{1,17},{17,1},{2,18},{18,2},{3,19},{19,3},{4,20},{20... | collective-permute-start | bytes 4325384 | tf_op jit(solution)/shard_map/ppermute | solution.py:28
  393.3 43.8 %collective-permute-start.50 = (bf16[256,2048]{1,0:T(8,128)(2,1)S(1)}, bf16[256,2048]{1,0:T(8,128)(2,1)S(1)}, u32[]{:S(2)}, u32[]{:S(2)}) collective-permute-start(bf16[256,2048]{1,0:T(8,128)(2,1)S(1)} %get-tuple-element.304.refs_9_), channel_id=1, source_target_pairs={{0,4},{4,0},{8,12},{12,8},{1,5},{5,1},{9,13},{13,9},{2,6},{6,2},{1... | collective-permute-start | bytes 3145736 | tf_op jit(solution)/shard_map/ppermute | solution.py:25
  393.6 43.5 %collective-permute-start.48 = (bf16[256,2048]{1,0:T(8,128)(2,1)S(1)}, bf16[256,2048]{1,0:T(8,128)(2,1)}, u32[]{:S(2)}, u32[]{:S(2)}) collective-permute-start(bf16[256,2048]{1,0:T(8,128)(2,1)S(1)} %get-tuple-element.305.refs_9_), channel_id=1, source_target_pairs={{0,8},{4,12},{8,0},{12,4},{1,9},{5,13},{9,1},{13,5},{2,10},{6,14},... | collective-permute-start | bytes 3145736 | tf_op jit(solution)/shard_map/ppermute | solution.py:25
  420.7 41.0 %collective-permute-start.47 = (bf16[256,2048]{1,0:T(8,128)(2,1)S(1)}, bf16[256,2048]{1,0:T(8,128)(2,1)}, u32[]{:S(2)}, u32[]{:S(2)}) collective-permute-start(bf16[256,2048]{1,0:T(8,128)(2,1)S(1)} %get-tuple-element.305.refs_9_), channel_id=1, source_target_pairs={{0,4},{4,0},{8,12},{12,8},{1,5},{5,1},{9,13},{13,9},{2,6},{6,2},{1... | collective-permute-start | bytes 3145736 | tf_op jit(solution)/shard_map/ppermute | solution.py:25
  543.4 565.1 %reduce-scatter.3.cloned.1.call-start = ((), (), s32[]{:S(2)}) async-start(), calls=%async_computation.2 | async-start | bytes 4718592 | tf_op jit(solution)/shard_map/reduce_scatter | solution.py:611
  569.3 35.2 %collective-permute-start.61 = (bf16[256,2048]{1,0:T(8,128)(2,1)}, bf16[256,2048]{1,0:T(8,128)(2,1)}, u32[]{:S(2)}, u32[]{:S(2)}) collective-permute-start(bf16[256,2048]{1,0:T(8,128)(2,1)} %add_convert_fusion.7.refs_9_), channel_id=1, source_target_pairs={{0,8},{4,12},{8,0},{12,4},{1,9},{5,13},{9,1},{13,5},{2,10},{6,14},... | collective-permute-start | bytes 3145736 | tf_op jit(solution)/shard_map/ppermute | solution.py:25
  623.9 164.0 %collective-permute-start.77 = (bf16[1024,2816]{1,0:T(8,128)(2,1)}, bf16[1024,2816]{1,0:T(8,128)(2,1)}, u32[]{:S(2)}, u32[]{:S(2)}) collective-permute-start(bf16[1024,2816]{1,0:T(8,128)(2,1)} %convolution_convert_fusion.2), channel_id=1, source_target_pairs={{0,16},{16,0},{1,17},{17,1},{2,18},{18,2},{3,19},{19,3},{4,20},{20... | collective-permute-start | bytes 17301512 | tf_op jit(solution)/shard_map/ppermute | solution.py:28
  627.3 34.9 %collective-permute-start.63 = (bf16[1,256,2048]{2,1,0:T(8,128)(2,1)}, bf16[1,256,2048]{2,1,0:T(8,128)(2,1)S(1)}, u32[]{:S(2)}, u32[]{:S(2)}) collective-permute-start(bf16[1,256,2048]{2,1,0:T(8,128)(2,1)} %fusion.51), channel_id=1, source_target_pairs={{0,8},{4,12},{8,0},{12,4},{1,9},{5,13},{9,1},{13,5},{2,10},{6,14},... | collective-permute-start | bytes 3145736 | tf_op jit(solution)/shard_map/ppermute | solution.py:25
  685.6 32.5 %collective-permute-start.67 = (bf16[256,2048]{1,0:T(8,128)(2,1)}, bf16[256,2048]{1,0:T(8,128)(2,1)}, u32[]{:S(2)}, u32[]{:S(2)}) collective-permute-start(bf16[256,2048]{1,0:T(8,128)(2,1)} %add_convert_fusion.5.refs_9_), channel_id=1, source_target_pairs={{0,4},{4,0},{8,12},{12,8},{1,5},{5,1},{9,13},{13,9},{2,6},{6,2},{1... | collective-permute-start | bytes 3145736 | tf_op jit(solution)/shard_map/ppermute | solution.py:25
  715.2 77.0 %collective-permute-start.65 = (bf16[4,256,2048]{2,1,0:T(8,128)(2,1)}, bf16[4,256,2048]{2,1,0:T(8,128)(2,1)}, u32[]{:S(2)}, u32[]{:S(2)}) collective-permute-start(bf16[4,256,2048]{2,1,0:T(8,128)(2,1)} %get-tuple-element.201), channel_id=1, source_target_pairs={{0,4},{4,0},{8,12},{12,8},{1,5},{5,1},{9,13},{13,9},{2,6},{6,2},{1... | collective-permute-start | bytes 12582920 | tf_op jit(solution)/shard_map/ppermute | solution.py:25
  748.6 38.2 %collective-permute-start.78 = (bf16[4,4,128,128]{3,2,1,0:T(8,128)(2,1)S(1)}, bf16[4,4,128,128]{3,2,1,0:T(8,128)(2,1)S(1)}, u32[]{:S(2)}, u32[]{:S(2)}) collective-permute-start(bf16[4,4,128,128]{3,2,1,0:T(8,128)(2,1)S(1)} %add_convert_fusion.15), channel_id=1, source_target_pairs={{1,0},{5,4},{9,8},{13,12},{17,16},{21,20},{25,24},{29,28}} | collective-permute-start | bytes 1572872 | tf_op jit(solution)/shard_map/ppermute | solution.py:546
  792.2 63.3 %collective-permute-start.79 = (bf16[4,2,64,2816]{3,2,1,0:T(8,128)(2,1)}, bf16[4,2,64,2816]{3,2,1,0:T(8,128)(2,1)}, u32[]{:S(2)}, u32[]{:S(2)}) collective-permute-start(bf16[4,2,64,2816]{3,2,1,0:T(8,128)(2,1)} %fusion.19), channel_id=1, source_target_pairs={{0,1},{1,0},{2,3},{3,2},{4,5},{5,4},{6,7},{7,6},{8,9},{9,8},{10,11... | collective-permute-start | bytes 8650760 | tf_op jit(solution)/shard_map/ppermute | solution.py:31
  795.9 37.6 %collective-permute-start.70 = (bf16[256,2048]{1,0:T(8,128)(2,1)}, bf16[256,2048]{1,0:T(8,128)(2,1)}, u32[]{:S(2)}, u32[]{:S(2)}) collective-permute-start(bf16[256,2048]{1,0:T(8,128)(2,1)} %get-tuple-element.270), channel_id=1, source_target_pairs={{0,8},{4,12},{8,0},{12,4},{1,9},{5,13},{9,1},{13,5},{2,10},{6,14},... | collective-permute-start | bytes 3145736 | tf_op jit(solution)/shard_map/ppermute | solution.py:25
  796.3 46.0 %collective-permute-start.71 = (bf16[256,2048]{1,0:T(8,128)(2,1)}, bf16[256,2048]{1,0:T(8,128)(2,1)}, u32[]{:S(2)}, u32[]{:S(2)}) collective-permute-start(bf16[256,2048]{1,0:T(8,128)(2,1)} %get-tuple-element.271), channel_id=1, source_target_pairs={{0,8},{4,12},{8,0},{12,4},{1,9},{5,13},{9,1},{13,5},{2,10},{6,14},... | collective-permute-start | bytes 3145736 | tf_op jit(solution)/shard_map/ppermute | solution.py:25
  832.7 79.1 %collective-permute-start.100 = (bf16[1024,512]{1,0:T(8,128)(2,1)}, bf16[1024,512]{1,0:T(8,128)(2,1)}, u32[]{:S(2)}, u32[]{:S(2)}) collective-permute-start(bf16[1024,512]{1,0:T(8,128)(2,1)} %fusion.27), channel_id=1, source_target_pairs={{0,16},{16,0},{1,17},{17,1},{2,18},{18,2},{3,19},{19,3},{4,20},{20... | collective-permute-start | bytes 3145736 | tf_op jit(solution)/shard_map/ppermute | solution.py:28
  833.5 58.5 %collective-permute-start.97 = (bf16[256,2048]{1,0:T(8,128)(2,1)}, bf16[256,2048]{1,0:T(8,128)(2,1)}, u32[]{:S(2)}, u32[]{:S(2)}) collective-permute-start(bf16[256,2048]{1,0:T(8,128)(2,1)} %convolution_convert_fusion.4), channel_id=1, source_target_pairs={{0,16},{16,0},{1,17},{17,1},{2,18},{18,2},{3,19},{19,3},{4,20},{20... | collective-permute-start | bytes 3145736 | tf_op jit(solution)/shard_map/ppermute | solution.py:28
  854.5 134.8 %collective-permute-start.76 = (bf16[1,256,2048]{2,1,0:T(8,128)(2,1)}, bf16[1,256,2048]{2,1,0:T(8,128)(2,1)}, u32[]{:S(2)}, u32[]{:S(2)}) collective-permute-start(bf16[1,256,2048]{2,1,0:T(8,128)(2,1)} %fusion.54), channel_id=1, source_target_pairs={{0,8},{4,12},{8,0},{12,4},{1,9},{5,13},{9,1},{13,5},{2,10},{6,14},... | collective-permute-start | bytes 3145736 | tf_op jit(solution)/shard_map/ppermute | solution.py:25
  862.1 153.7 %collective-permute-start.93 = (bf16[4,1,64,2816]{3,2,1,0:T(8,128)(2,1)}, bf16[4,1,64,2816]{3,2,1,0:T(8,128)(2,1)}, u32[]{:S(2)}, u32[]{:S(2)}) collective-permute-start(bf16[4,1,64,2816]{3,2,1,0:T(8,128)(2,1)} %bitcast.121), channel_id=1, source_target_pairs={{0,2},{1,3},{2,0},{3,1},{4,6},{5,7},{6,4},{7,5},{8,10},{9,11},{10,... | collective-permute-start | bytes 4325384 | tf_op jit(solution)/shard_map/ppermute | solution.py:31
  895.3 66.6 %collective-permute-start.98 = (bf16[1,2,64,2048]{3,2,1,0:T(8,128)(2,1)}, bf16[1,2,64,2048]{3,2,1,0:T(8,128)(2,1)}, u32[]{:S(2)}, u32[]{:S(2)}) collective-permute-start(bf16[1,2,64,2048]{3,2,1,0:T(8,128)(2,1)} %fusion.65), channel_id=1, source_target_pairs={{0,1},{1,0},{2,3},{3,2},{4,5},{5,4},{6,7},{7,6},{8,9},{9,8},{10,11... | collective-permute-start | bytes 1572872 | tf_op jit(solution)/shard_map/ppermute | solution.py:31
  913.2 73.9 %collective-permute-start.101 = (bf16[4,2,64,512]{3,2,1,0:T(8,128)(2,1)S(1)}, bf16[4,2,64,512]{3,2,1,0:T(8,128)(2,1)S(1)}, u32[]{:S(2)}, u32[]{:S(2)}) collective-permute-start(bf16[4,2,64,512]{3,2,1,0:T(8,128)(2,1)S(1)} %fusion.66), channel_id=1, source_target_pairs={{0,1},{1,0},{2,3},{3,2},{4,5},{5,4},{6,7},{7,6},{8,9},{9,8},{10,11... | collective-permute-start | bytes 1572872 | tf_op jit(solution)/shard_map/ppermute | solution.py:31
  920.5 95.2 %collective-permute-start.82 = (bf16[1024,512]{1,0:T(8,128)(2,1)}, bf16[1024,512]{1,0:T(8,128)(2,1)}, u32[]{:S(2)}, u32[]{:S(2)}) collective-permute-start(bf16[1024,512]{1,0:T(8,128)(2,1)} %fusion.33), channel_id=1, source_target_pairs={{0,16},{16,0},{1,17},{17,1},{2,18},{18,2},{3,19},{19,3},{4,20},{20... | collective-permute-start | bytes 3145736 | tf_op jit(solution)/shard_map/ppermute | solution.py:28
  963.8 41.9 %collective-permute-start.99 = (bf16[1,1,64,2048]{3,2,1,0:T(8,128)(2,1)}, bf16[1,1,64,2048]{3,2,1,0:T(8,128)(2,1)}, u32[]{:S(2)}, u32[]{:S(2)}) collective-permute-start(bf16[1,1,64,2048]{3,2,1,0:T(8,128)(2,1)} %fusion.68), channel_id=1, source_target_pairs={{0,2},{1,3},{2,0},{3,1},{4,6},{5,7},{6,4},{7,5},{8,10},{9,11},{10,... | collective-permute-start | bytes 786440 | tf_op jit(solution)/shard_map/ppermute | solution.py:31
  1010.1 29.5 %collective-permute-start.80 = (bf16[1,2,256,2048]{3,2,1,0:T(8,128)(2,1)}, bf16[1,2,256,2048]{3,2,1,0:T(8,128)(2,1)}, u32[]{:S(2)}, u32[]{:S(2)}) collective-permute-start(bf16[1,2,256,2048]{3,2,1,0:T(8,128)(2,1)} %bitcast.530), channel_id=1, source_target_pairs={{0,4},{4,0},{8,12},{12,8},{1,5},{5,1},{9,13},{13,9},{2,6},{6,2},{1... | collective-permute-start | bytes 6291464 | tf_op jit(solution)/shard_map/ppermute | solution.py:25
  1042.3 44.0 %collective-permute-start.81 = (bf16[1,256,2048]{2,1,0:T(8,128)(2,1)}, bf16[1,256,2048]{2,1,0:T(8,128)(2,1)}, u32[]{:S(2)}, u32[]{:S(2)}) collective-permute-start(bf16[1,256,2048]{2,1,0:T(8,128)(2,1)} %fusion.55), channel_id=1, source_target_pairs={{0,8},{4,12},{8,0},{12,4},{1,9},{5,13},{9,1},{13,5},{2,10},{6,14},... | collective-permute-start | bytes 3145736 | tf_op jit(solution)/shard_map/ppermute | solution.py:25
  (159 other events, 2242.9 us)
Sparse Core Ops, SparseCore 0:
  322.3 93.0 all-gather.2
  543.6 113.9 reduce-scatter.4
  911.9 110.9 reduce-scatter.2

commit v3 on v2

--- a/solution.py
+++ b/solution.py
@@ -35,14 +35,15 @@
         stack = jnp.where(odd, jnp.concatenate([stack[1:2], stack[0:1], stack[3:4], stack[2:3]]), stack)
         return jnp.where(high, jnp.concatenate([stack[2:], stack[:2]]), stack)
 
-    def team_gather(self, own):
+    def team_gather(self, own, *held):
         one, two = self.swap(own, 1), self.swap(own, 2)
-        return [own, one, two, self.swap(two, 1)]
+        return [own, one, two, self.swap(after(two, *held), 1)]
 
     def team_sum(self, even, odd, first_held, *held):
         near = self.swap(after(odd, *first_held), 1)
         sent = (even[:, 1].astype(F32) + after(near, *held)[:, 1].astype(F32)).astype(BF16)
-        return even[:, 0].astype(F32) + near[:, 0].astype(F32) + self.swap(sent, 2).astype(F32), sent
+        far = self.swap(sent, 2)
+        return lambda *held: even[:, 0].astype(F32) + near[:, 0].astype(F32) + after(far, *held).astype(F32), sent, far
 
 
     def gather_blocks(self, own):
@@ -182,6 +183,14 @@
             at = pl.multiple_of((k * TEAM + (rank ^ j)) * strip, strip)
             out_ref[:, k * strip : (k + 1) * strip] = w_ref[:, pl.ds(at, strip)]
         out_ref[:, count * strip :] = extra_ref[...]
+
+
+def place_kernel(strip, place_ref, *refs):
+    out_ref = refs[-1]
+    for j, ref in enumerate(refs[:-1]):
+        for k in range(ref.shape[1] // strip):
+            at = pl.multiple_of((k * TEAM + (place_ref[0] ^ j)) * strip, strip)
+            out_ref[:, pl.ds(at, strip)] = ref[:, k * strip : (k + 1) * strip].astype(F32)
 
 
 def mix_kernel(strip, step, fetch, piece_refs, place_ref, row_ref, col_ref, *refs):
@@ -505,7 +514,9 @@
             waits["out", 0] = (gy2,)
 
             def later(*held):
-                found_gu = found(gu_own, g1, g2, g12, gy, gy1, gy2, cross(g12))
+                gy12 = cross(g12)
+                waits["norm", 0] = (gy12,)
+                found_gu = found(gu_own, g1, g2, g12, gy, gy1, gy2, gy12)
                 return Weight(at, found_gu), Weight(at, lax.all_gather(after(w_down, *held), team)[:, None])
 
             def found(own, a1, a2, a12, y, y1, y2, y12):
@@ -539,14 +550,15 @@
         def pass_on(leaving, fade, sign, *held):
             factor = fade.reshape(TEAM, heads, HEAD)[..., None]
             entering = jnp.zeros(leaving.shape, F32)
-            hops = []
+            hops, moved = [], None
             for k in range(nz - 1):
+                if moved is not None:
+                    entering = entering + moved.astype(F32)
                 pair = (k, k + 1) if sign == 1 else (nz - 1 - k, nz - 2 - k)
                 moved = (factor * entering + leaving).astype(BF16)
                 moved = lax.ppermute(after(moved, *held) if k == 1 else moved, "seq", [pair])
                 hops.append(moved)
-                entering = entering + moved.astype(F32)
-            return entering.astype(BF16), hops
+            return lambda *held: (entering + after(moved, *held).astype(F32)).astype(BF16), hops
 
         span, part, pair = (total, length), (TEAM, length), (TEAM // 2, length, features)
         states = (TEAM, heads, HEAD, HEAD)
@@ -555,7 +567,7 @@
 
         normed = proj = running = qd = kg = mixed = gated = None
         normed2 = hidden = first = second = None
-        entering, residual, fades, team_normed2 = [], [], [], []
+        entering, residual, fades, own_normed2 = [], [], [], []
         insides, leavings = [], []
         for c in range(micro):
             rows_c, cols_c = (a[c * TEAM : (c + 1) * TEAM] for a in (count_row, count_col))
@@ -582,7 +594,7 @@
             fades.append(fade)
             insides.append(inside)
             leavings.append(leaving)
-            entering.append(pass_on(leaving, fade, 1, *waits.get(("hop", c), ()))[0])
+            entering.append(pass_on(leaving, fade, 1, *waits.get(("hop", c), ()))[0]())
         gu, down = later(*entering)
         for c in range(micro):
             cols_c = count_col[c * TEAM : (c + 1) * TEAM]
@@ -598,17 +610,19 @@
                 ],
                 [mixed, gated], [out], (), per_matmul * own_channels,
             )
-            residual.append(block_in[c].astype(F32) + at.team_sum(even[None], odd[None], ())[0][0])
+            summed = at.team_sum(even[None], odd[None], ())[0](*own_normed2)
+            residual.append(block_in[c].astype(F32) + summed[0])
             rms_two = lax.rsqrt(jnp.mean(residual[c] * residual[c], axis=-1, keepdims=True) + EPSILON)
-            team_normed2.append(at.team_gather((residual[c] * rms_two * ffn_scale).astype(BF16)))
+            own_normed2.append(after(residual[c] * rms_two * ffn_scale, *waits.get(("norm", c), ())).astype(BF16))
 
         def flat(a):
             return a.reshape(tokens, a.shape[-1])
 
-        def team_share(left, right, s):
+        def team_share(left, right, s, *held):
             product = tn(left, right).astype(BF16).reshape(ny, s, nz, -1, right.shape[1])
             product = jnp.swapaxes(product, 1, 2).reshape(ny * nz, -1, right.shape[1])
-            return lax.psum_scatter(product, team, scatter_dimension=0, tiled=False).reshape(s, -1, right.shape[1]), product
+            summed = lax.psum_scatter(after(product, *held), team, scatter_dimension=0, tiled=False)
+            return summed.reshape(s, -1, right.shape[1]), product
 
         def weight_half(left, right, k):
             size = left.shape[1] // ny
@@ -620,30 +634,41 @@
         def weight_halves(left, right):
             return [weight_half(left, right, k) for k in range(2 if ny == 2 else 1)]
 
-        def weight_sum(parts, s, held=(), first_held=()):
-            width = parts[0].shape[-1]
-            if ny == 2:
-                send, keep = parts
-                terms = [keep, after(at.swap_y(after(send, *first_held), 1), *held)]
-            else:
-                terms = parts
-                for step in [1 << i for i in reversed(range(ny.bit_length() - 1))]:
-                    halves = [t.reshape((t.shape[0] // 2 // step, 2, step) + t.shape[1:])[0] for t in terms]
-                    bit = (at.y // step) % 2
-                    pick = lambda k: [lax.dynamic_index_in_dim(t, k, 0, False) for t in halves]
-                    send = sum(t.astype(F32) for t in pick(1 - bit)).astype(BF16)
-                    terms = pick(bit) + [at.swap_y(send, step)]
-                terms = [t[0] for t in terms]
-            terms = [t.reshape(s, nz, -1, width) for t in terms]
-            count = nz
-            for i in range(nz.bit_length() - 1):
-                count //= 2
-                halves = [t.reshape((s, count, 2) + t.shape[2:]) for t in terms]
-                bit = (at.z // (1 << i)) % 2
+        class WeightSum:
+            def __init__(self, parts, s, moved=None, hold=()):
+                self.s, width = s, parts[0].shape[-1]
+                if ny == 2:
+                    send, keep = parts
+                    terms = [keep, at.swap_y(send, 1) if moved is None else moved]
+                else:
+                    terms = parts
+                    for step in [1 << i for i in reversed(range(ny.bit_length() - 1))]:
+                        halves = [t.reshape((t.shape[0] // 2 // step, 2, step) + t.shape[1:])[0] for t in terms]
+                        bit = (at.y // step) % 2
+                        pick = lambda k: [lax.dynamic_index_in_dim(t, k, 0, False) for t in halves]
+                        send = sum(t.astype(F32) for t in pick(1 - bit)).astype(BF16)
+                        terms = pick(bit) + [at.swap_y(send, step)]
+                    terms = [t[0] for t in terms]
+                self.terms = [t.reshape(s, nz, -1, width) for t in terms]
+                self.terms[-1] = after(self.terms[-1], *hold)
+                self.left, self.bit = nz, 0
+
+            def step(self, *held):
+                self.left //= 2
+                terms = self.terms[:-1] + [after(self.terms[-1], *held)]
+                halves = [t.reshape((self.s, self.left, 2) + t.shape[2:]) for t in terms]
+                bit = (at.z // (1 << self.bit)) % 2
                 pick = lambda k: [lax.dynamic_index_in_dim(t, k, 2, False) for t in halves]
                 send = sum(t.astype(F32) for t in pick(1 - bit)).astype(BF16)
-                terms = pick(bit) + [at.swap_z(send, 1 << i)]
-            return (lambda i: sum(lax.dynamic_index_in_dim(t[:, 0], i, 0, False).astype(F32) for t in terms)), send
+                self.terms = pick(bit) + [at.swap_z(send, 1 << self.bit)]
+                self.bit += 1
+                return send
+
+            def finish(self, *held):
+                while self.left > 1:
+                    self.step()
+                terms = self.terms[:-1] + [after(self.terms[-1], *held)]
+                return lambda i: sum(lax.dynamic_index_in_dim(t[:, 0], i, 0, False).astype(F32) for t in terms)
 
         def out_of_team(summed, count, *held):
             got = at.by_rank(trade([summed(at.rank ^ j).astype(BF16) for j in range(TEAM)], *held)).astype(F32)
@@ -658,10 +683,11 @@
                 up_kernel, turn("up", c), c, TEAM,
                 [],
                 [(span + (features,), BF16, "all")] + [(span + (own_ff,), BF16, "all")] * 3,
-                [normed2, hidden, first, second], [gu], team_normed2[c], per_matmul * 2 * own_ff,
+                [normed2, hidden, first, second], [gu],
+                at.team_gather(own_normed2[c], *(() if hidden is None else (hidden,))), per_matmul * 2 * own_ff,
             )
         d_residual, d_branch, branch_own, gain_sums, sents = [], [], [], [], []
-        held, branch_sum = (), ()
+        held, moved, sums_of = (), (), []
         for c in range(micro):
             both, even, odd = over_sequences(
                 down_back_kernel, turn("down_back", c, *held), c, TEAM,
@@ -672,21 +698,27 @@
             if c == 0:
                 grad_down, down_product = team_share(after(flat(hidden), even), flat(all_cot), 1)
                 grad_down = grad_down[0].astype(F32)
-            d_normed2, sent = at.team_sum(even[None], odd[None], branch_sum, *((down_product,) if c == 0 else branch_own))
-            held = (down_product, sent)
-            d_normed2 = d_normed2[0]
-            branch_sum = (d_normed2,)
+            else:
+                finish(c - 1, even)
+            d_normed2_of, sent, far = at.team_sum(even[None], odd[None], moved, *((down_product,) if c == 0 else branch_own))
+            held, moved = (down_product, sent), (far,)
             sents.append(sent)
-            res = residual[c]
-            rms_two = lax.rsqrt(jnp.mean(res * res, axis=-1, keepdims=True) + EPSILON)
-            gain_sums.append(jnp.sum(d_normed2 * res * rms_two, axis=0))
-            scaled = d_normed2 * ffn_scale
-            d_residual.append(
-                out_grad[c].astype(F32)
-                + rms_two * (scaled - res * rms_two * rms_two * jnp.mean(scaled * res, axis=-1, keepdims=True))
-            )
-            branch_own.append(d_residual[c].astype(BF16))
-            d_branch.append(at.team_gather(branch_own[c]))
+            sums_of.append(d_normed2_of)
+
+            def finish(c, *held):
+                d_normed2 = sums_of[c](*held)[0]
+                res = residual[c]
+                rms_two = lax.rsqrt(jnp.mean(res * res, axis=-1, keepdims=True) + EPSILON)
+                gain_sums.append(jnp.sum(d_normed2 * res * rms_two, axis=0))
+                scaled = d_normed2 * ffn_scale
+                d_residual.append(
+                    out_grad[c].astype(F32)
+                    + rms_two * (scaled - res * rms_two * rms_two * jnp.mean(scaled * res, axis=-1, keepdims=True))
+                )
+                branch_own.append(d_residual[c].astype(BF16))
+                return branch_own[c]
+
+        finish(micro - 1)
 
         d_q = d_fv = d_o = None
         gs, group_sums, logit_sums, adjoints = [], [], [], []
@@ -712,31 +744,24 @@
 
         toward = place
         gu_send = weight_half(after(flat(normed2), branch_own[0]), flat(both), 0)
+        d_branch = [at.team_gather(branch_own[0], gu_send)]
         hops = []
-        for c in range(micro - 1):
-            whole_branch, d_o, toward, hops = enter_back(c, whole_branch, d_o, gu_send, sents[c + 1])
+        whole_branch, d_o, toward, hops = enter_back(0, whole_branch, d_o, gu_send, *sents[1:])
         gu_halves = [gu_send] + ([weight_half(after(flat(normed2), toward), flat(both), 1)] if ny == 2 else [])
-        even, odd = over_sequences(
-            share_kernel, after(place, gu_halves[-1], branch_own[-1], *hops[:1]), 0, total, [(hidden, "part")],
-            [((micro * TEAM // 2, length, features), BF16, "pair")] * 2, (), [down], (), 2 * tokens * own_ff * features,
-        )
-        whole_branch, d_o, toward, last_hops = enter_back(micro - 1, whole_branch, d_o, even, *hops[1:2])
+        last_hops = hops
+        for c in range(1, micro):
+            d_branch.append(at.team_gather(branch_own[c], gu_halves[-1]))
+            whole_branch, d_o, toward, last_hops = enter_back(c, whole_branch, d_o, gu_halves[-1], grad_down, *hops[:1])
+        adjoints = [adjoint(toward) if c == 0 else adjoint() for c, adjoint in enumerate(adjoints)]
+        gu_rows = sum(t.astype(F32) for t in WeightSum(gu_halves, TEAM, hold=adjoints).terms).astype(BF16)
+        gu_rows = jnp.swapaxes(gu_rows, 0, 1).reshape(nz, TEAM * rows, 2 * own_ff)
+        gu_sum = lax.psum_scatter(gu_rows, "seq", scatter_dimension=0, tiled=False).reshape(TEAM, rows, 2 * own_ff)
         paired = (micro, TEAM // 2, length, features)
-        ffn_near = after(at.swap(odd, 1), toward).reshape(paired)
-        even = even.reshape(paired)
-        ffn_sent = [(even[c, 1].astype(F32) + ffn_near[c, 1].astype(F32)).astype(BF16) for c in range(micro)]
-        block_out = [
-            (residual[c] + (even[c, 0].astype(F32) + ffn_near[c, 0].astype(F32) + at.swap(ffn_sent[c], 2).astype(F32))).astype(BF16)
-            for c in range(micro)
-        ]
-        out_halves = weight_halves(flat(gated), flat(whole_branch))
-        mix_halves = {"o": weight_halves(after(flat(normed), *last_hops[:1]), flat(d_o))}
-        gu_sum, gu_sent = weight_sum(gu_halves, TEAM, adjoints)
 
         d_normed, dn_sent = [], []
         for c in range(micro):
             rows_c, cols_c = (a[c * TEAM : (c + 1) * TEAM] for a in (count_row, count_col))
-            held = (*ffn_sent, *last_hops[1:2], *out_halves, *mix_halves["o"]) if c == 0 else (gu_sent, block_out[0])
+            held = (toward,) if c == 0 else (*ffn_sent, *o_halves, *out_halves)
             d_q, d_fv, logit_sum, even, odd = over_sequences(
                 mix_back_kernel, turn("mix_back", c, *held), c, TEAM,
                 [
@@ -751,15 +776,48 @@
                 [d_q, d_fv], [mix], (), per_matmul * wide,
             )
             logit_sums.append(logit_sum)
-            summed, sent = at.team_sum(even[None], odd[None], ())
-            d_normed.append(summed[0])
+            summed, sent, _ = at.team_sum(even[None], odd[None], ())
+            d_normed.append(summed)
             dn_sent.append(sent)
+            if c == 0:
+                even, odd = over_sequences(
+                    share_kernel, after(place, d_q, *last_hops[:1]), 0, total, [(hidden, "part")],
+                    [((micro * TEAM // 2, length, features), BF16, "pair")] * 2, (), [down], (), 2 * tokens * own_ff * features,
+                )
+                o_halves = weight_halves(after(flat(normed), even, *last_hops[1:2], *dn_sent), flat(d_o))
+                out_halves = weight_halves(after(flat(gated), *o_halves), flat(whole_branch))
+                even, ffn_near = even.reshape(paired), after(at.swap(odd, 1), *o_halves).reshape(paired)
+                ffn_sent = [(even[k, 1].astype(F32) + ffn_near[k, 1].astype(F32)).astype(BF16) for k in range(micro)]
+                block_out = [
+                    residual[k] + (even[k, 0].astype(F32) + ffn_near[k, 0].astype(F32) + at.swap(ffn_sent[k], 2).astype(F32))
+                    for k in range(micro)
+                ]
+                block_out = [a.astype(BF16) for a in block_out]
         last, d_q = d_fv, after(d_q, d_fv)
-        fv_sum, fv_product = team_share(flat(normed), flat(d_fv), TEAM)
-        mix_halves["q"] = [weight_half(after(flat(normed), fv_product), flat(d_q), 0)]
+        d_normed = [summed(last)[0] for summed in d_normed]
         if ny == 2:
-            q_left = after(flat(normed), *dn_sent, *mix_halves["q"])
-            mix_halves["q"].append(weight_half(q_left, flat(d_q), 1))
+            fv_halves = [weight_half(flat(normed), flat(d_fv), 0)]
+            q_halves = [weight_half(after(flat(normed), *fv_halves), flat(d_q), 0)]
+            fv_moved = at.swap_y(fv_halves[0], 1)
+            q_moved = at.swap_y(after(q_halves[0], fv_moved), 1)
+            out_halves[0] = after(out_halves[0], q_moved)
+            left = after(flat(normed), *q_halves, *dn_sent)
+            fv_halves.append(weight_half(left, flat(d_fv), 1))
+            q_halves.append(weight_half(left, flat(d_q), 1))
+        else:
+            fv_halves, q_halves = weight_halves(flat(normed), flat(d_fv)), weight_halves(flat(normed), flat(d_q))
+            fv_moved, q_moved = None, None
+        o_part, out_part = WeightSum(o_halves, TEAM), WeightSum(out_halves, 1)
+        fv_part, q_part = WeightSum(fv_halves, TEAM, fv_moved), WeightSum(q_halves, TEAM, q_moved)
+        sent = o_part.step(fv_halves[-1], q_halves[-1])
+        sent = fv_part.step(sent, *d_normed)
+        q_sent = q_part.step(sent)
+        sent = o_part.step(q_sent)
+        sent = out_part.step(sent)
+        gu_final = lambda i: lax.dynamic_index_in_dim(after(gu_sum, q_sent), i, 0, False)
+        sent = fv_part.step(sent)
+        sent = q_part.step(sent)
+        sent = out_part.step(sent)
         d_normed, block_out = jnp.stack(d_normed), jnp.stack(block_out)
         x = block_in.astype(F32)
         rms_one = lax.rsqrt(jnp.mean(x * x, axis=-1, keepdims=True) + EPSILON)
@@ -774,17 +832,20 @@
             jnp.arange(TEAM)[None, :, None] == at.rank, logit_sum.reshape(ny, 1, strip), 0.0
         ).reshape(features)
         group_all = jnp.sum(sum(jnp.sum(a, axis=(0, 1)) for a in group_sums).reshape(heads, HEAD), axis=0)
-        sums = at.everyone_sum(jnp.concatenate([attn_sum, sum(gain_sums), logit_all, group_all]))
-
-        grad_gu = out_of_team(gu_sum, 2)
-        grad_out = weight_sum(out_halves, 1, (last,), adjoints)[0](0)
-        grads = [
-            out_of_team(weight_sum(mix_halves[name], TEAM, (last, fv_product), adjoints)[0], 1) for name in ("q", "o")
+        sums = at.everyone_sum(after(jnp.concatenate([attn_sum, sum(gain_sums), logit_all, group_all]), q_sent))
+
+        grad_gu = out_of_team(gu_final, 2)
+        parts = [part.finish(sums, grad_gu) for part in (q_part, fv_part, o_part)]
+        parts = [
+            jnp.concatenate([part(at.rank ^ j) for part in parts], axis=1).astype(BF16) for j in range(TEAM)
         ]
-        grad_fv = out_of_team(
-            lambda i: lax.dynamic_index_in_dim(fv_sum, i, 0, False), 2, sums, grad_gu, grad_out, *grads
-        )
-        grad_mix = jnp.concatenate([grads[0], grad_fv, grads[1]], axis=1)
+        grad_mix = pl.pallas_call(
+            partial(place_kernel, strip),
+            in_specs=[pl.BlockSpec(memory_space=pltpu.SMEM)] + [pl.BlockSpec(memory_space=pltpu.VMEM)] * TEAM,
+            out_specs=pl.BlockSpec(memory_space=pltpu.VMEM),
+            out_shape=jax.ShapeDtypeStruct((rows, TEAM * 4 * own_channels), F32),
+        )(place, parts[0], *(at.swap(parts[j], j) for j in range(1, TEAM)))
+        grad_out = out_part.finish(sums)(0)
         here = (at.y * TEAM + at.rank) * nz + at.z
 
         def mine(start, size):

time: 1140 us -> 1050 us (0.921)
  waiting for transfers between devices: 380 us -> 295 us
  starting transfers between devices: 84.3 us -> 117 us
  local copies, waits for them, and re-layouts: 107 us -> 86.3 us
    ppermute x19, waiting for transfers between devices: 131 us -> 58.6 us  [swap_z(): return lax.ppermute(value, 'seq', [(i, i ^ bits) for i in range(self.nz)])]
    ppermute x17 -> x18, waiting for transfers between devices: 49.1 us -> 111 us  [swap_y(): return lax.ppermute(value, 'y', [(i, i ^ bits) for i in range(self.ny)])]
    ppermute x61 -> x55, waiting for transfers between devices: 157 us -> 116 us  [swap(): return lax.ppermute(value, 'team', [(i, i ^ bits) for i in range(TEAM)])]
    ppermute x19, starting transfers between devices: 14.5 us -> 52.5 us  [swap_z(): return lax.ppermute(value, 'seq', [(i, i ^ bits) for i in range(self.nz)])]
    ppermute x12, waiting for transfers between devices: 42.8 us -> 9.53 us  [pass_on(): lax.ppermute(after(moved, *held) if k == 1 else moved, 'seq', [pair])]
    convert_element_type x32 -> x17, other arithmetic: 57.2 us -> 38.1 us  [the longest x8 9.66 us: step(): send = sum((t.astype(F32) for t in pick(1 - bit))).astype(BF16)]
    pallas_call x13, Pallas kernels: 303 us -> 291 us  [over_sequences(): pl.pallas_call(body, grid=(count,), in_specs=specs, out_specs=[spec(shape...]
    ppermute x61 -> x55, starting transfers between devices: 36.1 us -> 28.6 us  [swap(): return lax.ppermute(value, 'team', [(i, i ^ bits) for i in range(TEAM)])]
  transfers between devices with their start and end apart: 112 -> 107, of which waited for: 39 -> 34; matrix products, arithmetic and copies ran while one was open for 29% -> 30% of each run, Pallas kernels for 24% -> 25%
where the time goes in v3:
time: 1050 us; the launch traced here: 1040 us
  Pallas kernels  296 us (28%)
  waiting for transfers between devices  295 us (28%)
  other arithmetic  137 us (13%)
  starting transfers between devices  117 us (11%)
  matrix products  96.5 us (9%)
  local copies, waits for them, and re-layouts  86.3 us (8%)
  between operations  15.6 us (1%)
    pallas_call x13, Pallas kernels, over_sequences(): pl.pallas_call(body, grid=(count,), in_specs=specs, out_specs=[spec(shape...  291 us
    ppermute x55, waiting for transfers between devices, swap(): return lax.ppermute(value, 'team', [(i, i ^ bits) for i in range(TEAM)])  116 us
    ppermute x18, waiting for transfers between devices, swap_y(): return lax.ppermute(value, 'y', [(i, i ^ bits) for i in range(self.ny)])  111 us
    dot_general x11, matrix products, tn(): lax.dot_general(a, b, (((0,), (0,)), ((), ())), preferred_element_type=F32)  96.4 us
    ppermute x19, waiting for transfers between devices, swap_z(): return lax.ppermute(value, 'seq', [(i, i ^ bits) for i in range(self.nz)])  58.6 us
    ppermute x19, starting transfers between devices, swap_z(): return lax.ppermute(value, 'seq', [(i, i ^ bits) for i in range(self.nz)])  52.5 us
    ppermute x55, starting transfers between devices, swap(): return lax.ppermute(value, 'team', [(i, i ^ bits) for i in range(TEAM)])  28.6 us
  transfers between devices with their start and end apart: 107, of which 34 were waited for; matrix products, arithmetic and copies ran while one was open for 30% of the time, Pallas kernels for 25%

profile of v3, /device:TPU:0, one launch (start us, length us, event | category | flops | bytes accessed | tf_op | source)
XLA Modules:
  0.0 1044.3 jit_solution(13653414321044024478)
XLA Ops:
  15.5 7.6 collective-permute-done.1
  23.0 5.6 collective-permute-done.2
  44.1 14.7 %dynamic-slice_reduce_fusion.3 = (bf16[64,4,704]{2,1,0:T(4,128)(2,1)}, bf16[64,4,704]{2,1,0:T(4,128)(2,1)}, bf16[64,4,704]{2,1,0:T(4,128)(2,1)}, bf16[64,4,704]{2,1,0:T(4,128)(2,1)}) fusion(bf16[64,4,4,704]{3,2,1,0:T(4,128)(2,1)} %reshape.1166, s32[]{:T(128)S(6)} %select_n.233, s32[]{:T(128)S(6)} %select_n.235, s32[]{:T(128)S(6)} %select_n.234, ...), kind=kLoop, calls=%fused_computation.150 | loop fusion | bytes 2883600 | tf_op jit(solution)/shard_map/jit(dynamic_index_in_dim)/dynamic_slice | solution.py:471
  69.3 15.2 %collective-permute-done.7.refs_2_ = bf16[4,64,2176]{2,1,0:T(8,128)(2,1)} collective-permute-done((bf16[4,64,2176]{2,1,0:T(8,128)(2,1)S(1)}, bf16[4,64,2176]{2,1,0:T(8,128)(2,1)}, u32[]{:S(2)}, u32[]{:S(2)}) %collective-permute-start.7) | collective-permute-done | bytes 1114144 | tf_op jit(solution)/shard_map/ppermute | solution.py:31
  93.6 6.3 collective-permute-done.16.refs_3_
  104.0 11.6 %collective-permute-done.14.refs_11_ = bf16[256,2048]{1,0:T(8,128)(2,1)S(1)} collective-permute-done((bf16[256,2048]{1,0:T(8,128)(2,1)}, bf16[256,2048]{1,0:T(8,128)(2,1)S(1)}, u32[]{:S(2)}, u32[]{:S(2)}) %collective-permute-start.14) | collective-permute-done | bytes 1048608 | tf_op jit(solution)/shard_map/ppermute | solution.py:25
  120.3 5.7 collective-permute-done.11.refs_4_
  125.9 14.8 %collective-permute-done.12.refs_6_ = bf16[4,64,2176]{2,1,0:T(8,128)(2,1)} collective-permute-done((bf16[4,64,2176]{2,1,0:T(8,128)(2,1)}, bf16[4,64,2176]{2,1,0:T(8,128)(2,1)}, u32[]{:S(2)}, u32[]{:S(2)}) %collective-permute-start.12) | collective-permute-done | bytes 1114144 | tf_op jit(solution)/shard_map/ppermute | solution.py:28
  148.0 14.8 %collective-permute-done.41 = bf16[256,2048]{1,0:T(8,128)(2,1)} collective-permute-done((bf16[256,2048]{1,0:T(8,128)(2,1)}, bf16[256,2048]{1,0:T(8,128)(2,1)}, u32[]{:S(2)}, u32[]{:S(2)}) %collective-permute-start.41) | collective-permute-done | bytes 1048608 | tf_op jit(solution)/shard_map/ppermute | solution.py:25
  169.2 8.8 collective-permute-done.19.refs_4_
  181.7 23.8 %shard_map.187 = (bf16[8,256,2048]{2,1,0:T(8,128)(2,1)}, f32[8,256,2048]{2,1,0:T(8,128)}, f32[8,256,512]{2,1,0:T(8,128)}, bf16[8,256,512]{2,1,0:T(8,128)(2,1)}, ...) custom-call(s32[3]{0:T(128)} %pad_add_fusion.place_ref.refs_0_.refs_, ...), custom_call_target="tpu_custom_call" | custom-call | flops 8589934592 | bytes 3278854 | tf_op jit(solution)/shard_map/pallas_call | solution.py:432
  211.5 9.4 collective-permute-done.27.refs_6_
  230.8 7.7 collective-permute-done.17.refs_3_.refs_4_
  242.1 24.3 %shard_map.188 = (bf16[8,256,2048]{2,1,0:T(8,128)(2,1)}, f32[8,256,2048]{2,1,0:T(8,128)}, f32[8,256,512]{2,1,0:T(8,128)}, bf16[8,256,512]{2,1,0:T(8,128)(2,1)}, ...) custom-call(s32[3]{0:T(128)} %pad_add_fusion.place_ref.refs_0_.refs_, ...), custom_call_target="tpu_custom_call", output_to_operand_aliasing={{0}: (16, {}), {1}: (17, {}), {2}: (18, {}), {3}: (19, {}),... | custom-call | flops 8589934592 | bytes 11667462 | tf_op jit(solution)/shard_map/pallas_call | solution.py:432
  273.9 9.5 collective-permute-done.40
  291.7 10.9 %collective-permute-done.18.refs_7_.refs_8_ = bf16[4,64,2816]{2,1,0:T(8,128)(2,1)} collective-permute-done((bf16[4,64,2816]{2,1,0:T(8,128)(2,1)}, bf16[4,64,2816]{2,1,0:T(8,128)(2,1)}, u32[]{:S(2)}, u32[]{:S(2)}) %collective-permute-start.18) | collective-permute-done | bytes 1441824 | tf_op jit(solution)/shard_map/ppermute | solution.py:28
  307.7 12.2 %shard_map.189 = (f32[8,256,512]{2,1,0:T(8,128)}, bf16[8,256,512]{2,1,0:T(8,128)(2,1)}, bf16[2,256,2048]{2,1,0:T(8,128)(2,1)}, bf16[2,256,2048]{2,1,0:T(8,128)(2,1)}) custom-call(s32[3]{0:T(128)} %pad_add_fusion.place_ref.refs_0_.refs_13_, bf16[1,64,2048]{2,1,0:T(8,128)(2,1)} %bitcast.400, bf16[1,64,2048]{2,1,0:T(8,128)(2,1)} %copy-done.40, ...), custom_call_target="tpu_custom_call" | custom-call | flops 2147483648 | bytes 5899395 | tf_op jit(solution)/shard_map/pallas_call | solution.py:432
  322.1 12.7 %shard_map.190 = (f32[8,256,512]{2,1,0:T(8,128)}, bf16[8,256,512]{2,1,0:T(8,128)(2,1)}, bf16[2,256,2048]{2,1,0:T(8,128)(2,1)}, bf16[2,256,2048]{2,1,0:T(8,128)(2,1)}) custom-call(s32[3]{0:T(128)} %pad_add_fusion.place_ref.refs_0_.refs_13_, bf16[1,64,2048]{2,1,0:T(8,128)(2,1)} %bitcast.401, ...), custom_call_target="tpu_custom_call", output_to_operand_aliasing={{0}: (15, {}), {1}: (16, {})} | custom-call | flops 2147483648 | bytes 7472259 | tf_op jit(solution)/shard_map/pallas_call | solution.py:432
  342.9 20.6 %collective-permute-done.37 = bf16[1,256,2048]{2,1,0:T(8,128)(2,1)S(1)} collective-permute-done((bf16[1,256,2048]{2,1,0:T(8,128)(2,1)S(1)}, bf16[1,256,2048]{2,1,0:T(8,128)(2,1)S(1)}, u32[]{:S(2)}, u32[]{:S(2)}) %collective-permute-start.37) | collective-permute-done | bytes 1048608 | tf_op jit(solution)/shard_map/ppermute | solution.py:25
  368.4 13.9 %collective-permute-done.39.refs_8_.refs_9_ = bf16[4,64,2816]{2,1,0:T(8,128)(2,1)} collective-permute-done((bf16[4,64,2816]{2,1,0:T(8,128)(2,1)}, bf16[4,64,2816]{2,1,0:T(8,128)(2,1)}, u32[]{:S(2)}, u32[]{:S(2)}) %collective-permute-start.39) | collective-permute-done | bytes 1441824 | tf_op jit(solution)/shard_map/ppermute | solution.py:28
  386.0 21.7 %collective-permute-done.50.refs_11_ = bf16[256,2048]{1,0:T(8,128)(2,1)} collective-permute-done((bf16[256,2048]{1,0:T(8,128)(2,1)}, bf16[256,2048]{1,0:T(8,128)(2,1)}, u32[]{:S(2)}, u32[]{:S(2)}) %collective-permute-start.50) | collective-permute-done | bytes 1048608 | tf_op jit(solution)/shard_map/ppermute | solution.py:25
  413.4 22.5 %shard_map.191 = (bf16[8,256,2048]{2,1,0:T(8,128)(2,1)}, bf16[8,256,1408]{2,1,0:T(8,128)(2,1)}, bf16[8,256,1408]{2,1,0:T(8,128)(2,1)}, bf16[8,256,1408]{2,1,0:T(8,128)(2,1)}) custom-call(s32[3]{0:T(128)} %pad_add_fusion.place_ref.refs_0_.refs_13_, bf16[4,64,2816]{2,1,0:T(8,128)(2,1)} %pad_maximum_fusion.2.refs_1_.refs_2_, ...), custom_call_target="tpu_custom_call" | custom-call | flops 11811160064 | bytes 3932163 | tf_op jit(solution)/shard_map/pallas_call | solution.py:432
  444.3 22.7 %shard_map.192 = (bf16[8,256,2048]{2,1,0:T(8,128)(2,1)}, bf16[8,256,1408]{2,1,0:T(8,128)(2,1)}, bf16[8,256,1408]{2,1,0:T(8,128)(2,1)}, bf16[8,256,1408]{2,1,0:T(8,128)(2,1)}) custom-call(s32[3]{0:T(128)} %pad_add_fusion.place_ref.refs_0_.refs_13_, ...), custom_call_target="tpu_custom_call", output_to_operand_aliasing={{0}: (13, {}), {1}: (14, {}), {2}: (15, {}), {3}: (16, {})} | custom-call | flops 11811160064 | bytes 10354691 | tf_op jit(solution)/shard_map/pallas_call | solution.py:432
  467.0 32.2 %shard_map.193 = (bf16[8,256,2816]{2,1,0:T(8,128)(2,1)}, bf16[2,256,2048]{2,1,0:T(8,128)(2,1)}, bf16[2,256,2048]{2,1,0:T(8,128)(2,1)}) custom-call(s32[3]{0:T(128)} %pad_add_fusion.place_ref.refs_0_.refs_13_, bf16[8,1,176,2048]{3,2,1,0:T(8,128)(2,1)} %bitcast.467, bf16[4,64,2816]{2,1,0:T(8,128)(2,1)} %pad_maximum_fusion.2.refs_1_.refs_2_, ...), custom_call_target="tpu_custom_call" | custom-call | flops 17716740096 | bytes 9306115 | tf_op jit(solution)/shard_map/pallas_call | solution.py:432
  499.9 18.1 %convolution_convert_fusion = bf16[1408,2048]{1,0:T(8,128)(2,1)} fusion(bf16[2048,1408]{1,0:T(8,128)(2,1)} %bitcast.480, bf16[2048,2048]{1,0:T(8,128)(2,1)} %bitcast.459), kind=kOutput, calls=%fused_computation.2 | convolution fusion | flops 11814043648 | bytes 19922944 | tf_op jit(solution)/shard_map/dot_general | solution.py:122
  522.5 32.9 %shard_map.194 = (bf16[8,256,2816]{2,1,0:T(8,128)(2,1)}, bf16[2,256,2048]{2,1,0:T(8,128)(2,1)}, bf16[2,256,2048]{2,1,0:T(8,128)(2,1)}) custom-call(s32[3]{0:T(128)} %pad_add_fusion.place_ref.refs_0_.refs_13_, bf16[8,1,176,2048]{3,2,1,0:T(8,128)(2,1)} %bitcast.468, ...), custom_call_target="tpu_custom_call", output_to_operand_aliasing={{0}: (13, {})} | custom-call | flops 17716740096 | bytes 12189699 | tf_op jit(solution)/shard_map/pallas_call | solution.py:432
  564.3 19.7 %convolution_convert_fusion.2 = bf16[1024,2816]{1,0:T(8,128)(2,1)} fusion(bf16[2048,2816]{1,0:T(8,128)(2,1)} %bitcast.476, bf16[2048,2048]{1,0:T(8,128)(2,1)} %bitcast.478, s32[]{:T(128)S(6)} %select_n.237), kind=kOutput, calls=%fused_computation.8 | convolution fusion | flops 11814043648 | bytes 21495812 | tf_op jit(solution)/shard_map/dot_general | solution.py:122
  594.7 11.9 %shard_map.195 = (bf16[8,256,2048]{2,1,0:T(8,128)(2,1)}, bf16[8,256,512]{2,1,0:T(8,128)(2,1)}, bf16[4,256,512]{2,1,0:T(8,128)(2,1)}, f32[4,4,128,128]{3,2,1,0:T(8,128)}, f32[4,1,512]{2,1,0:T(1,128)}) custom-call(s32[3]{0:T(128)} %pad_add_fusion.place_ref.refs_0_.refs_13_, bf16[1,64,2048]{2,1,0:T(8,128)(2,1)} %bitcast.402, bf16[1,64,2048]{2,1,0:T(8,128)(2,1)} %copy-done.40, ...), custom_call_target="tpu_custom_call" | custom-call | flops 2147483648 | bytes 7341187 | tf_op jit(solution)/shard_map/pallas_call | solution.py:432
  609.2 6.7 collective-permute-done.64
  623.0 19.2 %convolution_convert_fusion.1 = bf16[1024,2816]{1,0:T(8,128)(2,1)} fusion(bf16[2048,2816]{1,0:T(8,128)(2,1)} %bitcast.477, bf16[2048,2048]{1,0:T(8,128)(2,1)} %bitcast.479, s32[]{:T(128)S(6)} %select_n.238), kind=kOutput, calls=%fused_computation.7 | convolution fusion | flops 11814043648 | bytes 21495812 | tf_op jit(solution)/shard_map/dot_general | solution.py:122
  658.1 11.7 %shard_map.196 = (bf16[8,256,2048]{2,1,0:T(8,128)(2,1)}, bf16[8,256,512]{2,1,0:T(8,128)(2,1)}, bf16[4,256,512]{2,1,0:T(8,128)(2,1)}, f32[4,4,128,128]{3,2,1,0:T(8,128)}, f32[4,1,512]{2,1,0:T(1,128)}) custom-call(s32[3]{0:T(128)} %pad_add_fusion.place_ref.refs_0_.refs_13_, ...), custom_call_target="tpu_custom_call", output_to_operand_aliasing={{0}: (18, {}), {1}: (19, {})} | custom-call | flops 2147483648 | bytes 9962627 | tf_op jit(solution)/shard_map/pallas_call | solution.py:432
  684.8 29.3 %shard_map.197 = (bf16[8,256,512]{2,1,0:T(8,128)(2,1)}, bf16[8,256,1024]{2,1,0:T(8,128)(2,1)}, f32[4,1,512]{2,1,0:T(1,128)}, bf16[2,256,2048]{2,1,0:T(8,128)(2,1)}, bf16[2,256,2048]{2,1,0:T(8,128)(2,1)}) custom-call(s32[3]{0:T(128)} %pad_add_fusion.place_ref.refs_0_.refs_13_, bf16[4,64,2176]{2,1,0:T(8,128)(2,1)} %copy-done.15, ...), custom_call_target="tpu_custom_call" | custom-call | flops 8589934592 | bytes 17959428 | tf_op jit(solution)/shard_map/pallas_call | solution.py:432
  718.2 25.2 %shard_map.198 = (bf16[4,256,2048]{2,1,0:T(8,128)(2,1)}, bf16[4,256,2048]{2,1,0:T(8,128)(2,1)}) custom-call(s32[3]{0:T(128)} %pad_add_fusion.place_ref.refs_0_.refs_13_, bf16[8,1,176,2048]{3,2,1,0:T(8,128)(2,1)} %bitcast.469, bf16[8,256,1408]{2,1,0:T(8,128)(2,1)} %get-tuple-element.204.refs_2_), custom_call_target="tpu_custom_call" | custom-call | flops 11811160064 | bytes 2883587 | tf_op jit(solution)/shard_map/pallas_call | solution.py:432
  745.8 8.5 fusion
  757.4 5.7 fusion.44
  763.1 5.7 fusion.41
  782.6 29.8 %shard_map.199 = (bf16[8,256,512]{2,1,0:T(8,128)(2,1)}, bf16[8,256,1024]{2,1,0:T(8,128)(2,1)}, f32[4,1,512]{2,1,0:T(1,128)}, bf16[2,256,2048]{2,1,0:T(8,128)(2,1)}, bf16[2,256,2048]{2,1,0:T(8,128)(2,1)}) custom-call(s32[3]{0:T(128)} %pad_add_fusion.place_ref.refs_0_.refs_13_, ...), custom_call_target="tpu_custom_call", output_to_operand_aliasing={{0}: (22, {}), {1}: (23, {})} | custom-call | flops 8589934592 | bytes 19532292 | tf_op jit(solution)/shard_map/pallas_call | solution.py:432
  812.5 9.4 fusion.35
  822.3 5.4 fusion.47
  833.9 36.2 %collective-permute-done.80 = bf16[1024,1024]{1,0:T(8,128)(2,1)} collective-permute-done((bf16[1024,1024]{1,0:T(8,128)(2,1)}, bf16[1024,1024]{1,0:T(8,128)(2,1)}, u32[]{:S(2)}, u32[]{:S(2)}) %collective-permute-start.80) | collective-permute-done | bytes 2097184 | tf_op jit(solution)/shard_map/ppermute | solution.py:28
  879.7 10.3 collective-permute-start.86
  895.0 9.7 collective-permute-start.84
  919.0 10.0 collective-permute-done.90
  940.2 7.0 collective-permute-start.92
  951.6 5.9 collective-permute-start.103
  972.1 6.4 collective-permute-done.95
  993.2 6.9 convert_bitcast_fusion
  1009.2 6.2 collective-permute-done.97
  (524 shorter events, 341.8 us)
Async XLA Ops:
  7.2 459.9 %all-gather.3.cloned.1.call-start = ((), (), s32[]{:S(2)}) async-start(), calls=%async_computation.4 | async-start | bytes 6488064 | tf_op jit(solution)/shard_map/all_gather | solution.py:520
  29.8 36.0 %collective-permute-start.8 = (bf16[4,64,2176]{2,1,0:T(8,128)(2,1)S(1)}, bf16[4,64,2176]{2,1,0:T(8,128)(2,1)}, u32[]{:S(2)}, u32[]{:S(2)}) collective-permute-start(bf16[4,64,2176]{2,1,0:T(8,128)(2,1)S(1)} %pad_maximum_fusion.3.refs_1_), channel_id=1, source_target_pairs={{0,16},{16,0},{1,17},{17,1},{2,18},{18,2},{3,19},{19,3},{4,20},{20... | collective-permute-start | bytes 3342344 | tf_op jit(solution)/shard_map/ppermute | solution.py:28
  33.1 32.1 %collective-permute-start.10 = (bf16[256,2048]{1,0:T(8,128)(2,1)}, bf16[256,2048]{1,0:T(8,128)(2,1)}, u32[]{:S(2)}, u32[]{:S(2)}) collective-permute-start(bf16[256,2048]{1,0:T(8,128)(2,1)} %get-tuple-element.153.refs_9_), channel_id=1, source_target_pairs={{0,8},{4,12},{8,0},{12,4},{1,9},{5,13},{9,1},{13,5},{2,10},{6,14},... | collective-permute-start | bytes 3145736 | tf_op jit(solution)/shard_map/ppermute | solution.py:25
  34.5 50.0 %collective-permute-start.7 = (bf16[4,64,2176]{2,1,0:T(8,128)(2,1)S(1)}, bf16[4,64,2176]{2,1,0:T(8,128)(2,1)}, u32[]{:S(2)}, u32[]{:S(2)}) collective-permute-start(bf16[4,64,2176]{2,1,0:T(8,128)(2,1)S(1)} %pad_maximum_fusion.3.refs_1_), channel_id=1, source_target_pairs={{0,1},{1,0},{2,3},{3,2},{4,5},{5,4},{6,7},{7,6},{8,9},{9,8},{10,11... | collective-permute-start | bytes 3342344 | tf_op jit(solution)/shard_map/ppermute | solution.py:31
  36.1 50.8 %collective-permute-start.6 = (bf16[4,64,2176]{2,1,0:T(8,128)(2,1)S(1)}, bf16[4,64,2176]{2,1,0:T(8,128)(2,1)}, u32[]{:S(2)}, u32[]{:S(2)}) collective-permute-start(bf16[4,64,2176]{2,1,0:T(8,128)(2,1)S(1)} %pad_maximum_fusion.3.refs_1_), channel_id=1, source_target_pairs={{0,2},{1,3},{2,0},{3,1},{4,6},{5,7},{6,4},{7,5},{8,10},{9,11},{10,... | collective-permute-start | bytes 3342344 | tf_op jit(solution)/shard_map/ppermute | solution.py:31
  93.0 32.9 %collective-permute-start.11 = (bf16[4,64,2176]{2,1,0:T(8,128)(2,1)}, bf16[4,64,2176]{2,1,0:T(8,128)(2,1)}, u32[]{:S(2)}, u32[]{:S(2)}) collective-permute-start(bf16[4,64,2176]{2,1,0:T(8,128)(2,1)} %collective-permute-done.6.refs_3_), channel_id=1, source_target_pairs={{0,1},{1,0},{2,3},{3,2},{4,5},{5,4},{6,7},{7,6},{8,9},{9,8},{10,11... | collective-permute-start | bytes 3342344 | tf_op jit(solution)/shard_map/ppermute | solution.py:31
  99.9 40.9 %collective-permute-start.12 = (bf16[4,64,2176]{2,1,0:T(8,128)(2,1)}, bf16[4,64,2176]{2,1,0:T(8,128)(2,1)}, u32[]{:S(2)}, u32[]{:S(2)}) collective-permute-start(bf16[4,64,2176]{2,1,0:T(8,128)(2,1)} %collective-permute-done.7.refs_2_), channel_id=1, source_target_pairs={{0,16},{16,0},{1,17},{17,1},{2,18},{18,2},{3,19},{19,3},{4,20},{20... | collective-permute-start | bytes 3342344 | tf_op jit(solution)/shard_map/ppermute | solution.py:28
  104.0 37.8 %collective-permute-start.53 = (bf16[256,2048]{1,0:T(8,128)(2,1)}, bf16[256,2048]{1,0:T(8,128)(2,1)}, u32[]{:S(2)}, u32[]{:S(2)}) collective-permute-start(bf16[256,2048]{1,0:T(8,128)(2,1)} %get-tuple-element.184), channel_id=1, source_target_pairs={{0,4},{4,0},{8,12},{12,8},{1,5},{5,1},{9,13},{13,9},{2,6},{6,2},{1... | collective-permute-start | bytes 3145736 | tf_op jit(solution)/shard_map/ppermute | solution.py:25
  120.3 59.4 %collective-permute-start.22 = (bf16[256,2048]{1,0:T(8,128)(2,1)}, bf16[256,2048]{1,0:T(8,128)(2,1)}, u32[]{:S(2)}, u32[]{:S(2)}) collective-permute-start(bf16[256,2048]{1,0:T(8,128)(2,1)} %get-tuple-element.153.refs_9_), channel_id=1, source_target_pairs={{0,4},{4,0},{8,12},{12,8},{1,5},{5,1},{9,13},{13,9},{2,6},{6,2},{1... | collective-permute-start | bytes 3145736 | tf_op jit(solution)/shard_map/ppermute | solution.py:25
  141.4 36.6 %collective-permute-start.20 = (bf16[4,64,2816]{2,1,0:T(8,128)(2,1)}, bf16[4,64,2816]{2,1,0:T(8,128)(2,1)}, u32[]{:S(2)}, u32[]{:S(2)}) collective-permute-start(bf16[4,64,2816]{2,1,0:T(8,128)(2,1)} %pad_maximum_fusion.2.refs_1_.refs_2_), channel_id=1, source_target_pairs={{0,1},{1,0},{2,3},{3,2},{4,5},{5,4},{6,7},{7,6},{8,9},{9,8},{10,11... | collective-permute-start | bytes 4325384 | tf_op jit(solution)/shard_map/ppermute | solution.py:31
  141.9 37.8 %collective-permute-start.23 = (bf16[256,2048]{1,0:T(8,128)(2,1)}, bf16[256,2048]{1,0:T(8,128)(2,1)}, u32[]{:S(2)}, u32[]{:S(2)}) collective-permute-start(bf16[256,2048]{1,0:T(8,128)(2,1)} %collective-permute-done.10.refs_11_), channel_id=1, source_target_pairs={{0,4},{4,0},{8,12},{12,8},{1,5},{5,1},{9,13},{13,9},{2,6},{6,2},{1... | collective-permute-start | bytes 3145736 | tf_op jit(solution)/shard_map/ppermute | solution.py:25
  169.2 70.9 %collective-permute-start.30 = (bf16[256,2048]{1,0:T(8,128)(2,1)}, bf16[256,2048]{1,0:T(8,128)(2,1)}, u32[]{:S(2)}, u32[]{:S(2)}) collective-permute-start(bf16[256,2048]{1,0:T(8,128)(2,1)} %get-tuple-element.156.refs_9_), channel_id=1, source_target_pairs={{0,4},{4,0},{8,12},{12,8},{1,5},{5,1},{9,13},{13,9},{2,6},{6,2},{1... | collective-permute-start | bytes 3145736 | tf_op jit(solution)/shard_map/ppermute | solution.py:25
  178.0 60.5 %collective-permute-start.17 = (bf16[4,64,2816]{2,1,0:T(8,128)(2,1)}, bf16[4,64,2816]{2,1,0:T(8,128)(2,1)}, u32[]{:S(2)}, u32[]{:S(2)}) collective-permute-start(bf16[4,64,2816]{2,1,0:T(8,128)(2,1)} %pad_maximum_fusion.2.refs_1_.refs_2_), channel_id=1, source_target_pairs={{0,2},{1,3},{2,0},{3,1},{4,6},{5,7},{6,4},{7,5},{8,10},{9,11},{10,... | collective-permute-start | bytes 4325384 | tf_op jit(solution)/shard_map/ppermute | solution.py:31
  179.6 29.3 %collective-permute-start.54 = (bf16[256,2048]{1,0:T(8,128)(2,1)}, bf16[256,2048]{1,0:T(8,128)(2,1)}, u32[]{:S(2)}, u32[]{:S(2)}) collective-permute-start(bf16[256,2048]{1,0:T(8,128)(2,1)} %collective-permute-done.41), channel_id=1, source_target_pairs={{0,4},{4,0},{8,12},{12,8},{1,5},{5,1},{9,13},{13,9},{2,6},{6,2},{1... | collective-permute-start | bytes 3145736 | tf_op jit(solution)/shard_map/ppermute | solution.py:25
  179.6 60.4 %collective-permute-start.26 = (bf16[4,64,2816]{2,1,0:T(8,128)(2,1)}, bf16[4,64,2816]{2,1,0:T(8,128)(2,1)}, u32[]{:S(2)}, u32[]{:S(2)}) collective-permute-start(bf16[4,64,2816]{2,1,0:T(8,128)(2,1)} %pad_maximum_fusion.2.refs_1_.refs_2_), channel_id=1, source_target_pairs={{0,16},{16,0},{1,17},{17,1},{2,18},{18,2},{3,19},{19,3},{4,20},{20... | collective-permute-start | bytes 4325384 | tf_op jit(solution)/shard_map/ppermute | solution.py:28
  206.4 34.3 %collective-permute-start.31 = (bf16[256,2048]{1,0:T(8,128)(2,1)}, bf16[256,2048]{1,0:T(8,128)(2,1)}, u32[]{:S(2)}, u32[]{:S(2)}) collective-permute-start(bf16[256,2048]{1,0:T(8,128)(2,1)} %copy-done.59), channel_id=1, source_target_pairs={{0,4},{4,0},{8,12},{12,8},{1,5},{5,1},{9,13},{13,9},{2,6},{6,2},{1... | collective-permute-start | bytes 3145736 | tf_op jit(solution)/shard_map/ppermute | solution.py:25
  228.2 40.7 %collective-permute-start.32 = (bf16[4,4,128,128]{3,2,1,0:T(8,128)(2,1)}, bf16[4,4,128,128]{3,2,1,0:T(8,128)(2,1)S(1)}, u32[]{:S(2)}, u32[]{:S(2)}) collective-permute-start(bf16[4,4,128,128]{3,2,1,0:T(8,128)(2,1)} %add_convert_fusion.25), channel_id=1, source_target_pairs={{0,1},{4,5},{8,9},{12,13},{16,17},{20,21},{24,25},{28,29}} | collective-permute-start | bytes 1572872 | tf_op jit(solution)/shard_map/ppermute | solution.py:559
  238.5 46.8 %collective-permute-start.38 = (bf16[4,64,2816]{2,1,0:T(8,128)(2,1)}, bf16[4,64,2816]{2,1,0:T(8,128)(2,1)}, u32[]{:S(2)}, u32[]{:S(2)}) collective-permute-start(bf16[4,64,2816]{2,1,0:T(8,128)(2,1)} %collective-permute-done.20.refs_2_.refs_3_), channel_id=1, source_target_pairs={{0,16},{16,0},{1,17},{17,1},{2,18},{18,2},{3,19},{19,3},{4,20},{20... | collective-permute-start | bytes 4325384 | tf_op jit(solution)/shard_map/ppermute | solution.py:28
  240.1 33.1 %collective-permute-start.33 = (bf16[4,64,2816]{2,1,0:T(8,128)(2,1)}, bf16[4,64,2816]{2,1,0:T(8,128)(2,1)}, u32[]{:S(2)}, u32[]{:S(2)}) collective-permute-start(bf16[4,64,2816]{2,1,0:T(8,128)(2,1)} %collective-permute-done.17.refs_3_.refs_4_), channel_id=1, source_target_pairs={{0,1},{1,0},{2,3},{3,2},{4,5},{5,4},{6,7},{7,6},{8,9},{9,8},{10,11... | collective-permute-start | bytes 4325384 | tf_op jit(solution)/shard_map/ppermute | solution.py:31
  240.1 62.6 %collective-permute-start.18 = (bf16[4,64,2816]{2,1,0:T(8,128)(2,1)}, bf16[4,64,2816]{2,1,0:T(8,128)(2,1)}, u32[]{:S(2)}, u32[]{:S(2)}) collective-permute-start(bf16[4,64,2816]{2,1,0:T(8,128)(2,1)} %collective-permute-done.17.refs_3_.refs_4_), channel_id=1, source_target_pairs={{0,16},{16,0},{1,17},{17,1},{2,18},{18,2},{3,19},{19,3},{4,20},{20... | collective-permute-start | bytes 4325384 | tf_op jit(solution)/shard_map/ppermute | solution.py:28
  240.6 44.7 %collective-permute-start.42 = (bf16[256,2048]{1,0:T(8,128)(2,1)}, bf16[256,2048]{1,0:T(8,128)(2,1)}, u32[]{:S(2)}, u32[]{:S(2)}) collective-permute-start(bf16[256,2048]{1,0:T(8,128)(2,1)} %get-tuple-element.185), channel_id=1, source_target_pairs={{0,8},{4,12},{8,0},{12,4},{1,9},{5,13},{9,1},{13,5},{2,10},{6,14},... | collective-permute-start | bytes 3145736 | tf_op jit(solution)/shard_map/ppermute | solution.py:25
  322.1 333.6 %reduce-scatter.3.cloned.1.call-start = ((), (), s32[]{:S(2)}) async-start(), calls=%async_computation.2 | async-start | bytes 6488064 | tf_op jit(solution)/shard_map/reduce_scatter | solution.py:624
  339.0 43.2 %collective-permute-start.39 = (bf16[4,64,2816]{2,1,0:T(8,128)(2,1)}, bf16[4,64,2816]{2,1,0:T(8,128)(2,1)}, u32[]{:S(2)}, u32[]{:S(2)}) collective-permute-start(bf16[4,64,2816]{2,1,0:T(8,128)(2,1)} %collective-permute-done.33.refs_4_.refs_5_), channel_id=1, source_target_pairs={{0,16},{16,0},{1,17},{17,1},{2,18},{18,2},{3,19},{19,3},{4,20},{20... | collective-permute-start | bytes 4325384 | tf_op jit(solution)/shard_map/ppermute | solution.py:28
  342.4 43.6 %collective-permute-start.46 = (bf16[1,256,2048]{2,1,0:T(8,128)(2,1)}, bf16[1,256,2048]{2,1,0:T(8,128)(2,1)S(1)}, u32[]{:S(2)}, u32[]{:S(2)}) collective-permute-start(bf16[1,256,2048]{2,1,0:T(8,128)(2,1)} %fusion.59), channel_id=1, source_target_pairs={{0,8},{4,12},{8,0},{12,4},{1,9},{5,13},{9,1},{13,5},{2,10},{6,14},... | collective-permute-start | bytes 3145736 | tf_op jit(solution)/shard_map/ppermute | solution.py:25
  382.2 55.1 %collective-permute-start.55 = (bf16[256,2048]{1,0:T(8,128)(2,1)}, bf16[256,2048]{1,0:T(8,128)(2,1)}, u32[]{:S(2)}, u32[]{:S(2)}) collective-permute-start(bf16[256,2048]{1,0:T(8,128)(2,1)} %get-tuple-element.185), channel_id=1, source_target_pairs={{0,4},{4,0},{8,12},{12,8},{1,5},{5,1},{9,13},{13,9},{2,6},{6,2},{1... | collective-permute-start | bytes 3145736 | tf_op jit(solution)/shard_map/ppermute | solution.py:25
  382.2 59.8 %collective-permute-start.56 = (bf16[256,2048]{1,0:T(8,128)(2,1)}, bf16[256,2048]{1,0:T(8,128)(2,1)}, u32[]{:S(2)}, u32[]{:S(2)}) collective-permute-start(bf16[256,2048]{1,0:T(8,128)(2,1)} %collective-permute-done.42), channel_id=1, source_target_pairs={{0,4},{4,0},{8,12},{12,8},{1,5},{5,1},{9,13},{13,9},{2,6},{6,2},{1... | collective-permute-start | bytes 3145736 | tf_op jit(solution)/shard_map/ppermute | solution.py:25
  382.7 30.4 %collective-permute-start.49 = (bf16[256,2048]{1,0:T(8,128)(2,1)}, bf16[256,2048]{1,0:T(8,128)(2,1)}, u32[]{:S(2)}, u32[]{:S(2)}) collective-permute-start(bf16[256,2048]{1,0:T(8,128)(2,1)} %multiply_multiply_fusion.refs_9_), channel_id=1, source_target_pairs={{0,4},{4,0},{8,12},{12,8},{1,5},{5,1},{9,13},{13,9},{2,6},{6,2},{1... | collective-permute-start | bytes 3145736 | tf_op jit(solution)/shard_map/ppermute | solution.py:25
  413.2 31.1 %collective-permute-start.47 = (bf16[256,2048]{1,0:T(8,128)(2,1)S(1)}, bf16[256,2048]{1,0:T(8,128)(2,1)}, u32[]{:S(2)}, u32[]{:S(2)}) collective-permute-start(bf16[256,2048]{1,0:T(8,128)(2,1)S(1)} %multiply_convert_fusion.refs_9_), channel_id=1, source_target_pairs={{0,4},{4,0},{8,12},{12,8},{1,5},{5,1},{9,13},{13,9},{2,6},{6,2},{1... | collective-permute-start | bytes 3145736 | tf_op jit(solution)/shard_map/ppermute | solution.py:25
  518.0 439.5 %reduce-scatter.5.cloned.1.call-start = ((), (), s32[]{:S(2)}) async-start(), calls=%async_computation.3 | async-start | bytes 7208960 | tf_op jit(solution)/shard_map/reduce_scatter | solution.py:758
  521.0 34.4 %collective-permute-start.58 = (bf16[1,256,2048]{2,1,0:T(8,128)(2,1)}, bf16[1,256,2048]{2,1,0:T(8,128)(2,1)S(1)}, u32[]{:S(2)}, u32[]{:S(2)}) collective-permute-start(bf16[1,256,2048]{2,1,0:T(8,128)(2,1)} %fusion.60), channel_id=1, source_target_pairs={{0,8},{4,12},{8,0},{12,4},{1,9},{5,13},{9,1},{13,5},{2,10},{6,14},... | collective-permute-start | bytes 3145736 | tf_op jit(solution)/shard_map/ppermute | solution.py:25
  563.8 30.9 %collective-permute-start.60 = (bf16[256,2048]{1,0:T(8,128)(2,1)}, bf16[256,2048]{1,0:T(8,128)(2,1)}, u32[]{:S(2)}, u32[]{:S(2)}) collective-permute-start(bf16[256,2048]{1,0:T(8,128)(2,1)} %add_convert_fusion.7.refs_9_), channel_id=1, source_target_pairs={{0,4},{4,0},{8,12},{12,8},{1,5},{5,1},{9,13},{13,9},{2,6},{6,2},{1... | collective-permute-start | bytes 3145736 | tf_op jit(solution)/shard_map/ppermute | solution.py:25
  592.9 152.9 %collective-permute-start.93 = (bf16[1024,2816]{1,0:T(8,128)(2,1)}, bf16[1024,2816]{1,0:T(8,128)(2,1)}, u32[]{:S(2)}, u32[]{:S(2)}) collective-permute-start(bf16[1024,2816]{1,0:T(8,128)(2,1)} %convolution_convert_fusion.2), channel_id=1, source_target_pairs={{0,16},{16,0},{1,17},{17,1},{2,18},{18,2},{3,19},{19,3},{4,20},{20... | collective-permute-start | bytes 17301512 | tf_op jit(solution)/shard_map/ppermute | solution.py:28
  608.3 33.9 %collective-permute-start.63 = (bf16[4,4,128,128]{3,2,1,0:T(8,128)(2,1)S(1)}, bf16[4,4,128,128]{3,2,1,0:T(8,128)(2,1)S(1)}, u32[]{:S(2)}, u32[]{:S(2)}) collective-permute-start(bf16[4,4,128,128]{3,2,1,0:T(8,128)(2,1)S(1)} %add_convert_fusion.19), channel_id=1, source_target_pairs={{3,2},{7,6},{11,10},{15,14},{19,18},{23,22},{27,26},{31,30}} | collective-permute-start | bytes 1572872 | tf_op jit(solution)/shard_map/ppermute | solution.py:559
  683.1 32.3 %collective-permute-start.72 = (bf16[4,4,128,128]{3,2,1,0:T(8,128)(2,1)}, bf16[4,4,128,128]{3,2,1,0:T(8,128)(2,1)}, u32[]{:S(2)}, u32[]{:S(2)}) collective-permute-start(bf16[4,4,128,128]{3,2,1,0:T(8,128)(2,1)} %fusion.57), channel_id=1, source_target_pairs={{2,1},{6,5},{10,9},{14,13},{18,17},{22,21},{26,25},{30,29}} | collective-permute-start | bytes 1572872 | tf_op jit(solution)/shard_map/ppermute | solution.py:559
  714.9 39.4 %collective-permute-start.73 = (bf16[1,2,256,2048]{3,2,1,0:T(8,128)(2,1)}, bf16[1,2,256,2048]{3,2,1,0:T(8,128)(2,1)}, u32[]{:S(2)}, u32[]{:S(2)}) collective-permute-start(bf16[1,2,256,2048]{3,2,1,0:T(8,128)(2,1)} %bitcast.470), channel_id=1, source_target_pairs={{0,4},{4,0},{8,12},{12,8},{1,5},{5,1},{9,13},{13,9},{2,6},{6,2},{1... | collective-permute-start | bytes 6291464 | tf_op jit(solution)/shard_map/ppermute | solution.py:25
  743.4 33.5 %collective-permute-start.71 = (bf16[4,256,2048]{2,1,0:T(8,128)(2,1)}, bf16[4,256,2048]{2,1,0:T(8,128)(2,1)}, u32[]{:S(2)}, u32[]{:S(2)}) collective-permute-start(bf16[4,256,2048]{2,1,0:T(8,128)(2,1)} %get-tuple-element.236), channel_id=1, source_target_pairs={{0,4},{4,0},{8,12},{12,8},{1,5},{5,1},{9,13},{13,9},{2,6},{6,2},{1... | collective-permute-start | bytes 12582920 | tf_op jit(solution)/shard_map/ppermute | solution.py:25
  768.8 53.1 %collective-permute-start.76 = (bf16[1,256,2048]{2,1,0:T(8,128)(2,1)}, bf16[1,256,2048]{2,1,0:T(8,128)(2,1)}, u32[]{:S(2)}, u32[]{:S(2)}) collective-permute-start(bf16[1,256,2048]{2,1,0:T(8,128)(2,1)} %fusion.62), channel_id=1, source_target_pairs={{0,8},{4,12},{8,0},{12,4},{1,9},{5,13},{9,1},{13,5},{2,10},{6,14},... | collective-permute-start | bytes 3145736 | tf_op jit(solution)/shard_map/ppermute | solution.py:25
  769.3 108.6 %collective-permute-start.82 = (bf16[1024,512]{1,0:T(8,128)(2,1)}, bf16[1024,512]{1,0:T(8,128)(2,1)}, u32[]{:S(2)}, u32[]{:S(2)}) collective-permute-start(bf16[1024,512]{1,0:T(8,128)(2,1)} %fusion.41), channel_id=1, source_target_pairs={{0,16},{16,0},{1,17},{17,1},{2,18},{18,2},{3,19},{19,3},{4,20},{20... | collective-permute-start | bytes 3145736 | tf_op jit(solution)/shard_map/ppermute | solution.py:28
  780.6 128.4 %collective-permute-start.74 = (bf16[256,2048]{1,0:T(8,128)(2,1)}, bf16[256,2048]{1,0:T(8,128)(2,1)}, u32[]{:S(2)}, u32[]{:S(2)}) collective-permute-start(bf16[256,2048]{1,0:T(8,128)(2,1)} %get-tuple-element.294), channel_id=1, source_target_pairs={{0,8},{4,12},{8,0},{12,4},{1,9},{5,13},{9,1},{13,5},{2,10},{6,14},... | collective-permute-start | bytes 3145736 | tf_op jit(solution)/shard_map/ppermute | solution.py:25
  782.1 127.4 %collective-permute-start.75 = (bf16[256,2048]{1,0:T(8,128)(2,1)}, bf16[256,2048]{1,0:T(8,128)(2,1)}, u32[]{:S(2)}, u32[]{:S(2)}) collective-permute-start(bf16[256,2048]{1,0:T(8,128)(2,1)} %get-tuple-element.295), channel_id=1, source_target_pairs={{0,8},{4,12},{8,0},{12,4},{1,9},{5,13},{9,1},{13,5},{2,10},{6,14},... | collective-permute-start | bytes 3145736 | tf_op jit(solution)/shard_map/ppermute | solution.py:25
  821.9 48.3 %collective-permute-start.80 = (bf16[1024,1024]{1,0:T(8,128)(2,1)}, bf16[1024,1024]{1,0:T(8,128)(2,1)}, u32[]{:S(2)}, u32[]{:S(2)}) collective-permute-start(bf16[1024,1024]{1,0:T(8,128)(2,1)} %fusion.35), channel_id=1, source_target_pairs={{0,16},{16,0},{1,17},{17,1},{2,18},{18,2},{3,19},{19,3},{4,20},{20... | collective-permute-start | bytes 6291464 | tf_op jit(solution)/shard_map/ppermute | solution.py:28
  832.4 72.3 %collective-permute-start.79 = (bf16[1,256,2048]{2,1,0:T(8,128)(2,1)S(1)}, bf16[1,256,2048]{2,1,0:T(8,128)(2,1)S(1)}, u32[]{:S(2)}, u32[]{:S(2)}) collective-permute-start(bf16[1,256,2048]{2,1,0:T(8,128)(2,1)S(1)} %fusion.65), channel_id=1, source_target_pairs={{0,8},{4,12},{8,0},{12,4},{1,9},{5,13},{9,1},{13,5},{2,10},{6,14},... | collective-permute-start | bytes 3145736 | tf_op jit(solution)/shard_map/ppermute | solution.py:25
  879.7 36.3 %collective-permute-start.86 = (bf16[4,2,64,512]{3,2,1,0:T(8,128)(2,1)S(1)}, bf16[4,2,64,512]{3,2,1,0:T(8,128)(2,1)S(1)}, u32[]{:S(2)}, u32[]{:S(2)}) collective-permute-start(bf16[4,2,64,512]{3,2,1,0:T(8,128)(2,1)S(1)} %fusion.72), channel_id=1, source_target_pairs={{0,1},{1,0},{2,3},{3,2},{4,5},{5,4},{6,7},{7,6},{8,9},{9,8},{10,11... | collective-permute-start | bytes 1572872 | tf_op jit(solution)/shard_map/ppermute | solution.py:31
  895.0 52.3 %collective-permute-start.84 = (bf16[4,2,64,1024]{3,2,1,0:T(8,128)(2,1)S(1)}, bf16[4,2,64,1024]{3,2,1,0:T(8,128)(2,1)S(1)}, u32[]{:S(2)}, u32[]{:S(2)}) collective-permute-start(bf16[4,2,64,1024]{3,2,1,0:T(8,128)(2,1)S(1)} %fusion.66), channel_id=1, source_target_pairs={{0,1},{1,0},{2,3},{3,2},{4,5},{5,4},{6,7},{7,6},{8,9},{9,8},{10,11... | collective-permute-start | bytes 3145736 | tf_op jit(solution)/shard_map/ppermute | solution.py:31
  915.9 33.8 %collective-permute-start.83 = (bf16[4,2,64,512]{3,2,1,0:T(8,128)(2,1)S(1)}, bf16[4,2,64,512]{3,2,1,0:T(8,128)(2,1)S(1)}, u32[]{:S(2)}, u32[]{:S(2)}) collective-permute-start(bf16[4,2,64,512]{3,2,1,0:T(8,128)(2,1)S(1)} %fusion.73), channel_id=1, source_target_pairs={{0,1},{1,0},{2,3},{3,2},{4,5},{5,4},{6,7},{7,6},{8,9},{9,8},{10,11... | collective-permute-start | bytes 1572872 | tf_op jit(solution)/shard_map/ppermute | solution.py:31
  966.6 42.6 %collective-permute-start.98 = (bf16[4,1,64,512]{3,2,1,0:T(8,128)(2,1)}, bf16[4,1,64,512]{3,2,1,0:T(8,128)(2,1)}, u32[]{:S(2)}, u32[]{:S(2)}) collective-permute-start(bf16[4,1,64,512]{3,2,1,0:T(8,128)(2,1)} %bitcast.123), channel_id=1, source_target_pairs={{0,2},{1,3},{2,0},{3,1},{4,6},{5,7},{6,4},{7,5},{8,10},{9,11},{10,... | collective-permute-start | bytes 786440 | tf_op jit(solution)/shard_map/ppermute | solution.py:31
  968.6 49.9 %collective-permute-start.87 = (bf16[4,1,64,512]{3,2,1,0:T(8,128)(2,1)}, bf16[4,1,64,512]{3,2,1,0:T(8,128)(2,1)}, u32[]{:S(2)}, u32[]{:S(2)}) collective-permute-start(bf16[4,1,64,512]{3,2,1,0:T(8,128)(2,1)} %bitcast.102), channel_id=1, source_target_pairs={{0,2},{1,3},{2,0},{3,1},{4,6},{5,7},{6,4},{7,5},{8,10},{9,11},{10,... | collective-permute-start | bytes 786440 | tf_op jit(solution)/shard_map/ppermute | solution.py:31
  971.9 43.4 %collective-permute-start.97 = (bf16[4,1,64,1024]{3,2,1,0:T(8,128)(2,1)}, bf16[4,1,64,1024]{3,2,1,0:T(8,128)(2,1)}, u32[]{:S(2)}, u32[]{:S(2)}) collective-permute-start(bf16[4,1,64,1024]{3,2,1,0:T(8,128)(2,1)} %bitcast.444), channel_id=1, source_target_pairs={{0,2},{1,3},{2,0},{3,1},{4,6},{5,7},{6,4},{7,5},{8,10},{9,11},{10,... | collective-permute-start | bytes 1572872 | tf_op jit(solution)/shard_map/ppermute | solution.py:31
  (154 other events, 2505.4 us)
Sparse Core Ops, SparseCore 0:
  322.2 100.8 all-gather.2
  518.1 114.6 reduce-scatter.2
  754.4 113.3 reduce-scatter.4

commit v4 on v3

--- a/solution.py
+++ b/solution.py
@@ -191,6 +191,18 @@
         for k in range(ref.shape[1] // strip):
             at = pl.multiple_of((k * TEAM + (place_ref[0] ^ j)) * strip, strip)
             out_ref[:, pl.ds(at, strip)] = ref[:, k * strip : (k + 1) * strip].astype(F32)
+
+
+def place_cases_kernel(strip, place_ref, *refs):
+    out_ref = refs[-1]
+    for rank in range(TEAM):
+
+        @pl.when(place_ref[0] == rank)
+        def _(rank=rank):
+            for j, ref in enumerate(refs[:-1]):
+                for k in range(ref.shape[1] // strip):
+                    at = (k * TEAM + (rank ^ j)) * strip
+                    out_ref[:, at : at + strip] = ref[:, k * strip : (k + 1) * strip].astype(F32)
 
 
 def mix_kernel(strip, step, fetch, piece_refs, place_ref, row_ref, col_ref, *refs):
@@ -670,11 +682,15 @@
                 terms = self.terms[:-1] + [after(self.terms[-1], *held)]
                 return lambda i: sum(lax.dynamic_index_in_dim(t[:, 0], i, 0, False).astype(F32) for t in terms)
 
-        def out_of_team(summed, count, *held):
-            got = at.by_rank(trade([summed(at.rank ^ j).astype(BF16) for j in range(TEAM)], *held)).astype(F32)
-            width = got.shape[2] // (count * ny)
-            got = got.reshape(TEAM, rows, count, ny, width)
-            return jnp.transpose(got, (1, 2, 3, 0, 4)).reshape(rows, -1)
+        def out_of_team(parts, kernel):
+            parts = [parts[0]] + [at.swap(parts[j], j) for j in range(1, TEAM)]
+            return pl.pallas_call(
+                kernel,
+                in_specs=[pl.BlockSpec(memory_space=pltpu.SMEM)] + [pl.BlockSpec(memory_space=pltpu.VMEM)] * TEAM,
+                out_specs=pl.BlockSpec(memory_space=pltpu.VMEM),
+                out_shape=jax.ShapeDtypeStruct((rows, TEAM * parts[0].shape[1]), F32),
+                compiler_params=pltpu.CompilerParams(vmem_limit_bytes=VMEM_LIMIT),
+            )(place, *parts)
 
         both = whole_branch = None
         all_cot = jnp.concatenate([jnp.stack(pieces) for pieces in cotangent])
@@ -834,17 +850,14 @@
         group_all = jnp.sum(sum(jnp.sum(a, axis=(0, 1)) for a in group_sums).reshape(heads, HEAD), axis=0)
         sums = at.everyone_sum(after(jnp.concatenate([attn_sum, sum(gain_sums), logit_all, group_all]), q_sent))
 
-        grad_gu = out_of_team(gu_final, 2)
+        grad_gu = out_of_team(
+            [gu_final(at.rank ^ j).astype(BF16) for j in range(TEAM)], partial(place_cases_kernel, ff_strip)
+        )
         parts = [part.finish(sums, grad_gu) for part in (q_part, fv_part, o_part)]
-        parts = [
-            jnp.concatenate([part(at.rank ^ j) for part in parts], axis=1).astype(BF16) for j in range(TEAM)
-        ]
-        grad_mix = pl.pallas_call(
+        grad_mix = out_of_team(
+            [jnp.concatenate([part(at.rank ^ j) for part in parts], axis=1).astype(BF16) for j in range(TEAM)],
             partial(place_kernel, strip),
-            in_specs=[pl.BlockSpec(memory_space=pltpu.SMEM)] + [pl.BlockSpec(memory_space=pltpu.VMEM)] * TEAM,
-            out_specs=pl.BlockSpec(memory_space=pltpu.VMEM),
-            out_shape=jax.ShapeDtypeStruct((rows, TEAM * 4 * own_channels), F32),
-        )(place, parts[0], *(at.swap(parts[j], j) for j in range(1, TEAM)))
+        )
         grad_out = out_part.finish(sums)(0)
         here = (at.y * TEAM + at.rank) * nz + at.z
 

time: 1050 us -> 1040 us (level)
  local copies, waits for them, and re-layouts: 86.3 us -> 65.4 us
  waiting for transfers between devices: 295 us -> 311 us
    ppermute x19, waiting for transfers between devices: 58.6 us -> 87 us  [swap_z(): return lax.ppermute(value, 'seq', [(i, i ^ bits) for i in range(self.nz)])]
    concatenate x6 -> x0, local copies, waits for them, and re-layouts: 12 us -> none  [the longest x4 6.16 us: by_rank(): jnp.concatenate([stack[1:2], stack[0:1], stack[3:4], stack[2:3]])]
    unnamed x198 -> x204, local copies, waits for them, and re-layouts: 20.9 us -> 22.5 us
  transfers between devices with their start and end apart: 107 -> 107, of which waited for: 34 -> 36; matrix products, arithmetic and copies ran while one was open for 30% -> 27% of each run, Pallas kernels for 25% -> 25%
where the time goes in v4:
time: 1040 us; the launch traced here: 1030 us
  waiting for transfers between devices  311 us (30%)
  Pallas kernels  300 us (29%)
  other arithmetic  128 us (12%)
  starting transfers between devices  117 us (11%)
  matrix products  96.4 us (9%)
  local copies, waits for them, and re-layouts  65.4 us (6%)
  between operations  15.3 us (1%)
    pallas_call x13, Pallas kernels, over_sequences(): pl.pallas_call(body, grid=(count,), in_specs=specs, out_specs=[spec(shape...  291 us
    ppermute x55, waiting for transfers between devices, swap(): return lax.ppermute(value, 'team', [(i, i ^ bits) for i in range(TEAM)])  110 us
    ppermute x18, waiting for transfers between devices, swap_y(): return lax.ppermute(value, 'y', [(i, i ^ bits) for i in range(self.ny)])  104 us
    dot_general x11, matrix products, tn(): lax.dot_general(a, b, (((0,), (0,)), ((), ())), preferred_element_type=F32)  96.2 us
    ppermute x19, waiting for transfers between devices, swap_z(): return lax.ppermute(value, 'seq', [(i, i ^ bits) for i in range(self.nz)])  87 us
    ppermute x19, starting transfers between devices, swap_z(): return lax.ppermute(value, 'seq', [(i, i ^ bits) for i in range(self.nz)])  53.5 us
    ppermute x55, starting transfers between devices, swap(): return lax.ppermute(value, 'team', [(i, i ^ bits) for i in range(TEAM)])  27.2 us
    unnamed x204, local copies, waits for them, and re-layouts  22.5 us
  transfers between devices with their start and end apart: 107, of which 36 were waited for; matrix products, arithmetic and copies ran while one was open for 27% of the time, Pallas kernels for 25%

profile of v4, /device:TPU:0, one launch (start us, length us, event | category | flops | bytes accessed | tf_op | source)
XLA Modules:
  0.0 1032.5 jit_solution(11309124603673555685)
XLA Ops:
  15.6 7.6 collective-permute-done.1
  23.1 5.6 collective-permute-done.2
  44.3 14.6 %dynamic-slice_reduce_fusion.3 = (bf16[64,4,704]{2,1,0:T(4,128)(2,1)}, bf16[64,4,704]{2,1,0:T(4,128)(2,1)}, bf16[64,4,704]{2,1,0:T(4,128)(2,1)}, bf16[64,4,704]{2,1,0:T(4,128)(2,1)}) fusion(bf16[64,4,4,704]{3,2,1,0:T(4,128)(2,1)} %reshape.1143, s32[]{:T(128)S(6)} %select_n.213, s32[]{:T(128)S(6)} %select_n.215, s32[]{:T(128)S(6)} %select_n.214, ...), kind=kLoop, calls=%fused_computation.146 | loop fusion | bytes 2883600 | tf_op jit(solution)/shard_map/jit(dynamic_index_in_dim)/dynamic_slice | solution.py:483
  69.4 15.2 %collective-permute-done.7.refs_2_ = bf16[4,64,2176]{2,1,0:T(8,128)(2,1)} collective-permute-done((bf16[4,64,2176]{2,1,0:T(8,128)(2,1)S(1)}, bf16[4,64,2176]{2,1,0:T(8,128)(2,1)}, u32[]{:S(2)}, u32[]{:S(2)}) %collective-permute-start.7) | collective-permute-done | bytes 1114144 | tf_op jit(solution)/shard_map/ppermute | solution.py:31
  93.7 6.3 collective-permute-done.16.refs_3_
  104.1 11.6 %collective-permute-done.14.refs_11_ = bf16[256,2048]{1,0:T(8,128)(2,1)S(1)} collective-permute-done((bf16[256,2048]{1,0:T(8,128)(2,1)}, bf16[256,2048]{1,0:T(8,128)(2,1)S(1)}, u32[]{:S(2)}, u32[]{:S(2)}) %collective-permute-start.14) | collective-permute-done | bytes 1048608 | tf_op jit(solution)/shard_map/ppermute | solution.py:25
  120.4 5.7 collective-permute-done.11.refs_4_
  126.1 14.8 %collective-permute-done.12.refs_6_ = bf16[4,64,2176]{2,1,0:T(8,128)(2,1)} collective-permute-done((bf16[4,64,2176]{2,1,0:T(8,128)(2,1)}, bf16[4,64,2176]{2,1,0:T(8,128)(2,1)}, u32[]{:S(2)}, u32[]{:S(2)}) %collective-permute-start.12) | collective-permute-done | bytes 1114144 | tf_op jit(solution)/shard_map/ppermute | solution.py:28
  148.1 14.8 %collective-permute-done.41 = bf16[256,2048]{1,0:T(8,128)(2,1)} collective-permute-done((bf16[256,2048]{1,0:T(8,128)(2,1)}, bf16[256,2048]{1,0:T(8,128)(2,1)}, u32[]{:S(2)}, u32[]{:S(2)}) %collective-permute-start.41) | collective-permute-done | bytes 1048608 | tf_op jit(solution)/shard_map/ppermute | solution.py:25
  169.3 8.8 collective-permute-done.19.refs_4_
  181.8 23.8 %shard_map.187 = (bf16[8,256,2048]{2,1,0:T(8,128)(2,1)}, f32[8,256,2048]{2,1,0:T(8,128)}, f32[8,256,512]{2,1,0:T(8,128)}, bf16[8,256,512]{2,1,0:T(8,128)(2,1)}, ...) custom-call(s32[3]{0:T(128)} %pad_add_fusion.place_ref.refs_0_.refs_, ...), custom_call_target="tpu_custom_call" | custom-call | flops 8589934592 | bytes 3278854 | tf_op jit(solution)/shard_map/pallas_call | solution.py:444
  211.6 9.4 collective-permute-done.27.refs_6_
  223.2 5.1 collective-permute-done.29.refs_8_
  230.9 7.7 collective-permute-done.17.refs_3_.refs_4_
  242.2 24.2 %shard_map.188 = (bf16[8,256,2048]{2,1,0:T(8,128)(2,1)}, f32[8,256,2048]{2,1,0:T(8,128)}, f32[8,256,512]{2,1,0:T(8,128)}, bf16[8,256,512]{2,1,0:T(8,128)(2,1)}, ...) custom-call(s32[3]{0:T(128)} %pad_add_fusion.place_ref.refs_0_.refs_, ...), custom_call_target="tpu_custom_call", output_to_operand_aliasing={{0}: (16, {}), {1}: (17, {}), {2}: (18, {}), {3}: (19, {}),... | custom-call | flops 8589934592 | bytes 11667462 | tf_op jit(solution)/shard_map/pallas_call | solution.py:444
  274.0 9.5 collective-permute-done.40
  291.8 10.9 %collective-permute-done.18.refs_7_.refs_8_ = bf16[4,64,2816]{2,1,0:T(8,128)(2,1)} collective-permute-done((bf16[4,64,2816]{2,1,0:T(8,128)(2,1)}, bf16[4,64,2816]{2,1,0:T(8,128)(2,1)}, u32[]{:S(2)}, u32[]{:S(2)}) %collective-permute-start.18) | collective-permute-done | bytes 1441824 | tf_op jit(solution)/shard_map/ppermute | solution.py:28
  307.9 12.1 %shard_map.189 = (f32[8,256,512]{2,1,0:T(8,128)}, bf16[8,256,512]{2,1,0:T(8,128)(2,1)}, bf16[2,256,2048]{2,1,0:T(8,128)(2,1)}, bf16[2,256,2048]{2,1,0:T(8,128)(2,1)}) custom-call(s32[3]{0:T(128)} %pad_add_fusion.place_ref.refs_0_.refs_13_, bf16[1,64,2048]{2,1,0:T(8,128)(2,1)} %bitcast.397, bf16[1,64,2048]{2,1,0:T(8,128)(2,1)} %copy-done.40, ...), custom_call_target="tpu_custom_call" | custom-call | flops 2147483648 | bytes 5899395 | tf_op jit(solution)/shard_map/pallas_call | solution.py:444
  322.2 12.5 %shard_map.190 = (f32[8,256,512]{2,1,0:T(8,128)}, bf16[8,256,512]{2,1,0:T(8,128)(2,1)}, bf16[2,256,2048]{2,1,0:T(8,128)(2,1)}, bf16[2,256,2048]{2,1,0:T(8,128)(2,1)}) custom-call(s32[3]{0:T(128)} %pad_add_fusion.place_ref.refs_0_.refs_13_, bf16[1,64,2048]{2,1,0:T(8,128)(2,1)} %bitcast.398, ...), custom_call_target="tpu_custom_call", output_to_operand_aliasing={{0}: (15, {}), {1}: (16, {})} | custom-call | flops 2147483648 | bytes 7472259 | tf_op jit(solution)/shard_map/pallas_call | solution.py:444
  342.8 20.6 %collective-permute-done.37 = bf16[1,256,2048]{2,1,0:T(8,128)(2,1)S(1)} collective-permute-done((bf16[1,256,2048]{2,1,0:T(8,128)(2,1)S(1)}, bf16[1,256,2048]{2,1,0:T(8,128)(2,1)S(1)}, u32[]{:S(2)}, u32[]{:S(2)}) %collective-permute-start.37) | collective-permute-done | bytes 1048608 | tf_op jit(solution)/shard_map/ppermute | solution.py:25
  368.2 13.7 %collective-permute-done.39.refs_8_.refs_9_ = bf16[4,64,2816]{2,1,0:T(8,128)(2,1)} collective-permute-done((bf16[4,64,2816]{2,1,0:T(8,128)(2,1)}, bf16[4,64,2816]{2,1,0:T(8,128)(2,1)}, u32[]{:S(2)}, u32[]{:S(2)}) %collective-permute-start.39) | collective-permute-done | bytes 1441824 | tf_op jit(solution)/shard_map/ppermute | solution.py:28
  385.8 21.7 %collective-permute-done.50.refs_11_ = bf16[256,2048]{1,0:T(8,128)(2,1)} collective-permute-done((bf16[256,2048]{1,0:T(8,128)(2,1)}, bf16[256,2048]{1,0:T(8,128)(2,1)}, u32[]{:S(2)}, u32[]{:S(2)}) %collective-permute-start.50) | collective-permute-done | bytes 1048608 | tf_op jit(solution)/shard_map/ppermute | solution.py:25
  413.3 22.6 %shard_map.191 = (bf16[8,256,2048]{2,1,0:T(8,128)(2,1)}, bf16[8,256,1408]{2,1,0:T(8,128)(2,1)}, bf16[8,256,1408]{2,1,0:T(8,128)(2,1)}, bf16[8,256,1408]{2,1,0:T(8,128)(2,1)}) custom-call(s32[3]{0:T(128)} %pad_add_fusion.place_ref.refs_0_.refs_13_, bf16[4,64,2816]{2,1,0:T(8,128)(2,1)} %pad_maximum_fusion.2.refs_1_.refs_2_, ...), custom_call_target="tpu_custom_call" | custom-call | flops 11811160064 | bytes 3932163 | tf_op jit(solution)/shard_map/pallas_call | solution.py:444
  444.2 23.0 %shard_map.192 = (bf16[8,256,2048]{2,1,0:T(8,128)(2,1)}, bf16[8,256,1408]{2,1,0:T(8,128)(2,1)}, bf16[8,256,1408]{2,1,0:T(8,128)(2,1)}, bf16[8,256,1408]{2,1,0:T(8,128)(2,1)}) custom-call(s32[3]{0:T(128)} %pad_add_fusion.place_ref.refs_0_.refs_13_, ...), custom_call_target="tpu_custom_call", output_to_operand_aliasing={{0}: (13, {}), {1}: (14, {}), {2}: (15, {}), {3}: (16, {})} | custom-call | flops 11811160064 | bytes 10354691 | tf_op jit(solution)/shard_map/pallas_call | solution.py:444
  467.2 32.3 %shard_map.193 = (bf16[8,256,2816]{2,1,0:T(8,128)(2,1)}, bf16[2,256,2048]{2,1,0:T(8,128)(2,1)}, bf16[2,256,2048]{2,1,0:T(8,128)(2,1)}) custom-call(s32[3]{0:T(128)} %pad_add_fusion.place_ref.refs_0_.refs_13_, bf16[8,1,176,2048]{3,2,1,0:T(8,128)(2,1)} %bitcast.463, bf16[4,64,2816]{2,1,0:T(8,128)(2,1)} %pad_maximum_fusion.2.refs_1_.refs_2_, ...), custom_call_target="tpu_custom_call" | custom-call | flops 17716740096 | bytes 9306115 | tf_op jit(solution)/shard_map/pallas_call | solution.py:444
  500.1 18.1 %convolution_convert_fusion = bf16[1408,2048]{1,0:T(8,128)(2,1)} fusion(bf16[2048,1408]{1,0:T(8,128)(2,1)} %bitcast.476, bf16[2048,2048]{1,0:T(8,128)(2,1)} %bitcast.455), kind=kOutput, calls=%fused_computation.2 | convolution fusion | flops 11814043648 | bytes 19922944 | tf_op jit(solution)/shard_map/dot_general | solution.py:122
  522.7 32.9 %shard_map.194 = (bf16[8,256,2816]{2,1,0:T(8,128)(2,1)}, bf16[2,256,2048]{2,1,0:T(8,128)(2,1)}, bf16[2,256,2048]{2,1,0:T(8,128)(2,1)}) custom-call(s32[3]{0:T(128)} %pad_add_fusion.place_ref.refs_0_.refs_13_, bf16[8,1,176,2048]{3,2,1,0:T(8,128)(2,1)} %bitcast.464, ...), custom_call_target="tpu_custom_call", output_to_operand_aliasing={{0}: (13, {})} | custom-call | flops 17716740096 | bytes 12189699 | tf_op jit(solution)/shard_map/pallas_call | solution.py:444
  564.5 19.6 %convolution_convert_fusion.2 = bf16[1024,2816]{1,0:T(8,128)(2,1)} fusion(bf16[2048,2816]{1,0:T(8,128)(2,1)} %bitcast.472, bf16[2048,2048]{1,0:T(8,128)(2,1)} %bitcast.474, s32[]{:T(128)S(6)} %select_n.217), kind=kOutput, calls=%fused_computation.8 | convolution fusion | flops 11814043648 | bytes 21495812 | tf_op jit(solution)/shard_map/dot_general | solution.py:122
  594.9 11.8 %shard_map.195 = (bf16[8,256,2048]{2,1,0:T(8,128)(2,1)}, bf16[8,256,512]{2,1,0:T(8,128)(2,1)}, bf16[4,256,512]{2,1,0:T(8,128)(2,1)}, f32[4,4,128,128]{3,2,1,0:T(8,128)}, f32[4,1,512]{2,1,0:T(1,128)}) custom-call(s32[3]{0:T(128)} %pad_add_fusion.place_ref.refs_0_.refs_13_, bf16[1,64,2048]{2,1,0:T(8,128)(2,1)} %bitcast.399, bf16[1,64,2048]{2,1,0:T(8,128)(2,1)} %copy-done.40, ...), custom_call_target="tpu_custom_call" | custom-call | flops 2147483648 | bytes 7341187 | tf_op jit(solution)/shard_map/pallas_call | solution.py:444
  609.3 6.7 collective-permute-done.64
  623.1 19.2 %convolution_convert_fusion.1 = bf16[1024,2816]{1,0:T(8,128)(2,1)} fusion(bf16[2048,2816]{1,0:T(8,128)(2,1)} %bitcast.473, bf16[2048,2048]{1,0:T(8,128)(2,1)} %bitcast.475, s32[]{:T(128)S(6)} %select_n.218), kind=kOutput, calls=%fused_computation.7 | convolution fusion | flops 11814043648 | bytes 21495812 | tf_op jit(solution)/shard_map/dot_general | solution.py:122
  658.2 11.7 %shard_map.196 = (bf16[8,256,2048]{2,1,0:T(8,128)(2,1)}, bf16[8,256,512]{2,1,0:T(8,128)(2,1)}, bf16[4,256,512]{2,1,0:T(8,128)(2,1)}, f32[4,4,128,128]{3,2,1,0:T(8,128)}, f32[4,1,512]{2,1,0:T(1,128)}) custom-call(s32[3]{0:T(128)} %pad_add_fusion.place_ref.refs_0_.refs_13_, ...), custom_call_target="tpu_custom_call", output_to_operand_aliasing={{0}: (18, {}), {1}: (19, {})} | custom-call | flops 2147483648 | bytes 9962627 | tf_op jit(solution)/shard_map/pallas_call | solution.py:444
  684.9 29.3 %shard_map.197 = (bf16[8,256,512]{2,1,0:T(8,128)(2,1)}, bf16[8,256,1024]{2,1,0:T(8,128)(2,1)}, f32[4,1,512]{2,1,0:T(1,128)}, bf16[2,256,2048]{2,1,0:T(8,128)(2,1)}, bf16[2,256,2048]{2,1,0:T(8,128)(2,1)}) custom-call(s32[3]{0:T(128)} %pad_add_fusion.place_ref.refs_0_.refs_13_, bf16[4,64,2176]{2,1,0:T(8,128)(2,1)} %copy-done.15, ...), custom_call_target="tpu_custom_call" | custom-call | flops 8589934592 | bytes 17959428 | tf_op jit(solution)/shard_map/pallas_call | solution.py:444
  718.3 25.1 %shard_map.198 = (bf16[4,256,2048]{2,1,0:T(8,128)(2,1)}, bf16[4,256,2048]{2,1,0:T(8,128)(2,1)}) custom-call(s32[3]{0:T(128)} %pad_add_fusion.place_ref.refs_0_.refs_13_, bf16[8,1,176,2048]{3,2,1,0:T(8,128)(2,1)} %bitcast.465, bf16[8,256,1408]{2,1,0:T(8,128)(2,1)} %get-tuple-element.204.refs_2_), custom_call_target="tpu_custom_call" | custom-call | flops 11811160064 | bytes 2883587 | tf_op jit(solution)/shard_map/pallas_call | solution.py:444
  745.8 8.5 fusion
  757.4 5.7 fusion.44
  763.0 5.7 fusion.41
  782.5 29.8 %shard_map.199 = (bf16[8,256,512]{2,1,0:T(8,128)(2,1)}, bf16[8,256,1024]{2,1,0:T(8,128)(2,1)}, f32[4,1,512]{2,1,0:T(1,128)}, bf16[2,256,2048]{2,1,0:T(8,128)(2,1)}, bf16[2,256,2048]{2,1,0:T(8,128)(2,1)}) custom-call(s32[3]{0:T(128)} %pad_add_fusion.place_ref.refs_0_.refs_13_, ...), custom_call_target="tpu_custom_call", output_to_operand_aliasing={{0}: (22, {}), {1}: (23, {})} | custom-call | flops 8589934592 | bytes 19532292 | tf_op jit(solution)/shard_map/pallas_call | solution.py:444
  812.4 9.4 fusion.35
  822.3 5.4 fusion.47
  833.9 36.2 %collective-permute-done.80 = bf16[1024,1024]{1,0:T(8,128)(2,1)} collective-permute-done((bf16[1024,1024]{1,0:T(8,128)(2,1)}, bf16[1024,1024]{1,0:T(8,128)(2,1)}, u32[]{:S(2)}, u32[]{:S(2)}) %collective-permute-start.80) | collective-permute-done | bytes 2097184 | tf_op jit(solution)/shard_map/ppermute | solution.py:28
  879.6 10.3 %collective-permute-start.86 = (bf16[4,2,64,512]{3,2,1,0:T(8,128)(2,1)S(1)}, bf16[4,2,64,512]{3,2,1,0:T(8,128)(2,1)S(1)}, u32[]{:S(2)}, u32[]{:S(2)}) collective-permute-start(bf16[4,2,64,512]{3,2,1,0:T(8,128)(2,1)S(1)} %fusion.72), channel_id=1, source_target_pairs={{0,1},{1,0},{2,3},{3,2},{4,5},{5,4},{6,7},{7,6},{8,9},{9,8},{10,11... | collective-permute-start | bytes 1572872 | tf_op jit(solution)/shard_map/ppermute | solution.py:31
  894.9 9.8 collective-permute-start.84
  919.0 6.6 collective-permute-start.98
  935.8 9.9 collective-permute-done.91
  945.7 7.1 collective-permute-start.92
  956.3 5.7 collective-permute-done.102
  968.9 19.6 %collective-permute-done.103 = bf16[1,1,64,2048]{3,2,1,0:T(8,128)(2,1)} collective-permute-done((bf16[1,1,64,2048]{3,2,1,0:T(8,128)(2,1)}, bf16[1,1,64,2048]{3,2,1,0:T(8,128)(2,1)}, u32[]{:S(2)}, u32[]{:S(2)}) %collective-permute-start.103) | collective-permute-done | bytes 262176 | tf_op jit(solution)/shard_map/ppermute | solution.py:31
  (520 shorter events, 319.0 us)
Async XLA Ops:
  7.2 460.0 %all-gather.3.cloned.1.call-start = ((), (), s32[]{:S(2)}) async-start(), calls=%async_computation.4 | async-start | bytes 6488064 | tf_op jit(solution)/shard_map/all_gather | solution.py:532
  29.9 35.9 %collective-permute-start.8 = (bf16[4,64,2176]{2,1,0:T(8,128)(2,1)S(1)}, bf16[4,64,2176]{2,1,0:T(8,128)(2,1)}, u32[]{:S(2)}, u32[]{:S(2)}) collective-permute-start(bf16[4,64,2176]{2,1,0:T(8,128)(2,1)S(1)} %pad_maximum_fusion.3.refs_1_), channel_id=1, source_target_pairs={{0,16},{16,0},{1,17},{17,1},{2,18},{18,2},{3,19},{19,3},{4,20},{20... | collective-permute-start | bytes 3342344 | tf_op jit(solution)/shard_map/ppermute | solution.py:28
  33.2 32.0 %collective-permute-start.10 = (bf16[256,2048]{1,0:T(8,128)(2,1)}, bf16[256,2048]{1,0:T(8,128)(2,1)}, u32[]{:S(2)}, u32[]{:S(2)}) collective-permute-start(bf16[256,2048]{1,0:T(8,128)(2,1)} %get-tuple-element.153.refs_9_), channel_id=1, source_target_pairs={{0,8},{4,12},{8,0},{12,4},{1,9},{5,13},{9,1},{13,5},{2,10},{6,14},... | collective-permute-start | bytes 3145736 | tf_op jit(solution)/shard_map/ppermute | solution.py:25
  34.7 50.0 %collective-permute-start.7 = (bf16[4,64,2176]{2,1,0:T(8,128)(2,1)S(1)}, bf16[4,64,2176]{2,1,0:T(8,128)(2,1)}, u32[]{:S(2)}, u32[]{:S(2)}) collective-permute-start(bf16[4,64,2176]{2,1,0:T(8,128)(2,1)S(1)} %pad_maximum_fusion.3.refs_1_), channel_id=1, source_target_pairs={{0,1},{1,0},{2,3},{3,2},{4,5},{5,4},{6,7},{7,6},{8,9},{9,8},{10,11... | collective-permute-start | bytes 3342344 | tf_op jit(solution)/shard_map/ppermute | solution.py:31
  36.2 50.8 %collective-permute-start.6 = (bf16[4,64,2176]{2,1,0:T(8,128)(2,1)S(1)}, bf16[4,64,2176]{2,1,0:T(8,128)(2,1)}, u32[]{:S(2)}, u32[]{:S(2)}) collective-permute-start(bf16[4,64,2176]{2,1,0:T(8,128)(2,1)S(1)} %pad_maximum_fusion.3.refs_1_), channel_id=1, source_target_pairs={{0,2},{1,3},{2,0},{3,1},{4,6},{5,7},{6,4},{7,5},{8,10},{9,11},{10,... | collective-permute-start | bytes 3342344 | tf_op jit(solution)/shard_map/ppermute | solution.py:31
  93.1 32.9 %collective-permute-start.11 = (bf16[4,64,2176]{2,1,0:T(8,128)(2,1)}, bf16[4,64,2176]{2,1,0:T(8,128)(2,1)}, u32[]{:S(2)}, u32[]{:S(2)}) collective-permute-start(bf16[4,64,2176]{2,1,0:T(8,128)(2,1)} %collective-permute-done.6.refs_3_), channel_id=1, source_target_pairs={{0,1},{1,0},{2,3},{3,2},{4,5},{5,4},{6,7},{7,6},{8,9},{9,8},{10,11... | collective-permute-start | bytes 3342344 | tf_op jit(solution)/shard_map/ppermute | solution.py:31
  100.0 40.9 %collective-permute-start.12 = (bf16[4,64,2176]{2,1,0:T(8,128)(2,1)}, bf16[4,64,2176]{2,1,0:T(8,128)(2,1)}, u32[]{:S(2)}, u32[]{:S(2)}) collective-permute-start(bf16[4,64,2176]{2,1,0:T(8,128)(2,1)} %collective-permute-done.7.refs_2_), channel_id=1, source_target_pairs={{0,16},{16,0},{1,17},{17,1},{2,18},{18,2},{3,19},{19,3},{4,20},{20... | collective-permute-start | bytes 3342344 | tf_op jit(solution)/shard_map/ppermute | solution.py:28
  104.1 37.8 %collective-permute-start.53 = (bf16[256,2048]{1,0:T(8,128)(2,1)}, bf16[256,2048]{1,0:T(8,128)(2,1)}, u32[]{:S(2)}, u32[]{:S(2)}) collective-permute-start(bf16[256,2048]{1,0:T(8,128)(2,1)} %get-tuple-element.184), channel_id=1, source_target_pairs={{0,4},{4,0},{8,12},{12,8},{1,5},{5,1},{9,13},{13,9},{2,6},{6,2},{1... | collective-permute-start | bytes 3145736 | tf_op jit(solution)/shard_map/ppermute | solution.py:25
  120.4 59.4 %collective-permute-start.22 = (bf16[256,2048]{1,0:T(8,128)(2,1)}, bf16[256,2048]{1,0:T(8,128)(2,1)}, u32[]{:S(2)}, u32[]{:S(2)}) collective-permute-start(bf16[256,2048]{1,0:T(8,128)(2,1)} %get-tuple-element.153.refs_9_), channel_id=1, source_target_pairs={{0,4},{4,0},{8,12},{12,8},{1,5},{5,1},{9,13},{13,9},{2,6},{6,2},{1... | collective-permute-start | bytes 3145736 | tf_op jit(solution)/shard_map/ppermute | solution.py:25
  141.5 36.6 %collective-permute-start.20 = (bf16[4,64,2816]{2,1,0:T(8,128)(2,1)}, bf16[4,64,2816]{2,1,0:T(8,128)(2,1)}, u32[]{:S(2)}, u32[]{:S(2)}) collective-permute-start(bf16[4,64,2816]{2,1,0:T(8,128)(2,1)} %pad_maximum_fusion.2.refs_1_.refs_2_), channel_id=1, source_target_pairs={{0,1},{1,0},{2,3},{3,2},{4,5},{5,4},{6,7},{7,6},{8,9},{9,8},{10,11... | collective-permute-start | bytes 4325384 | tf_op jit(solution)/shard_map/ppermute | solution.py:31
  142.0 37.8 %collective-permute-start.23 = (bf16[256,2048]{1,0:T(8,128)(2,1)}, bf16[256,2048]{1,0:T(8,128)(2,1)}, u32[]{:S(2)}, u32[]{:S(2)}) collective-permute-start(bf16[256,2048]{1,0:T(8,128)(2,1)} %collective-permute-done.10.refs_11_), channel_id=1, source_target_pairs={{0,4},{4,0},{8,12},{12,8},{1,5},{5,1},{9,13},{13,9},{2,6},{6,2},{1... | collective-permute-start | bytes 3145736 | tf_op jit(solution)/shard_map/ppermute | solution.py:25
  169.3 70.9 %collective-permute-start.30 = (bf16[256,2048]{1,0:T(8,128)(2,1)}, bf16[256,2048]{1,0:T(8,128)(2,1)}, u32[]{:S(2)}, u32[]{:S(2)}) collective-permute-start(bf16[256,2048]{1,0:T(8,128)(2,1)} %get-tuple-element.156.refs_9_), channel_id=1, source_target_pairs={{0,4},{4,0},{8,12},{12,8},{1,5},{5,1},{9,13},{13,9},{2,6},{6,2},{1... | collective-permute-start | bytes 3145736 | tf_op jit(solution)/shard_map/ppermute | solution.py:25
  178.1 60.5 %collective-permute-start.17 = (bf16[4,64,2816]{2,1,0:T(8,128)(2,1)}, bf16[4,64,2816]{2,1,0:T(8,128)(2,1)}, u32[]{:S(2)}, u32[]{:S(2)}) collective-permute-start(bf16[4,64,2816]{2,1,0:T(8,128)(2,1)} %pad_maximum_fusion.2.refs_1_.refs_2_), channel_id=1, source_target_pairs={{0,2},{1,3},{2,0},{3,1},{4,6},{5,7},{6,4},{7,5},{8,10},{9,11},{10,... | collective-permute-start | bytes 4325384 | tf_op jit(solution)/shard_map/ppermute | solution.py:31
  179.7 29.3 %collective-permute-start.54 = (bf16[256,2048]{1,0:T(8,128)(2,1)}, bf16[256,2048]{1,0:T(8,128)(2,1)}, u32[]{:S(2)}, u32[]{:S(2)}) collective-permute-start(bf16[256,2048]{1,0:T(8,128)(2,1)} %collective-permute-done.41), channel_id=1, source_target_pairs={{0,4},{4,0},{8,12},{12,8},{1,5},{5,1},{9,13},{13,9},{2,6},{6,2},{1... | collective-permute-start | bytes 3145736 | tf_op jit(solution)/shard_map/ppermute | solution.py:25
  179.7 60.4 %collective-permute-start.26 = (bf16[4,64,2816]{2,1,0:T(8,128)(2,1)}, bf16[4,64,2816]{2,1,0:T(8,128)(2,1)}, u32[]{:S(2)}, u32[]{:S(2)}) collective-permute-start(bf16[4,64,2816]{2,1,0:T(8,128)(2,1)} %pad_maximum_fusion.2.refs_1_.refs_2_), channel_id=1, source_target_pairs={{0,16},{16,0},{1,17},{17,1},{2,18},{18,2},{3,19},{19,3},{4,20},{20... | collective-permute-start | bytes 4325384 | tf_op jit(solution)/shard_map/ppermute | solution.py:28
  206.5 34.3 %collective-permute-start.31 = (bf16[256,2048]{1,0:T(8,128)(2,1)}, bf16[256,2048]{1,0:T(8,128)(2,1)}, u32[]{:S(2)}, u32[]{:S(2)}) collective-permute-start(bf16[256,2048]{1,0:T(8,128)(2,1)} %copy-done.59), channel_id=1, source_target_pairs={{0,4},{4,0},{8,12},{12,8},{1,5},{5,1},{9,13},{13,9},{2,6},{6,2},{1... | collective-permute-start | bytes 3145736 | tf_op jit(solution)/shard_map/ppermute | solution.py:25
  228.3 40.7 %collective-permute-start.32 = (bf16[4,4,128,128]{3,2,1,0:T(8,128)(2,1)}, bf16[4,4,128,128]{3,2,1,0:T(8,128)(2,1)S(1)}, u32[]{:S(2)}, u32[]{:S(2)}) collective-permute-start(bf16[4,4,128,128]{3,2,1,0:T(8,128)(2,1)} %add_convert_fusion.25), channel_id=1, source_target_pairs={{0,1},{4,5},{8,9},{12,13},{16,17},{20,21},{24,25},{28,29}} | collective-permute-start | bytes 1572872 | tf_op jit(solution)/shard_map/ppermute | solution.py:571
  238.6 46.8 %collective-permute-start.38 = (bf16[4,64,2816]{2,1,0:T(8,128)(2,1)}, bf16[4,64,2816]{2,1,0:T(8,128)(2,1)}, u32[]{:S(2)}, u32[]{:S(2)}) collective-permute-start(bf16[4,64,2816]{2,1,0:T(8,128)(2,1)} %collective-permute-done.20.refs_2_.refs_3_), channel_id=1, source_target_pairs={{0,16},{16,0},{1,17},{17,1},{2,18},{18,2},{3,19},{19,3},{4,20},{20... | collective-permute-start | bytes 4325384 | tf_op jit(solution)/shard_map/ppermute | solution.py:28
  240.2 33.1 %collective-permute-start.33 = (bf16[4,64,2816]{2,1,0:T(8,128)(2,1)}, bf16[4,64,2816]{2,1,0:T(8,128)(2,1)}, u32[]{:S(2)}, u32[]{:S(2)}) collective-permute-start(bf16[4,64,2816]{2,1,0:T(8,128)(2,1)} %collective-permute-done.17.refs_3_.refs_4_), channel_id=1, source_target_pairs={{0,1},{1,0},{2,3},{3,2},{4,5},{5,4},{6,7},{7,6},{8,9},{9,8},{10,11... | collective-permute-start | bytes 4325384 | tf_op jit(solution)/shard_map/ppermute | solution.py:31
  240.2 62.6 %collective-permute-start.18 = (bf16[4,64,2816]{2,1,0:T(8,128)(2,1)}, bf16[4,64,2816]{2,1,0:T(8,128)(2,1)}, u32[]{:S(2)}, u32[]{:S(2)}) collective-permute-start(bf16[4,64,2816]{2,1,0:T(8,128)(2,1)} %collective-permute-done.17.refs_3_.refs_4_), channel_id=1, source_target_pairs={{0,16},{16,0},{1,17},{17,1},{2,18},{18,2},{3,19},{19,3},{4,20},{20... | collective-permute-start | bytes 4325384 | tf_op jit(solution)/shard_map/ppermute | solution.py:28
  240.7 44.7 %collective-permute-start.42 = (bf16[256,2048]{1,0:T(8,128)(2,1)}, bf16[256,2048]{1,0:T(8,128)(2,1)}, u32[]{:S(2)}, u32[]{:S(2)}) collective-permute-start(bf16[256,2048]{1,0:T(8,128)(2,1)} %get-tuple-element.185), channel_id=1, source_target_pairs={{0,8},{4,12},{8,0},{12,4},{1,9},{5,13},{9,1},{13,5},{2,10},{6,14},... | collective-permute-start | bytes 3145736 | tf_op jit(solution)/shard_map/ppermute | solution.py:25
  322.2 333.7 %reduce-scatter.3.cloned.1.call-start = ((), (), s32[]{:S(2)}) async-start(), calls=%async_computation.2 | async-start | bytes 6488064 | tf_op jit(solution)/shard_map/reduce_scatter | solution.py:636
  338.9 43.1 %collective-permute-start.39 = (bf16[4,64,2816]{2,1,0:T(8,128)(2,1)}, bf16[4,64,2816]{2,1,0:T(8,128)(2,1)}, u32[]{:S(2)}, u32[]{:S(2)}) collective-permute-start(bf16[4,64,2816]{2,1,0:T(8,128)(2,1)} %collective-permute-done.33.refs_4_.refs_5_), channel_id=1, source_target_pairs={{0,16},{16,0},{1,17},{17,1},{2,18},{18,2},{3,19},{19,3},{4,20},{20... | collective-permute-start | bytes 4325384 | tf_op jit(solution)/shard_map/ppermute | solution.py:28
  342.3 43.6 %collective-permute-start.46 = (bf16[1,256,2048]{2,1,0:T(8,128)(2,1)}, bf16[1,256,2048]{2,1,0:T(8,128)(2,1)S(1)}, u32[]{:S(2)}, u32[]{:S(2)}) collective-permute-start(bf16[1,256,2048]{2,1,0:T(8,128)(2,1)} %fusion.59), channel_id=1, source_target_pairs={{0,8},{4,12},{8,0},{12,4},{1,9},{5,13},{9,1},{13,5},{2,10},{6,14},... | collective-permute-start | bytes 3145736 | tf_op jit(solution)/shard_map/ppermute | solution.py:25
  382.0 55.3 %collective-permute-start.55 = (bf16[256,2048]{1,0:T(8,128)(2,1)}, bf16[256,2048]{1,0:T(8,128)(2,1)}, u32[]{:S(2)}, u32[]{:S(2)}) collective-permute-start(bf16[256,2048]{1,0:T(8,128)(2,1)} %get-tuple-element.185), channel_id=1, source_target_pairs={{0,4},{4,0},{8,12},{12,8},{1,5},{5,1},{9,13},{13,9},{2,6},{6,2},{1... | collective-permute-start | bytes 3145736 | tf_op jit(solution)/shard_map/ppermute | solution.py:25
  382.0 59.9 %collective-permute-start.56 = (bf16[256,2048]{1,0:T(8,128)(2,1)}, bf16[256,2048]{1,0:T(8,128)(2,1)}, u32[]{:S(2)}, u32[]{:S(2)}) collective-permute-start(bf16[256,2048]{1,0:T(8,128)(2,1)} %collective-permute-done.42), channel_id=1, source_target_pairs={{0,4},{4,0},{8,12},{12,8},{1,5},{5,1},{9,13},{13,9},{2,6},{6,2},{1... | collective-permute-start | bytes 3145736 | tf_op jit(solution)/shard_map/ppermute | solution.py:25
  382.5 30.6 %collective-permute-start.49 = (bf16[256,2048]{1,0:T(8,128)(2,1)}, bf16[256,2048]{1,0:T(8,128)(2,1)}, u32[]{:S(2)}, u32[]{:S(2)}) collective-permute-start(bf16[256,2048]{1,0:T(8,128)(2,1)} %multiply_multiply_fusion.refs_9_), channel_id=1, source_target_pairs={{0,4},{4,0},{8,12},{12,8},{1,5},{5,1},{9,13},{13,9},{2,6},{6,2},{1... | collective-permute-start | bytes 3145736 | tf_op jit(solution)/shard_map/ppermute | solution.py:25
  413.1 31.1 %collective-permute-start.47 = (bf16[256,2048]{1,0:T(8,128)(2,1)S(1)}, bf16[256,2048]{1,0:T(8,128)(2,1)}, u32[]{:S(2)}, u32[]{:S(2)}) collective-permute-start(bf16[256,2048]{1,0:T(8,128)(2,1)S(1)} %multiply_convert_fusion.refs_9_), channel_id=1, source_target_pairs={{0,4},{4,0},{8,12},{12,8},{1,5},{5,1},{9,13},{13,9},{2,6},{6,2},{1... | collective-permute-start | bytes 3145736 | tf_op jit(solution)/shard_map/ppermute | solution.py:25
  518.2 447.7 %reduce-scatter.5.cloned.1.call-start = ((), (), s32[]{:S(2)}) async-start(), calls=%async_computation.3 | async-start | bytes 7208960 | tf_op jit(solution)/shard_map/reduce_scatter | solution.py:774
  521.2 34.4 %collective-permute-start.58 = (bf16[1,256,2048]{2,1,0:T(8,128)(2,1)}, bf16[1,256,2048]{2,1,0:T(8,128)(2,1)S(1)}, u32[]{:S(2)}, u32[]{:S(2)}) collective-permute-start(bf16[1,256,2048]{2,1,0:T(8,128)(2,1)} %fusion.60), channel_id=1, source_target_pairs={{0,8},{4,12},{8,0},{12,4},{1,9},{5,13},{9,1},{13,5},{2,10},{6,14},... | collective-permute-start | bytes 3145736 | tf_op jit(solution)/shard_map/ppermute | solution.py:25
  563.9 30.9 %collective-permute-start.60 = (bf16[256,2048]{1,0:T(8,128)(2,1)}, bf16[256,2048]{1,0:T(8,128)(2,1)}, u32[]{:S(2)}, u32[]{:S(2)}) collective-permute-start(bf16[256,2048]{1,0:T(8,128)(2,1)} %add_convert_fusion.7.refs_9_), channel_id=1, source_target_pairs={{0,4},{4,0},{8,12},{12,8},{1,5},{5,1},{9,13},{13,9},{2,6},{6,2},{1... | collective-permute-start | bytes 3145736 | tf_op jit(solution)/shard_map/ppermute | solution.py:25
  593.1 152.7 %collective-permute-start.93 = (bf16[1024,2816]{1,0:T(8,128)(2,1)}, bf16[1024,2816]{1,0:T(8,128)(2,1)}, u32[]{:S(2)}, u32[]{:S(2)}) collective-permute-start(bf16[1024,2816]{1,0:T(8,128)(2,1)} %convolution_convert_fusion.2), channel_id=1, source_target_pairs={{0,16},{16,0},{1,17},{17,1},{2,18},{18,2},{3,19},{19,3},{4,20},{20... | collective-permute-start | bytes 17301512 | tf_op jit(solution)/shard_map/ppermute | solution.py:28
  608.5 33.9 %collective-permute-start.63 = (bf16[4,4,128,128]{3,2,1,0:T(8,128)(2,1)S(1)}, bf16[4,4,128,128]{3,2,1,0:T(8,128)(2,1)S(1)}, u32[]{:S(2)}, u32[]{:S(2)}) collective-permute-start(bf16[4,4,128,128]{3,2,1,0:T(8,128)(2,1)S(1)} %add_convert_fusion.19), channel_id=1, source_target_pairs={{3,2},{7,6},{11,10},{15,14},{19,18},{23,22},{27,26},{31,30}} | collective-permute-start | bytes 1572872 | tf_op jit(solution)/shard_map/ppermute | solution.py:571
  683.2 32.2 %collective-permute-start.72 = (bf16[4,4,128,128]{3,2,1,0:T(8,128)(2,1)}, bf16[4,4,128,128]{3,2,1,0:T(8,128)(2,1)}, u32[]{:S(2)}, u32[]{:S(2)}) collective-permute-start(bf16[4,4,128,128]{3,2,1,0:T(8,128)(2,1)} %fusion.57), channel_id=1, source_target_pairs={{2,1},{6,5},{10,9},{14,13},{18,17},{22,21},{26,25},{30,29}} | collective-permute-start | bytes 1572872 | tf_op jit(solution)/shard_map/ppermute | solution.py:571
  714.9 39.4 %collective-permute-start.73 = (bf16[1,2,256,2048]{3,2,1,0:T(8,128)(2,1)}, bf16[1,2,256,2048]{3,2,1,0:T(8,128)(2,1)}, u32[]{:S(2)}, u32[]{:S(2)}) collective-permute-start(bf16[1,2,256,2048]{3,2,1,0:T(8,128)(2,1)} %bitcast.466), channel_id=1, source_target_pairs={{0,4},{4,0},{8,12},{12,8},{1,5},{5,1},{9,13},{13,9},{2,6},{6,2},{1... | collective-permute-start | bytes 6291464 | tf_op jit(solution)/shard_map/ppermute | solution.py:25
  743.4 33.4 %collective-permute-start.71 = (bf16[4,256,2048]{2,1,0:T(8,128)(2,1)}, bf16[4,256,2048]{2,1,0:T(8,128)(2,1)}, u32[]{:S(2)}, u32[]{:S(2)}) collective-permute-start(bf16[4,256,2048]{2,1,0:T(8,128)(2,1)} %get-tuple-element.236), channel_id=1, source_target_pairs={{0,4},{4,0},{8,12},{12,8},{1,5},{5,1},{9,13},{13,9},{2,6},{6,2},{1... | collective-permute-start | bytes 12582920 | tf_op jit(solution)/shard_map/ppermute | solution.py:25
  768.7 53.0 %collective-permute-start.76 = (bf16[1,256,2048]{2,1,0:T(8,128)(2,1)}, bf16[1,256,2048]{2,1,0:T(8,128)(2,1)}, u32[]{:S(2)}, u32[]{:S(2)}) collective-permute-start(bf16[1,256,2048]{2,1,0:T(8,128)(2,1)} %fusion.62), channel_id=1, source_target_pairs={{0,8},{4,12},{8,0},{12,4},{1,9},{5,13},{9,1},{13,5},{2,10},{6,14},... | collective-permute-start | bytes 3145736 | tf_op jit(solution)/shard_map/ppermute | solution.py:25
  769.3 108.6 %collective-permute-start.82 = (bf16[1024,512]{1,0:T(8,128)(2,1)}, bf16[1024,512]{1,0:T(8,128)(2,1)}, u32[]{:S(2)}, u32[]{:S(2)}) collective-permute-start(bf16[1024,512]{1,0:T(8,128)(2,1)} %fusion.41), channel_id=1, source_target_pairs={{0,16},{16,0},{1,17},{17,1},{2,18},{18,2},{3,19},{19,3},{4,20},{20... | collective-permute-start | bytes 3145736 | tf_op jit(solution)/shard_map/ppermute | solution.py:28
  780.5 128.6 %collective-permute-start.74 = (bf16[256,2048]{1,0:T(8,128)(2,1)}, bf16[256,2048]{1,0:T(8,128)(2,1)}, u32[]{:S(2)}, u32[]{:S(2)}) collective-permute-start(bf16[256,2048]{1,0:T(8,128)(2,1)} %get-tuple-element.294), channel_id=1, source_target_pairs={{0,8},{4,12},{8,0},{12,4},{1,9},{5,13},{9,1},{13,5},{2,10},{6,14},... | collective-permute-start | bytes 3145736 | tf_op jit(solution)/shard_map/ppermute | solution.py:25
  782.0 127.3 %collective-permute-start.75 = (bf16[256,2048]{1,0:T(8,128)(2,1)}, bf16[256,2048]{1,0:T(8,128)(2,1)}, u32[]{:S(2)}, u32[]{:S(2)}) collective-permute-start(bf16[256,2048]{1,0:T(8,128)(2,1)} %get-tuple-element.295), channel_id=1, source_target_pairs={{0,8},{4,12},{8,0},{12,4},{1,9},{5,13},{9,1},{13,5},{2,10},{6,14},... | collective-permute-start | bytes 3145736 | tf_op jit(solution)/shard_map/ppermute | solution.py:25
  821.8 48.3 %collective-permute-start.80 = (bf16[1024,1024]{1,0:T(8,128)(2,1)}, bf16[1024,1024]{1,0:T(8,128)(2,1)}, u32[]{:S(2)}, u32[]{:S(2)}) collective-permute-start(bf16[1024,1024]{1,0:T(8,128)(2,1)} %fusion.35), channel_id=1, source_target_pairs={{0,16},{16,0},{1,17},{17,1},{2,18},{18,2},{3,19},{19,3},{4,20},{20... | collective-permute-start | bytes 6291464 | tf_op jit(solution)/shard_map/ppermute | solution.py:28
  832.4 72.3 %collective-permute-start.79 = (bf16[1,256,2048]{2,1,0:T(8,128)(2,1)S(1)}, bf16[1,256,2048]{2,1,0:T(8,128)(2,1)S(1)}, u32[]{:S(2)}, u32[]{:S(2)}) collective-permute-start(bf16[1,256,2048]{2,1,0:T(8,128)(2,1)S(1)} %fusion.65), channel_id=1, source_target_pairs={{0,8},{4,12},{8,0},{12,4},{1,9},{5,13},{9,1},{13,5},{2,10},{6,14},... | collective-permute-start | bytes 3145736 | tf_op jit(solution)/shard_map/ppermute | solution.py:25
  879.6 36.3 %collective-permute-start.86 = (bf16[4,2,64,512]{3,2,1,0:T(8,128)(2,1)S(1)}, bf16[4,2,64,512]{3,2,1,0:T(8,128)(2,1)S(1)}, u32[]{:S(2)}, u32[]{:S(2)}) collective-permute-start(bf16[4,2,64,512]{3,2,1,0:T(8,128)(2,1)S(1)} %fusion.72), channel_id=1, source_target_pairs={{0,1},{1,0},{2,3},{3,2},{4,5},{5,4},{6,7},{7,6},{8,9},{9,8},{10,11... | collective-permute-start | bytes 1572872 | tf_op jit(solution)/shard_map/ppermute | solution.py:31
  894.9 57.9 %collective-permute-start.84 = (bf16[4,2,64,1024]{3,2,1,0:T(8,128)(2,1)S(1)}, bf16[4,2,64,1024]{3,2,1,0:T(8,128)(2,1)S(1)}, u32[]{:S(2)}, u32[]{:S(2)}) collective-permute-start(bf16[4,2,64,1024]{3,2,1,0:T(8,128)(2,1)S(1)} %fusion.66), channel_id=1, source_target_pairs={{0,1},{1,0},{2,3},{3,2},{4,5},{5,4},{6,7},{7,6},{8,9},{9,8},{10,11... | collective-permute-start | bytes 3145736 | tf_op jit(solution)/shard_map/ppermute | solution.py:31
  904.7 29.2 %collective-permute-start.85 = (bf16[256,2048]{1,0:T(8,128)(2,1)S(1)}, bf16[256,2048]{1,0:T(8,128)(2,1)S(1)}, u32[]{:S(2)}, u32[]{:S(2)}) collective-permute-start(bf16[256,2048]{1,0:T(8,128)(2,1)S(1)} %copy-done.60), channel_id=1, source_target_pairs={{0,16},{16,0},{1,17},{17,1},{2,18},{18,2},{3,19},{19,3},{4,20},{20... | collective-permute-start | bytes 3145736 | tf_op jit(solution)/shard_map/ppermute | solution.py:28
  915.9 39.4 %collective-permute-start.83 = (bf16[4,2,64,512]{3,2,1,0:T(8,128)(2,1)S(1)}, bf16[4,2,64,512]{3,2,1,0:T(8,128)(2,1)S(1)}, u32[]{:S(2)}, u32[]{:S(2)}) collective-permute-start(bf16[4,2,64,512]{3,2,1,0:T(8,128)(2,1)S(1)} %fusion.73), channel_id=1, source_target_pairs={{0,1},{1,0},{2,3},{3,2},{4,5},{5,4},{6,7},{7,6},{8,9},{9,8},{10,11... | collective-permute-start | bytes 1572872 | tf_op jit(solution)/shard_map/ppermute | solution.py:31
  919.0 81.2 %collective-permute-start.98 = (bf16[4,1,64,512]{3,2,1,0:T(8,128)(2,1)}, bf16[4,1,64,512]{3,2,1,0:T(8,128)(2,1)}, u32[]{:S(2)}, u32[]{:S(2)}) collective-permute-start(bf16[4,1,64,512]{3,2,1,0:T(8,128)(2,1)} %bitcast.120), channel_id=1, source_target_pairs={{0,2},{1,3},{2,0},{3,1},{4,6},{5,7},{6,4},{7,5},{8,10},{9,11},{10,... | collective-permute-start | bytes 786440 | tf_op jit(solution)/shard_map/ppermute | solution.py:31
  955.3 44.8 %collective-permute-start.97 = (bf16[4,1,64,1024]{3,2,1,0:T(8,128)(2,1)}, bf16[4,1,64,1024]{3,2,1,0:T(8,128)(2,1)}, u32[]{:S(2)}, u32[]{:S(2)}) collective-permute-start(bf16[4,1,64,1024]{3,2,1,0:T(8,128)(2,1)} %bitcast.116), channel_id=1, source_target_pairs={{0,2},{1,3},{2,0},{3,1},{4,6},{5,7},{6,4},{7,5},{8,10},{9,11},{10,... | collective-permute-start | bytes 1572872 | tf_op jit(solution)/shard_map/ppermute | solution.py:31
  (157 other events, 2581.6 us)
Sparse Core Ops, SparseCore 0:
  322.3 100.7 all-gather.2
  518.3 114.5 reduce-scatter.2
  754.4 113.3 reduce-scatter.4

commit v5 on v4

--- a/solution.py
+++ b/solution.py
@@ -696,7 +696,7 @@
         all_cot = jnp.concatenate([jnp.stack(pieces) for pieces in cotangent])
         for c in range(micro):
             normed2, hidden, first, second = over_sequences(
-                up_kernel, turn("up", c), c, TEAM,
+                up_kernel, turn("up", c, all_cot), c, TEAM,
                 [],
                 [(span + (features,), BF16, "all")] + [(span + (own_ff,), BF16, "all")] * 3,
                 [normed2, hidden, first, second], [gu],

time: 1040 us -> 1040 us (level)
    unnamed x204 -> x212, local copies, waits for them, and re-layouts: 22.5 us -> 22.2 us
  transfers between devices with their start and end apart: 107 -> 107, of which waited for: 36 -> 36; matrix products, arithmetic and copies ran while one was open for 27% -> 26% of each run, Pallas kernels for 25% -> 25%
where the time goes in v5:
time: 1040 us; the launch traced here: 1030 us
  waiting for transfers between devices  313 us (30%)
  Pallas kernels  300 us (29%)
  other arithmetic  126 us (12%)
  starting transfers between devices  115 us (11%)
  matrix products  96.4 us (9%)
  local copies, waits for them, and re-layouts  63.8 us (6%)
  between operations  15.3 us (1%)
    pallas_call x13, Pallas kernels, over_sequences(): pl.pallas_call(body, grid=(count,), in_specs=specs, out_specs=[spec(shape...  291 us
    ppermute x55, waiting for transfers between devices, swap(): return lax.ppermute(value, 'team', [(i, i ^ bits) for i in range(TEAM)])  108 us
    ppermute x18, waiting for transfers between devices, swap_y(): return lax.ppermute(value, 'y', [(i, i ^ bits) for i in range(self.ny)])  107 us
    dot_general x11, matrix products, tn(): lax.dot_general(a, b, (((0,), (0,)), ((), ())), preferred_element_type=F32)  96.2 us
    ppermute x19, waiting for transfers between devices, swap_z(): return lax.ppermute(value, 'seq', [(i, i ^ bits) for i in range(self.nz)])  87.3 us
    ppermute x19, starting transfers between devices, swap_z(): return lax.ppermute(value, 'seq', [(i, i ^ bits) for i in range(self.nz)])  53.1 us
    ppermute x55, starting transfers between devices, swap(): return lax.ppermute(value, 'team', [(i, i ^ bits) for i in range(TEAM)])  26.3 us
    unnamed x212, local copies, waits for them, and re-layouts  22.2 us
  transfers between devices with their start and end apart: 107, of which 36 were waited for; matrix products, arithmetic and copies ran while one was open for 26% of the time, Pallas kernels for 25%

profile of v5, /device:TPU:0, one launch (start us, length us, event | category | flops | bytes accessed | tf_op | source)
XLA Modules:
  0.0 1029.3 jit_solution(7898983980229616999)
XLA Ops:
  15.5 7.6 collective-permute-done.1
  23.0 5.6 collective-permute-done.2
  44.1 14.6 %dynamic-slice_reduce_fusion.3 = (bf16[64,4,704]{2,1,0:T(4,128)(2,1)}, bf16[64,4,704]{2,1,0:T(4,128)(2,1)}, bf16[64,4,704]{2,1,0:T(4,128)(2,1)}, bf16[64,4,704]{2,1,0:T(4,128)(2,1)}) fusion(bf16[64,4,4,704]{3,2,1,0:T(4,128)(2,1)} %reshape.1143, s32[]{:T(128)S(6)} %select_n.213, s32[]{:T(128)S(6)} %select_n.215, s32[]{:T(128)S(6)} %select_n.214, ...), kind=kLoop, calls=%fused_computation.146 | loop fusion | bytes 2883600 | tf_op jit(solution)/shard_map/jit(dynamic_index_in_dim)/dynamic_slice | solution.py:483
  69.3 15.2 %collective-permute-done.7.refs_2_ = bf16[4,64,2176]{2,1,0:T(8,128)(2,1)} collective-permute-done((bf16[4,64,2176]{2,1,0:T(8,128)(2,1)S(1)}, bf16[4,64,2176]{2,1,0:T(8,128)(2,1)}, u32[]{:S(2)}, u32[]{:S(2)}) %collective-permute-start.7) | collective-permute-done | bytes 1114144 | tf_op jit(solution)/shard_map/ppermute | solution.py:31
  93.6 6.3 collective-permute-done.16.refs_3_
  104.0 11.6 %collective-permute-done.14.refs_11_ = bf16[256,2048]{1,0:T(8,128)(2,1)S(1)} collective-permute-done((bf16[256,2048]{1,0:T(8,128)(2,1)}, bf16[256,2048]{1,0:T(8,128)(2,1)S(1)}, u32[]{:S(2)}, u32[]{:S(2)}) %collective-permute-start.14) | collective-permute-done | bytes 1048608 | tf_op jit(solution)/shard_map/ppermute | solution.py:25
  120.3 5.7 collective-permute-done.11.refs_4_
  125.9 14.8 %collective-permute-done.12.refs_6_ = bf16[4,64,2176]{2,1,0:T(8,128)(2,1)} collective-permute-done((bf16[4,64,2176]{2,1,0:T(8,128)(2,1)}, bf16[4,64,2176]{2,1,0:T(8,128)(2,1)}, u32[]{:S(2)}, u32[]{:S(2)}) %collective-permute-start.12) | collective-permute-done | bytes 1114144 | tf_op jit(solution)/shard_map/ppermute | solution.py:28
  148.0 14.8 %collective-permute-done.39 = bf16[256,2048]{1,0:T(8,128)(2,1)} collective-permute-done((bf16[256,2048]{1,0:T(8,128)(2,1)}, bf16[256,2048]{1,0:T(8,128)(2,1)}, u32[]{:S(2)}, u32[]{:S(2)}) %collective-permute-start.39) | collective-permute-done | bytes 1048608 | tf_op jit(solution)/shard_map/ppermute | solution.py:25
  169.2 8.8 collective-permute-done.19.refs_4_
  181.6 23.8 %shard_map.187 = (bf16[8,256,2048]{2,1,0:T(8,128)(2,1)}, f32[8,256,2048]{2,1,0:T(8,128)}, f32[8,256,512]{2,1,0:T(8,128)}, bf16[8,256,512]{2,1,0:T(8,128)(2,1)}, ...) custom-call(s32[3]{0:T(128)} %pad_add_fusion.place_ref.refs_0_.refs_, ...), custom_call_target="tpu_custom_call" | custom-call | flops 8589934592 | bytes 3278854 | tf_op jit(solution)/shard_map/pallas_call | solution.py:444
  211.5 9.4 collective-permute-done.27.refs_6_
  223.0 5.1 collective-permute-done.29.refs_8_
  230.8 7.7 collective-permute-done.17.refs_3_.refs_4_
  242.1 24.2 %shard_map.188 = (bf16[8,256,2048]{2,1,0:T(8,128)(2,1)}, f32[8,256,2048]{2,1,0:T(8,128)}, f32[8,256,512]{2,1,0:T(8,128)}, bf16[8,256,512]{2,1,0:T(8,128)(2,1)}, ...) custom-call(s32[3]{0:T(128)} %pad_add_fusion.place_ref.refs_0_.refs_, ...), custom_call_target="tpu_custom_call", output_to_operand_aliasing={{0}: (16, {}), {1}: (17, {}), {2}: (18, {}), {3}: (19, {}),... | custom-call | flops 8589934592 | bytes 11667462 | tf_op jit(solution)/shard_map/pallas_call | solution.py:444
  273.9 9.5 collective-permute-done.46
  291.7 10.9 %collective-permute-done.18.refs_7_.refs_8_ = bf16[4,64,2816]{2,1,0:T(8,128)(2,1)} collective-permute-done((bf16[4,64,2816]{2,1,0:T(8,128)(2,1)}, bf16[4,64,2816]{2,1,0:T(8,128)(2,1)}, u32[]{:S(2)}, u32[]{:S(2)}) %collective-permute-start.18) | collective-permute-done | bytes 1441824 | tf_op jit(solution)/shard_map/ppermute | solution.py:28
  307.8 12.2 %shard_map.189 = (f32[8,256,512]{2,1,0:T(8,128)}, bf16[8,256,512]{2,1,0:T(8,128)(2,1)}, bf16[2,256,2048]{2,1,0:T(8,128)(2,1)}, bf16[2,256,2048]{2,1,0:T(8,128)(2,1)}) custom-call(s32[3]{0:T(128)} %pad_add_fusion.place_ref.refs_0_.refs_13_, bf16[1,64,2048]{2,1,0:T(8,128)(2,1)} %bitcast.397, bf16[1,64,2048]{2,1,0:T(8,128)(2,1)} %copy-done.40, ...), custom_call_target="tpu_custom_call" | custom-call | flops 2147483648 | bytes 5899395 | tf_op jit(solution)/shard_map/pallas_call | solution.py:444
  322.2 12.5 %shard_map.190 = (f32[8,256,512]{2,1,0:T(8,128)}, bf16[8,256,512]{2,1,0:T(8,128)(2,1)}, bf16[2,256,2048]{2,1,0:T(8,128)(2,1)}, bf16[2,256,2048]{2,1,0:T(8,128)(2,1)}) custom-call(s32[3]{0:T(128)} %pad_add_fusion.place_ref.refs_0_.refs_13_, bf16[1,64,2048]{2,1,0:T(8,128)(2,1)} %bitcast.398, ...), custom_call_target="tpu_custom_call", output_to_operand_aliasing={{0}: (15, {}), {1}: (16, {})} | custom-call | flops 2147483648 | bytes 7472259 | tf_op jit(solution)/shard_map/pallas_call | solution.py:444
  341.7 21.5 %collective-permute-done.37 = bf16[1,256,2048]{2,1,0:T(8,128)(2,1)S(1)} collective-permute-done((bf16[1,256,2048]{2,1,0:T(8,128)(2,1)S(1)}, bf16[1,256,2048]{2,1,0:T(8,128)(2,1)S(1)}, u32[]{:S(2)}, u32[]{:S(2)}) %collective-permute-start.37) | collective-permute-done | bytes 1048608 | tf_op jit(solution)/shard_map/ppermute | solution.py:25
  365.9 16.6 %collective-permute-done.45.refs_8_.refs_9_ = bf16[4,64,2816]{2,1,0:T(8,128)(2,1)S(1)} collective-permute-done((bf16[4,64,2816]{2,1,0:T(8,128)(2,1)}, bf16[4,64,2816]{2,1,0:T(8,128)(2,1)S(1)}, u32[]{:S(2)}, u32[]{:S(2)}) %collective-permute-start.45) | collective-permute-done | bytes 1441824 | tf_op jit(solution)/shard_map/ppermute | solution.py:28
  387.0 20.4 %collective-permute-done.54.refs_11_ = bf16[256,2048]{1,0:T(8,128)(2,1)S(1)} collective-permute-done((bf16[256,2048]{1,0:T(8,128)(2,1)S(1)}, bf16[256,2048]{1,0:T(8,128)(2,1)S(1)}, u32[]{:S(2)}, u32[]{:S(2)}) %collective-permute-start.54) | collective-permute-done | bytes 1048608 | tf_op jit(solution)/shard_map/ppermute | solution.py:25
  413.5 22.6 %shard_map.191 = (bf16[8,256,2048]{2,1,0:T(8,128)(2,1)}, bf16[8,256,1408]{2,1,0:T(8,128)(2,1)}, bf16[8,256,1408]{2,1,0:T(8,128)(2,1)}, bf16[8,256,1408]{2,1,0:T(8,128)(2,1)}) custom-call(s32[3]{0:T(128)} %pad_add_fusion.place_ref.refs_0_.refs_13_, bf16[4,64,2816]{2,1,0:T(8,128)(2,1)} %pad_maximum_fusion.2.refs_1_.refs_2_, ...), custom_call_target="tpu_custom_call" | custom-call | flops 11811160064 | bytes 3932163 | tf_op jit(solution)/shard_map/pallas_call | solution.py:444
  440.6 23.0 %shard_map.192 = (bf16[8,256,2048]{2,1,0:T(8,128)(2,1)}, bf16[8,256,1408]{2,1,0:T(8,128)(2,1)}, bf16[8,256,1408]{2,1,0:T(8,128)(2,1)}, bf16[8,256,1408]{2,1,0:T(8,128)(2,1)}) custom-call(s32[3]{0:T(128)} %pad_add_fusion.place_ref.refs_0_.refs_13_, ...), custom_call_target="tpu_custom_call", output_to_operand_aliasing={{0}: (13, {}), {1}: (14, {}), {2}: (15, {}), {3}: (16, {})} | custom-call | flops 11811160064 | bytes 10354691 | tf_op jit(solution)/shard_map/pallas_call | solution.py:444
  463.7 32.3 %shard_map.193 = (bf16[8,256,2816]{2,1,0:T(8,128)(2,1)}, bf16[2,256,2048]{2,1,0:T(8,128)(2,1)}, bf16[2,256,2048]{2,1,0:T(8,128)(2,1)}) custom-call(s32[3]{0:T(128)} %pad_add_fusion.place_ref.refs_0_.refs_13_, bf16[8,1,176,2048]{3,2,1,0:T(8,128)(2,1)} %bitcast.463, bf16[4,64,2816]{2,1,0:T(8,128)(2,1)} %pad_maximum_fusion.2.refs_1_.refs_2_, ...), custom_call_target="tpu_custom_call" | custom-call | flops 17716740096 | bytes 9306115 | tf_op jit(solution)/shard_map/pallas_call | solution.py:444
  496.2 18.1 %convolution_convert_fusion = bf16[1408,2048]{1,0:T(8,128)(2,1)} fusion(bf16[2048,1408]{1,0:T(8,128)(2,1)} %bitcast.476, bf16[2048,2048]{1,0:T(8,128)(2,1)} %bitcast.455), kind=kOutput, calls=%fused_computation.2 | convolution fusion | flops 11814043648 | bytes 19922944 | tf_op jit(solution)/shard_map/dot_general | solution.py:122
  518.8 32.9 %shard_map.194 = (bf16[8,256,2816]{2,1,0:T(8,128)(2,1)}, bf16[2,256,2048]{2,1,0:T(8,128)(2,1)}, bf16[2,256,2048]{2,1,0:T(8,128)(2,1)}) custom-call(s32[3]{0:T(128)} %pad_add_fusion.place_ref.refs_0_.refs_13_, bf16[8,1,176,2048]{3,2,1,0:T(8,128)(2,1)} %bitcast.464, ...), custom_call_target="tpu_custom_call", output_to_operand_aliasing={{0}: (13, {})} | custom-call | flops 17716740096 | bytes 12189699 | tf_op jit(solution)/shard_map/pallas_call | solution.py:444
  560.6 19.6 %convolution_convert_fusion.2 = bf16[1024,2816]{1,0:T(8,128)(2,1)} fusion(bf16[2048,2816]{1,0:T(8,128)(2,1)} %bitcast.472, bf16[2048,2048]{1,0:T(8,128)(2,1)} %bitcast.474, s32[]{:T(128)S(6)} %select_n.217), kind=kOutput, calls=%fused_computation.8 | convolution fusion | flops 11814043648 | bytes 21495812 | tf_op jit(solution)/shard_map/dot_general | solution.py:122
  591.3 11.8 %shard_map.195 = (bf16[8,256,2048]{2,1,0:T(8,128)(2,1)}, bf16[8,256,512]{2,1,0:T(8,128)(2,1)}, bf16[4,256,512]{2,1,0:T(8,128)(2,1)}, f32[4,4,128,128]{3,2,1,0:T(8,128)}, f32[4,1,512]{2,1,0:T(1,128)}) custom-call(s32[3]{0:T(128)} %pad_add_fusion.place_ref.refs_0_.refs_13_, bf16[1,64,2048]{2,1,0:T(8,128)(2,1)} %bitcast.399, bf16[1,64,2048]{2,1,0:T(8,128)(2,1)} %copy-done.40, ...), custom_call_target="tpu_custom_call" | custom-call | flops 2147483648 | bytes 7341187 | tf_op jit(solution)/shard_map/pallas_call | solution.py:444
  605.7 6.7 collective-permute-done.64
  619.7 19.2 %convolution_convert_fusion.1 = bf16[1024,2816]{1,0:T(8,128)(2,1)} fusion(bf16[2048,2816]{1,0:T(8,128)(2,1)} %bitcast.473, bf16[2048,2048]{1,0:T(8,128)(2,1)} %bitcast.475, s32[]{:T(128)S(6)} %select_n.218), kind=kOutput, calls=%fused_computation.7 | convolution fusion | flops 11814043648 | bytes 21495812 | tf_op jit(solution)/shard_map/dot_general | solution.py:122
  654.8 11.7 %shard_map.196 = (bf16[8,256,2048]{2,1,0:T(8,128)(2,1)}, bf16[8,256,512]{2,1,0:T(8,128)(2,1)}, bf16[4,256,512]{2,1,0:T(8,128)(2,1)}, f32[4,4,128,128]{3,2,1,0:T(8,128)}, f32[4,1,512]{2,1,0:T(1,128)}) custom-call(s32[3]{0:T(128)} %pad_add_fusion.place_ref.refs_0_.refs_13_, ...), custom_call_target="tpu_custom_call", output_to_operand_aliasing={{0}: (18, {}), {1}: (19, {})} | custom-call | flops 2147483648 | bytes 9962627 | tf_op jit(solution)/shard_map/pallas_call | solution.py:444
  681.4 29.4 %shard_map.197 = (bf16[8,256,512]{2,1,0:T(8,128)(2,1)}, bf16[8,256,1024]{2,1,0:T(8,128)(2,1)}, f32[4,1,512]{2,1,0:T(1,128)}, bf16[2,256,2048]{2,1,0:T(8,128)(2,1)}, bf16[2,256,2048]{2,1,0:T(8,128)(2,1)}) custom-call(s32[3]{0:T(128)} %pad_add_fusion.place_ref.refs_0_.refs_13_, bf16[4,64,2176]{2,1,0:T(8,128)(2,1)} %copy-done.15, ...), custom_call_target="tpu_custom_call" | custom-call | flops 8589934592 | bytes 17959428 | tf_op jit(solution)/shard_map/pallas_call | solution.py:444
  714.9 25.2 %shard_map.198 = (bf16[4,256,2048]{2,1,0:T(8,128)(2,1)}, bf16[4,256,2048]{2,1,0:T(8,128)(2,1)}) custom-call(s32[3]{0:T(128)} %pad_add_fusion.place_ref.refs_0_.refs_13_, bf16[8,1,176,2048]{3,2,1,0:T(8,128)(2,1)} %bitcast.465, bf16[8,256,1408]{2,1,0:T(8,128)(2,1)} %get-tuple-element.206.refs_2_), custom_call_target="tpu_custom_call" | custom-call | flops 11811160064 | bytes 2883587 | tf_op jit(solution)/shard_map/pallas_call | solution.py:444
  742.4 8.5 fusion
  754.0 5.7 fusion.44
  759.7 5.7 fusion.41
  779.2 29.8 %shard_map.199 = (bf16[8,256,512]{2,1,0:T(8,128)(2,1)}, bf16[8,256,1024]{2,1,0:T(8,128)(2,1)}, f32[4,1,512]{2,1,0:T(1,128)}, bf16[2,256,2048]{2,1,0:T(8,128)(2,1)}, bf16[2,256,2048]{2,1,0:T(8,128)(2,1)}) custom-call(s32[3]{0:T(128)} %pad_add_fusion.place_ref.refs_0_.refs_13_, ...), custom_call_target="tpu_custom_call", output_to_operand_aliasing={{0}: (22, {}), {1}: (23, {})} | custom-call | flops 8589934592 | bytes 19532292 | tf_op jit(solution)/shard_map/pallas_call | solution.py:444
  809.1 9.4 fusion.35
  819.1 5.4 fusion.47
  830.6 36.2 %collective-permute-done.80 = bf16[1024,1024]{1,0:T(8,128)(2,1)} collective-permute-done((bf16[1024,1024]{1,0:T(8,128)(2,1)}, bf16[1024,1024]{1,0:T(8,128)(2,1)}, u32[]{:S(2)}, u32[]{:S(2)}) %collective-permute-start.80) | collective-permute-done | bytes 2097184 | tf_op jit(solution)/shard_map/ppermute | solution.py:28
  876.4 10.2 collective-permute-start.86
  891.6 9.9 collective-permute-start.84
  915.8 6.5 collective-permute-start.98
  932.5 10.0 collective-permute-done.91
  942.5 7.0 collective-permute-start.92
  953.0 5.8 collective-permute-done.102
  965.6 19.6 %collective-permute-done.103 = bf16[1,1,64,2048]{3,2,1,0:T(8,128)(2,1)} collective-permute-done((bf16[1,1,64,2048]{3,2,1,0:T(8,128)(2,1)}, bf16[1,1,64,2048]{3,2,1,0:T(8,128)(2,1)}, u32[]{:S(2)}, u32[]{:S(2)}) %collective-permute-start.103) | collective-permute-done | bytes 262176 | tf_op jit(solution)/shard_map/ppermute | solution.py:31
  (528 shorter events, 312.8 us)
Async XLA Ops:
  7.2 456.5 %all-gather.3.cloned.1.call-start = ((), (), s32[]{:S(2)}) async-start(), calls=%async_computation.4 | async-start | bytes 6488064 | tf_op jit(solution)/shard_map/all_gather | solution.py:532
  29.8 35.9 %collective-permute-start.8 = (bf16[4,64,2176]{2,1,0:T(8,128)(2,1)S(1)}, bf16[4,64,2176]{2,1,0:T(8,128)(2,1)}, u32[]{:S(2)}, u32[]{:S(2)}) collective-permute-start(bf16[4,64,2176]{2,1,0:T(8,128)(2,1)S(1)} %pad_maximum_fusion.3.refs_1_), channel_id=1, source_target_pairs={{0,16},{16,0},{1,17},{17,1},{2,18},{18,2},{3,19},{19,3},{4,20},{20... | collective-permute-start | bytes 3342344 | tf_op jit(solution)/shard_map/ppermute | solution.py:28
  33.0 32.0 %collective-permute-start.10 = (bf16[256,2048]{1,0:T(8,128)(2,1)}, bf16[256,2048]{1,0:T(8,128)(2,1)}, u32[]{:S(2)}, u32[]{:S(2)}) collective-permute-start(bf16[256,2048]{1,0:T(8,128)(2,1)} %get-tuple-element.154.refs_9_), channel_id=1, source_target_pairs={{0,8},{4,12},{8,0},{12,4},{1,9},{5,13},{9,1},{13,5},{2,10},{6,14},... | collective-permute-start | bytes 3145736 | tf_op jit(solution)/shard_map/ppermute | solution.py:25
  34.5 50.0 %collective-permute-start.7 = (bf16[4,64,2176]{2,1,0:T(8,128)(2,1)S(1)}, bf16[4,64,2176]{2,1,0:T(8,128)(2,1)}, u32[]{:S(2)}, u32[]{:S(2)}) collective-permute-start(bf16[4,64,2176]{2,1,0:T(8,128)(2,1)S(1)} %pad_maximum_fusion.3.refs_1_), channel_id=1, source_target_pairs={{0,1},{1,0},{2,3},{3,2},{4,5},{5,4},{6,7},{7,6},{8,9},{9,8},{10,11... | collective-permute-start | bytes 3342344 | tf_op jit(solution)/shard_map/ppermute | solution.py:31
  36.1 50.8 %collective-permute-start.6 = (bf16[4,64,2176]{2,1,0:T(8,128)(2,1)S(1)}, bf16[4,64,2176]{2,1,0:T(8,128)(2,1)}, u32[]{:S(2)}, u32[]{:S(2)}) collective-permute-start(bf16[4,64,2176]{2,1,0:T(8,128)(2,1)S(1)} %pad_maximum_fusion.3.refs_1_), channel_id=1, source_target_pairs={{0,2},{1,3},{2,0},{3,1},{4,6},{5,7},{6,4},{7,5},{8,10},{9,11},{10,... | collective-permute-start | bytes 3342344 | tf_op jit(solution)/shard_map/ppermute | solution.py:31
  93.0 32.9 %collective-permute-start.11 = (bf16[4,64,2176]{2,1,0:T(8,128)(2,1)}, bf16[4,64,2176]{2,1,0:T(8,128)(2,1)}, u32[]{:S(2)}, u32[]{:S(2)}) collective-permute-start(bf16[4,64,2176]{2,1,0:T(8,128)(2,1)} %collective-permute-done.6.refs_3_), channel_id=1, source_target_pairs={{0,1},{1,0},{2,3},{3,2},{4,5},{5,4},{6,7},{7,6},{8,9},{9,8},{10,11... | collective-permute-start | bytes 3342344 | tf_op jit(solution)/shard_map/ppermute | solution.py:31
  99.9 40.9 %collective-permute-start.12 = (bf16[4,64,2176]{2,1,0:T(8,128)(2,1)}, bf16[4,64,2176]{2,1,0:T(8,128)(2,1)}, u32[]{:S(2)}, u32[]{:S(2)}) collective-permute-start(bf16[4,64,2176]{2,1,0:T(8,128)(2,1)} %collective-permute-done.7.refs_2_), channel_id=1, source_target_pairs={{0,16},{16,0},{1,17},{17,1},{2,18},{18,2},{3,19},{19,3},{4,20},{20... | collective-permute-start | bytes 3342344 | tf_op jit(solution)/shard_map/ppermute | solution.py:28
  104.0 37.8 %collective-permute-start.38 = (bf16[256,2048]{1,0:T(8,128)(2,1)}, bf16[256,2048]{1,0:T(8,128)(2,1)}, u32[]{:S(2)}, u32[]{:S(2)}) collective-permute-start(bf16[256,2048]{1,0:T(8,128)(2,1)} %get-tuple-element.182), channel_id=1, source_target_pairs={{0,4},{4,0},{8,12},{12,8},{1,5},{5,1},{9,13},{13,9},{2,6},{6,2},{1... | collective-permute-start | bytes 3145736 | tf_op jit(solution)/shard_map/ppermute | solution.py:25
  120.2 59.4 %collective-permute-start.22 = (bf16[256,2048]{1,0:T(8,128)(2,1)}, bf16[256,2048]{1,0:T(8,128)(2,1)}, u32[]{:S(2)}, u32[]{:S(2)}) collective-permute-start(bf16[256,2048]{1,0:T(8,128)(2,1)} %get-tuple-element.154.refs_9_), channel_id=1, source_target_pairs={{0,4},{4,0},{8,12},{12,8},{1,5},{5,1},{9,13},{13,9},{2,6},{6,2},{1... | collective-permute-start | bytes 3145736 | tf_op jit(solution)/shard_map/ppermute | solution.py:25
  141.4 36.6 %collective-permute-start.20 = (bf16[4,64,2816]{2,1,0:T(8,128)(2,1)}, bf16[4,64,2816]{2,1,0:T(8,128)(2,1)}, u32[]{:S(2)}, u32[]{:S(2)}) collective-permute-start(bf16[4,64,2816]{2,1,0:T(8,128)(2,1)} %pad_maximum_fusion.2.refs_1_.refs_2_), channel_id=1, source_target_pairs={{0,1},{1,0},{2,3},{3,2},{4,5},{5,4},{6,7},{7,6},{8,9},{9,8},{10,11... | collective-permute-start | bytes 4325384 | tf_op jit(solution)/shard_map/ppermute | solution.py:31
  141.8 37.8 %collective-permute-start.23 = (bf16[256,2048]{1,0:T(8,128)(2,1)}, bf16[256,2048]{1,0:T(8,128)(2,1)}, u32[]{:S(2)}, u32[]{:S(2)}) collective-permute-start(bf16[256,2048]{1,0:T(8,128)(2,1)} %collective-permute-done.10.refs_11_), channel_id=1, source_target_pairs={{0,4},{4,0},{8,12},{12,8},{1,5},{5,1},{9,13},{13,9},{2,6},{6,2},{1... | collective-permute-start | bytes 3145736 | tf_op jit(solution)/shard_map/ppermute | solution.py:25
  169.2 70.9 %collective-permute-start.30 = (bf16[256,2048]{1,0:T(8,128)(2,1)}, bf16[256,2048]{1,0:T(8,128)(2,1)}, u32[]{:S(2)}, u32[]{:S(2)}) collective-permute-start(bf16[256,2048]{1,0:T(8,128)(2,1)} %get-tuple-element.157.refs_9_), channel_id=1, source_target_pairs={{0,4},{4,0},{8,12},{12,8},{1,5},{5,1},{9,13},{13,9},{2,6},{6,2},{1... | collective-permute-start | bytes 3145736 | tf_op jit(solution)/shard_map/ppermute | solution.py:25
  178.0 28.4 %collective-permute-start.28 = (bf16[1,64,2048]{2,1,0:T(8,128)(2,1)S(1)}, bf16[1,64,2048]{2,1,0:T(8,128)(2,1)S(1)}, u32[]{:S(2)}, u32[]{:S(2)}) collective-permute-start(bf16[1,64,2048]{2,1,0:T(8,128)(2,1)S(1)} %copy-done.39), channel_id=1, source_target_pairs={{0,16},{16,0},{1,17},{17,1},{2,18},{18,2},{3,19},{19,3},{4,20},{20... | collective-permute-start | bytes 786440 | tf_op jit(solution)/shard_map/ppermute | solution.py:28
  178.0 60.5 %collective-permute-start.17 = (bf16[4,64,2816]{2,1,0:T(8,128)(2,1)}, bf16[4,64,2816]{2,1,0:T(8,128)(2,1)}, u32[]{:S(2)}, u32[]{:S(2)}) collective-permute-start(bf16[4,64,2816]{2,1,0:T(8,128)(2,1)} %pad_maximum_fusion.2.refs_1_.refs_2_), channel_id=1, source_target_pairs={{0,2},{1,3},{2,0},{3,1},{4,6},{5,7},{6,4},{7,5},{8,10},{9,11},{10,... | collective-permute-start | bytes 4325384 | tf_op jit(solution)/shard_map/ppermute | solution.py:31
  179.6 29.3 %collective-permute-start.40 = (bf16[256,2048]{1,0:T(8,128)(2,1)}, bf16[256,2048]{1,0:T(8,128)(2,1)}, u32[]{:S(2)}, u32[]{:S(2)}) collective-permute-start(bf16[256,2048]{1,0:T(8,128)(2,1)} %collective-permute-done.39), channel_id=1, source_target_pairs={{0,4},{4,0},{8,12},{12,8},{1,5},{5,1},{9,13},{13,9},{2,6},{6,2},{1... | collective-permute-start | bytes 3145736 | tf_op jit(solution)/shard_map/ppermute | solution.py:25
  179.6 60.4 %collective-permute-start.26 = (bf16[4,64,2816]{2,1,0:T(8,128)(2,1)}, bf16[4,64,2816]{2,1,0:T(8,128)(2,1)}, u32[]{:S(2)}, u32[]{:S(2)}) collective-permute-start(bf16[4,64,2816]{2,1,0:T(8,128)(2,1)} %pad_maximum_fusion.2.refs_1_.refs_2_), channel_id=1, source_target_pairs={{0,16},{16,0},{1,17},{17,1},{2,18},{18,2},{3,19},{19,3},{4,20},{20... | collective-permute-start | bytes 4325384 | tf_op jit(solution)/shard_map/ppermute | solution.py:28
  206.4 34.3 %collective-permute-start.31 = (bf16[256,2048]{1,0:T(8,128)(2,1)}, bf16[256,2048]{1,0:T(8,128)(2,1)}, u32[]{:S(2)}, u32[]{:S(2)}) collective-permute-start(bf16[256,2048]{1,0:T(8,128)(2,1)} %copy-done.59), channel_id=1, source_target_pairs={{0,4},{4,0},{8,12},{12,8},{1,5},{5,1},{9,13},{13,9},{2,6},{6,2},{1... | collective-permute-start | bytes 3145736 | tf_op jit(solution)/shard_map/ppermute | solution.py:25
  228.2 40.7 %collective-permute-start.32 = (bf16[4,4,128,128]{3,2,1,0:T(8,128)(2,1)}, bf16[4,4,128,128]{3,2,1,0:T(8,128)(2,1)S(1)}, u32[]{:S(2)}, u32[]{:S(2)}) collective-permute-start(bf16[4,4,128,128]{3,2,1,0:T(8,128)(2,1)} %add_convert_fusion.25), channel_id=1, source_target_pairs={{0,1},{4,5},{8,9},{12,13},{16,17},{20,21},{24,25},{28,29}} | collective-permute-start | bytes 1572872 | tf_op jit(solution)/shard_map/ppermute | solution.py:571
  238.5 46.8 %collective-permute-start.44 = (bf16[4,64,2816]{2,1,0:T(8,128)(2,1)}, bf16[4,64,2816]{2,1,0:T(8,128)(2,1)}, u32[]{:S(2)}, u32[]{:S(2)}) collective-permute-start(bf16[4,64,2816]{2,1,0:T(8,128)(2,1)} %collective-permute-done.20.refs_2_.refs_3_), channel_id=1, source_target_pairs={{0,16},{16,0},{1,17},{17,1},{2,18},{18,2},{3,19},{19,3},{4,20},{20... | collective-permute-start | bytes 4325384 | tf_op jit(solution)/shard_map/ppermute | solution.py:28
  240.0 33.1 %collective-permute-start.33 = (bf16[4,64,2816]{2,1,0:T(8,128)(2,1)}, bf16[4,64,2816]{2,1,0:T(8,128)(2,1)}, u32[]{:S(2)}, u32[]{:S(2)}) collective-permute-start(bf16[4,64,2816]{2,1,0:T(8,128)(2,1)} %collective-permute-done.17.refs_3_.refs_4_), channel_id=1, source_target_pairs={{0,1},{1,0},{2,3},{3,2},{4,5},{5,4},{6,7},{7,6},{8,9},{9,8},{10,11... | collective-permute-start | bytes 4325384 | tf_op jit(solution)/shard_map/ppermute | solution.py:31
  240.1 62.6 %collective-permute-start.18 = (bf16[4,64,2816]{2,1,0:T(8,128)(2,1)}, bf16[4,64,2816]{2,1,0:T(8,128)(2,1)}, u32[]{:S(2)}, u32[]{:S(2)}) collective-permute-start(bf16[4,64,2816]{2,1,0:T(8,128)(2,1)} %collective-permute-done.17.refs_3_.refs_4_), channel_id=1, source_target_pairs={{0,16},{16,0},{1,17},{17,1},{2,18},{18,2},{3,19},{19,3},{4,20},{20... | collective-permute-start | bytes 4325384 | tf_op jit(solution)/shard_map/ppermute | solution.py:28
  240.6 44.7 %collective-permute-start.42 = (bf16[256,2048]{1,0:T(8,128)(2,1)}, bf16[256,2048]{1,0:T(8,128)(2,1)}, u32[]{:S(2)}, u32[]{:S(2)}) collective-permute-start(bf16[256,2048]{1,0:T(8,128)(2,1)} %get-tuple-element.183), channel_id=1, source_target_pairs={{0,8},{4,12},{8,0},{12,4},{1,9},{5,13},{9,1},{13,5},{2,10},{6,14},... | collective-permute-start | bytes 3145736 | tf_op jit(solution)/shard_map/ppermute | solution.py:25
  322.1 330.3 %reduce-scatter.3.cloned.1.call-start = ((), (), s32[]{:S(2)}) async-start(), calls=%async_computation.2 | async-start | bytes 6488064 | tf_op jit(solution)/shard_map/reduce_scatter | solution.py:636
  338.8 43.7 %collective-permute-start.41 = (bf16[256,2048]{1,0:T(8,128)(2,1)}, bf16[256,2048]{1,0:T(8,128)(2,1)S(1)}, u32[]{:S(2)}, u32[]{:S(2)}) collective-permute-start(bf16[256,2048]{1,0:T(8,128)(2,1)} %get-tuple-element.183), channel_id=1, source_target_pairs={{0,4},{4,0},{8,12},{12,8},{1,5},{5,1},{9,13},{13,9},{2,6},{6,2},{1... | collective-permute-start | bytes 3145736 | tf_op jit(solution)/shard_map/ppermute | solution.py:25
  338.8 43.7 %collective-permute-start.45 = (bf16[4,64,2816]{2,1,0:T(8,128)(2,1)}, bf16[4,64,2816]{2,1,0:T(8,128)(2,1)S(1)}, u32[]{:S(2)}, u32[]{:S(2)}) collective-permute-start(bf16[4,64,2816]{2,1,0:T(8,128)(2,1)} %collective-permute-done.33.refs_4_.refs_5_), channel_id=1, source_target_pairs={{0,16},{16,0},{1,17},{17,1},{2,18},{18,2},{3,19},{19,3},{4,20},{20... | collective-permute-start | bytes 4325384 | tf_op jit(solution)/shard_map/ppermute | solution.py:28
  340.5 45.4 %collective-permute-start.43 = (bf16[256,2048]{1,0:T(8,128)(2,1)}, bf16[256,2048]{1,0:T(8,128)(2,1)S(1)}, u32[]{:S(2)}, u32[]{:S(2)}) collective-permute-start(bf16[256,2048]{1,0:T(8,128)(2,1)} %collective-permute-done.42), channel_id=1, source_target_pairs={{0,4},{4,0},{8,12},{12,8},{1,5},{5,1},{9,13},{13,9},{2,6},{6,2},{1... | collective-permute-start | bytes 3145736 | tf_op jit(solution)/shard_map/ppermute | solution.py:25
  341.1 45.9 %collective-permute-start.50 = (bf16[1,256,2048]{2,1,0:T(8,128)(2,1)S(1)}, bf16[1,256,2048]{2,1,0:T(8,128)(2,1)S(1)}, u32[]{:S(2)}, u32[]{:S(2)}) collective-permute-start(bf16[1,256,2048]{2,1,0:T(8,128)(2,1)S(1)} %fusion.59), channel_id=1, source_target_pairs={{0,8},{4,12},{8,0},{12,4},{1,9},{5,13},{9,1},{13,5},{2,10},{6,14},... | collective-permute-start | bytes 3145736 | tf_op jit(solution)/shard_map/ppermute | solution.py:25
  514.3 448.4 %reduce-scatter.5.cloned.1.call-start = ((), (), s32[]{:S(2)}) async-start(), calls=%async_computation.3 | async-start | bytes 7208960 | tf_op jit(solution)/shard_map/reduce_scatter | solution.py:774
  517.3 34.4 %collective-permute-start.58 = (bf16[1,256,2048]{2,1,0:T(8,128)(2,1)}, bf16[1,256,2048]{2,1,0:T(8,128)(2,1)S(1)}, u32[]{:S(2)}, u32[]{:S(2)}) collective-permute-start(bf16[1,256,2048]{2,1,0:T(8,128)(2,1)} %fusion.60), channel_id=1, source_target_pairs={{0,8},{4,12},{8,0},{12,4},{1,9},{5,13},{9,1},{13,5},{2,10},{6,14},... | collective-permute-start | bytes 3145736 | tf_op jit(solution)/shard_map/ppermute | solution.py:25
  560.1 31.2 %collective-permute-start.60 = (bf16[256,2048]{1,0:T(8,128)(2,1)}, bf16[256,2048]{1,0:T(8,128)(2,1)}, u32[]{:S(2)}, u32[]{:S(2)}) collective-permute-start(bf16[256,2048]{1,0:T(8,128)(2,1)} %add_convert_fusion.7.refs_9_), channel_id=1, source_target_pairs={{0,4},{4,0},{8,12},{12,8},{1,5},{5,1},{9,13},{13,9},{2,6},{6,2},{1... | collective-permute-start | bytes 3145736 | tf_op jit(solution)/shard_map/ppermute | solution.py:25
  589.5 152.9 %collective-permute-start.93 = (bf16[1024,2816]{1,0:T(8,128)(2,1)}, bf16[1024,2816]{1,0:T(8,128)(2,1)}, u32[]{:S(2)}, u32[]{:S(2)}) collective-permute-start(bf16[1024,2816]{1,0:T(8,128)(2,1)} %convolution_convert_fusion.2), channel_id=1, source_target_pairs={{0,16},{16,0},{1,17},{17,1},{2,18},{18,2},{3,19},{19,3},{4,20},{20... | collective-permute-start | bytes 17301512 | tf_op jit(solution)/shard_map/ppermute | solution.py:28
  604.9 34.0 %collective-permute-start.63 = (bf16[4,4,128,128]{3,2,1,0:T(8,128)(2,1)S(1)}, bf16[4,4,128,128]{3,2,1,0:T(8,128)(2,1)S(1)}, u32[]{:S(2)}, u32[]{:S(2)}) collective-permute-start(bf16[4,4,128,128]{3,2,1,0:T(8,128)(2,1)S(1)} %add_convert_fusion.19), channel_id=1, source_target_pairs={{3,2},{7,6},{11,10},{15,14},{19,18},{23,22},{27,26},{31,30}} | collective-permute-start | bytes 1572872 | tf_op jit(solution)/shard_map/ppermute | solution.py:571
  679.7 32.3 %collective-permute-start.72 = (bf16[4,4,128,128]{3,2,1,0:T(8,128)(2,1)}, bf16[4,4,128,128]{3,2,1,0:T(8,128)(2,1)}, u32[]{:S(2)}, u32[]{:S(2)}) collective-permute-start(bf16[4,4,128,128]{3,2,1,0:T(8,128)(2,1)} %fusion.57), channel_id=1, source_target_pairs={{2,1},{6,5},{10,9},{14,13},{18,17},{22,21},{26,25},{30,29}} | collective-permute-start | bytes 1572872 | tf_op jit(solution)/shard_map/ppermute | solution.py:571
  711.5 39.5 %collective-permute-start.73 = (bf16[1,2,256,2048]{3,2,1,0:T(8,128)(2,1)}, bf16[1,2,256,2048]{3,2,1,0:T(8,128)(2,1)}, u32[]{:S(2)}, u32[]{:S(2)}) collective-permute-start(bf16[1,2,256,2048]{3,2,1,0:T(8,128)(2,1)} %bitcast.466), channel_id=1, source_target_pairs={{0,4},{4,0},{8,12},{12,8},{1,5},{5,1},{9,13},{13,9},{2,6},{6,2},{1... | collective-permute-start | bytes 6291464 | tf_op jit(solution)/shard_map/ppermute | solution.py:25
  740.1 33.4 %collective-permute-start.71 = (bf16[4,256,2048]{2,1,0:T(8,128)(2,1)}, bf16[4,256,2048]{2,1,0:T(8,128)(2,1)}, u32[]{:S(2)}, u32[]{:S(2)}) collective-permute-start(bf16[4,256,2048]{2,1,0:T(8,128)(2,1)} %get-tuple-element.238), channel_id=1, source_target_pairs={{0,4},{4,0},{8,12},{12,8},{1,5},{5,1},{9,13},{13,9},{2,6},{6,2},{1... | collective-permute-start | bytes 12582920 | tf_op jit(solution)/shard_map/ppermute | solution.py:25
  765.4 53.1 %collective-permute-start.76 = (bf16[1,256,2048]{2,1,0:T(8,128)(2,1)}, bf16[1,256,2048]{2,1,0:T(8,128)(2,1)}, u32[]{:S(2)}, u32[]{:S(2)}) collective-permute-start(bf16[1,256,2048]{2,1,0:T(8,128)(2,1)} %fusion.62), channel_id=1, source_target_pairs={{0,8},{4,12},{8,0},{12,4},{1,9},{5,13},{9,1},{13,5},{2,10},{6,14},... | collective-permute-start | bytes 3145736 | tf_op jit(solution)/shard_map/ppermute | solution.py:25
  766.0 108.7 %collective-permute-start.82 = (bf16[1024,512]{1,0:T(8,128)(2,1)}, bf16[1024,512]{1,0:T(8,128)(2,1)}, u32[]{:S(2)}, u32[]{:S(2)}) collective-permute-start(bf16[1024,512]{1,0:T(8,128)(2,1)} %fusion.41), channel_id=1, source_target_pairs={{0,16},{16,0},{1,17},{17,1},{2,18},{18,2},{3,19},{19,3},{4,20},{20... | collective-permute-start | bytes 3145736 | tf_op jit(solution)/shard_map/ppermute | solution.py:28
  777.2 128.5 %collective-permute-start.74 = (bf16[256,2048]{1,0:T(8,128)(2,1)}, bf16[256,2048]{1,0:T(8,128)(2,1)}, u32[]{:S(2)}, u32[]{:S(2)}) collective-permute-start(bf16[256,2048]{1,0:T(8,128)(2,1)} %get-tuple-element.296), channel_id=1, source_target_pairs={{0,8},{4,12},{8,0},{12,4},{1,9},{5,13},{9,1},{13,5},{2,10},{6,14},... | collective-permute-start | bytes 3145736 | tf_op jit(solution)/shard_map/ppermute | solution.py:25
  778.7 127.3 %collective-permute-start.75 = (bf16[256,2048]{1,0:T(8,128)(2,1)}, bf16[256,2048]{1,0:T(8,128)(2,1)}, u32[]{:S(2)}, u32[]{:S(2)}) collective-permute-start(bf16[256,2048]{1,0:T(8,128)(2,1)} %get-tuple-element.297), channel_id=1, source_target_pairs={{0,8},{4,12},{8,0},{12,4},{1,9},{5,13},{9,1},{13,5},{2,10},{6,14},... | collective-permute-start | bytes 3145736 | tf_op jit(solution)/shard_map/ppermute | solution.py:25
  818.5 48.3 %collective-permute-start.80 = (bf16[1024,1024]{1,0:T(8,128)(2,1)}, bf16[1024,1024]{1,0:T(8,128)(2,1)}, u32[]{:S(2)}, u32[]{:S(2)}) collective-permute-start(bf16[1024,1024]{1,0:T(8,128)(2,1)} %fusion.35), channel_id=1, source_target_pairs={{0,16},{16,0},{1,17},{17,1},{2,18},{18,2},{3,19},{19,3},{4,20},{20... | collective-permute-start | bytes 6291464 | tf_op jit(solution)/shard_map/ppermute | solution.py:28
  829.1 72.3 %collective-permute-start.79 = (bf16[1,256,2048]{2,1,0:T(8,128)(2,1)S(1)}, bf16[1,256,2048]{2,1,0:T(8,128)(2,1)S(1)}, u32[]{:S(2)}, u32[]{:S(2)}) collective-permute-start(bf16[1,256,2048]{2,1,0:T(8,128)(2,1)S(1)} %fusion.65), channel_id=1, source_target_pairs={{0,8},{4,12},{8,0},{12,4},{1,9},{5,13},{9,1},{13,5},{2,10},{6,14},... | collective-permute-start | bytes 3145736 | tf_op jit(solution)/shard_map/ppermute | solution.py:25
  876.4 36.2 %collective-permute-start.86 = (bf16[4,2,64,512]{3,2,1,0:T(8,128)(2,1)S(1)}, bf16[4,2,64,512]{3,2,1,0:T(8,128)(2,1)S(1)}, u32[]{:S(2)}, u32[]{:S(2)}) collective-permute-start(bf16[4,2,64,512]{3,2,1,0:T(8,128)(2,1)S(1)} %fusion.72), channel_id=1, source_target_pairs={{0,1},{1,0},{2,3},{3,2},{4,5},{5,4},{6,7},{7,6},{8,9},{9,8},{10,11... | collective-permute-start | bytes 1572872 | tf_op jit(solution)/shard_map/ppermute | solution.py:31
  891.6 57.9 %collective-permute-start.84 = (bf16[4,2,64,1024]{3,2,1,0:T(8,128)(2,1)S(1)}, bf16[4,2,64,1024]{3,2,1,0:T(8,128)(2,1)S(1)}, u32[]{:S(2)}, u32[]{:S(2)}) collective-permute-start(bf16[4,2,64,1024]{3,2,1,0:T(8,128)(2,1)S(1)} %fusion.66), channel_id=1, source_target_pairs={{0,1},{1,0},{2,3},{3,2},{4,5},{5,4},{6,7},{7,6},{8,9},{9,8},{10,11... | collective-permute-start | bytes 3145736 | tf_op jit(solution)/shard_map/ppermute | solution.py:31
  901.5 29.1 %collective-permute-start.85 = (bf16[256,2048]{1,0:T(8,128)(2,1)S(1)}, bf16[256,2048]{1,0:T(8,128)(2,1)S(1)}, u32[]{:S(2)}, u32[]{:S(2)}) collective-permute-start(bf16[256,2048]{1,0:T(8,128)(2,1)S(1)} %copy-done.60), channel_id=1, source_target_pairs={{0,16},{16,0},{1,17},{17,1},{2,18},{18,2},{3,19},{19,3},{4,20},{20... | collective-permute-start | bytes 3145736 | tf_op jit(solution)/shard_map/ppermute | solution.py:28
  912.6 39.5 %collective-permute-start.83 = (bf16[4,2,64,512]{3,2,1,0:T(8,128)(2,1)S(1)}, bf16[4,2,64,512]{3,2,1,0:T(8,128)(2,1)S(1)}, u32[]{:S(2)}, u32[]{:S(2)}) collective-permute-start(bf16[4,2,64,512]{3,2,1,0:T(8,128)(2,1)S(1)} %fusion.73), channel_id=1, source_target_pairs={{0,1},{1,0},{2,3},{3,2},{4,5},{5,4},{6,7},{7,6},{8,9},{9,8},{10,11... | collective-permute-start | bytes 1572872 | tf_op jit(solution)/shard_map/ppermute | solution.py:31
  915.8 81.1 %collective-permute-start.98 = (bf16[4,1,64,512]{3,2,1,0:T(8,128)(2,1)}, bf16[4,1,64,512]{3,2,1,0:T(8,128)(2,1)}, u32[]{:S(2)}, u32[]{:S(2)}) collective-permute-start(bf16[4,1,64,512]{3,2,1,0:T(8,128)(2,1)} %bitcast.120), channel_id=1, source_target_pairs={{0,2},{1,3},{2,0},{3,1},{4,6},{5,7},{6,4},{7,5},{8,10},{9,11},{10,... | collective-permute-start | bytes 786440 | tf_op jit(solution)/shard_map/ppermute | solution.py:31
  930.7 28.1 %collective-permute-start.102 = (bf16[1,2,64,2048]{3,2,1,0:T(8,128)(2,1)S(1)}, bf16[1,2,64,2048]{3,2,1,0:T(8,128)(2,1)S(1)}, u32[]{:S(2)}, u32[]{:S(2)}) collective-permute-start(bf16[1,2,64,2048]{3,2,1,0:T(8,128)(2,1)S(1)} %fusion.74), channel_id=1, source_target_pairs={{0,1},{1,0},{2,3},{3,2},{4,5},{5,4},{6,7},{7,6},{8,9},{9,8},{10,11... | collective-permute-start | bytes 1572872 | tf_op jit(solution)/shard_map/ppermute | solution.py:31
  952.1 44.8 %collective-permute-start.97 = (bf16[4,1,64,1024]{3,2,1,0:T(8,128)(2,1)}, bf16[4,1,64,1024]{3,2,1,0:T(8,128)(2,1)}, u32[]{:S(2)}, u32[]{:S(2)}) collective-permute-start(bf16[4,1,64,1024]{3,2,1,0:T(8,128)(2,1)} %bitcast.116), channel_id=1, source_target_pairs={{0,2},{1,3},{2,0},{3,1},{4,6},{5,7},{6,4},{7,5},{8,10},{9,11},{10,... | collective-permute-start | bytes 1572872 | tf_op jit(solution)/shard_map/ppermute | solution.py:31
  (161 other events, 2653.4 us)
Sparse Core Ops, SparseCore 0:
  322.2 101.0 all-gather.2
  514.4 114.6 reduce-scatter.2
  751.0 113.3 reduce-scatter.4
